TPU v7x, 512 devices: a whole 4x8x8 slice. The times are simulated.
512 devices in a mesh: seg: 16 (over z, y_lo), dp: 32 (over y_hi, x, core).
Axes of the slice: x: 4, y: 8 (y_hi: 4, y_lo: 2; y = y_hi * 2 + y_lo), z: 8, core: 2. Of those that a mesh axis runs over, the one named last changes fastest.
Arguments:
- tokens: bfloat16 [32, 2048, 1024], P('dp', 'seg'), may hold values from -6 to 6
- grad_output: bfloat16 [32, 2048, 1024], P('dp', 'seg'), may hold values from -6 to 6
- memories: bfloat16 [32, 16, 32, 1024], P('dp', 'seg'), may hold values from -6 to 6
- grad_last: bfloat16 [32, 32, 1024], P('dp'), may hold values from -6 to 6
- norm_gain: float32 [1024], replicated, may hold values from 0.1 to 1.9
- query_weight: bfloat16 [1024, 1024], P('dp'), may hold values from -0.1875 to 0.1875
- key_weight: bfloat16 [1024, 256], P('dp'), may hold values from -0.1875 to 0.1875
- value_weight: bfloat16 [1024, 256], P('dp'), may hold values from -0.1875 to 0.1875
- out_weight: bfloat16 [1024, 1024], P(None, 'dp'), may hold values from -0.1875 to 0.1875
Outputs:
- grad_tokens: bfloat16 [32, 2048, 1024], P('dp', 'seg')
- grad_memories: bfloat16 [32, 16, 32, 1024], P('dp', 'seg')
- grad_key: float32 [1024, 256], P('dp')
- grad_value: float32 [1024, 256], P('dp')
All inputs are finite; a program needn't handle non-finite values.
Results may differ from a plain program's by a relative error of at most 0.035.
Values may be sent and summed in bfloat16 or wider, within the bound.
No kernel may reach another device: no remote copies, remote signals or barrier semaphores. Data moves between devices by JAX's collectives and lax.ppermute only.
A program may use at most 64 MiB of HBM per device.

v0:
```python
import math

import jax
import jax.numpy as jnp
from jax import lax
from jax.sharding import PartitionSpec as P

HEADS = 16
KV_HEADS = 4
HEAD_DIM = 64


epsilon = 1e-05


def passed_along(block, axis, distance):
    devices = range(lax.axis_size(axis))
    route = [(i - distance, i) for i in devices if i - distance in devices]
    return lax.ppermute(block, axis, route)


def norm_backward(cotangent, normed_grad, hidden, inverse_norm, norm_gain):
    scaled_grad = normed_grad * norm_gain
    return cotangent + inverse_norm * (
        scaled_grad
        - hidden
        * inverse_norm
        * inverse_norm
        * jnp.mean(scaled_grad * hidden, axis=-1, keepdims=True)
    )


def contract_last(left_side, right_side):
    return lax.dot_general(
        left_side, right_side, (((1,), (1,)), ((), ())), preferred_element_type=jnp.float32
    )


def contract_first(left_side, right_side):
    return lax.dot_general(
        left_side, right_side, (((0,), (0,)), ((), ())), preferred_element_type=jnp.float32
    )


def body(
    tokens,
    grad_output,
    memories,
    grad_last,
    norm_gain,
    query_weight,
    key_weight,
    value_weight,
    out_weight,
):
    memory_rows = memories.shape[2]
    segment_rows = tokens.shape[1]
    model_width = tokens.shape[2]
    total_rows = memory_rows + segment_rows
    group_size = HEADS // KV_HEADS
    score_scale = 1.0 / math.sqrt(HEAD_DIM)
    query_width = query_weight.shape[1]
    key_width = key_weight.shape[1]
    hidden = jnp.concatenate(
        [memories[0, 0].astype(jnp.float32), tokens[0].astype(jnp.float32)], axis=0
    )
    inverse_norm = lax.rsqrt(jnp.mean(hidden * hidden, axis=-1, keepdims=True) + epsilon)
    normed = (hidden * inverse_norm * norm_gain).astype(jnp.bfloat16)
    pieces = (
        lax.all_gather(query_weight, "dp", axis=0, tiled=True),
        lax.all_gather(key_weight, "dp", axis=0, tiled=True),
        lax.all_gather(value_weight, "dp", axis=0, tiled=True),
    )
    columns = normed
    products = tuple(
        (
            jnp.dot(columns, pieces[member], preferred_element_type=jnp.float32)
            for member in range(3)
        )
    )
    copies = tuple((pieces[member] for member in range(3)))
    folded = products + copies
    query_full = folded[3]
    key_full = folded[4]
    value_full = folded[5]
    query_heads = folded[0].astype(jnp.bfloat16).reshape(total_rows, KV_HEADS, group_size, HEAD_DIM)
    key_heads = folded[1].astype(jnp.bfloat16).reshape(total_rows, KV_HEADS, HEAD_DIM)
    value_heads = folded[2].astype(jnp.bfloat16).reshape(total_rows, KV_HEADS, HEAD_DIM)
    scores = (
        jnp.einsum("igad,jgd->gaij", query_heads, key_heads, preferred_element_type=jnp.float32)
        * score_scale
    )
    row_index = lax.broadcasted_iota(jnp.int32, (total_rows, total_rows), 0)
    column_index = lax.broadcasted_iota(jnp.int32, (total_rows, total_rows), 1)
    allowed = (row_index < memory_rows) | (column_index <= row_index)
    raised = jnp.where(allowed, jnp.exp(scores), 0.0)
    softmax_full = raised / jnp.sum(raised, axis=-1, keepdims=True)
    softmax_half = softmax_full.astype(jnp.bfloat16)
    token_cotangent = grad_output[0]
    piece = lax.all_gather(out_weight, "dp", axis=1, tiled=True)
    columns = token_cotangent
    token_sum = contract_last(columns, piece)
    token_upstream = token_sum.astype(jnp.bfloat16).reshape(
        segment_rows, KV_HEADS, group_size, HEAD_DIM
    )
    token_probs = softmax_full[:, :, memory_rows:]
    token_prob_grad = jnp.einsum(
        "igad,jgd->gaij", token_upstream, value_heads, preferred_element_type=jnp.float32
    )
    token_score_grad = (
        token_probs
        * (token_prob_grad - jnp.sum(token_probs * token_prob_grad, axis=-1, keepdims=True))
        * score_scale
    ).astype(jnp.bfloat16)
    token_query_grad = (
        jnp.einsum(
            "gaij,jgd->igad", token_score_grad, key_heads, preferred_element_type=jnp.float32
        )
        .reshape(segment_rows, query_width)
        .astype(jnp.bfloat16)
    )
    key_partial = jnp.einsum(
        "gaij,igad->jgd",
        token_score_grad,
        query_heads[memory_rows:],
        preferred_element_type=jnp.float32,
    ).reshape(total_rows, key_width)
    value_partial = jnp.einsum(
        "gaij,igad->jgd",
        softmax_half[:, :, memory_rows:],
        token_upstream,
        preferred_element_type=jnp.float32,
    ).reshape(total_rows, key_width)

    def chain_step(incoming):
        memory_upstream = (
            contract_last(incoming, piece)
            .astype(jnp.bfloat16)
            .reshape(memory_rows, KV_HEADS, group_size, HEAD_DIM)
        )
        memory_probs = softmax_full[:, :, :memory_rows]
        memory_prob_grad = jnp.einsum(
            "igad,jgd->gaij", memory_upstream, value_heads, preferred_element_type=jnp.float32
        )
        memory_score_grad = (
            memory_probs
            * (memory_prob_grad - jnp.sum(memory_probs * memory_prob_grad, axis=-1, keepdims=True))
            * score_scale
        ).astype(jnp.bfloat16)
        memory_query_grad = (
            jnp.einsum(
                "gaij,jgd->igad", memory_score_grad, key_heads, preferred_element_type=jnp.float32
            )
            .reshape(memory_rows, query_width)
            .astype(jnp.bfloat16)
        )
        key_grad = (
            key_partial
            + jnp.einsum(
                "gaij,igad->jgd",
                memory_score_grad,
                query_heads[:memory_rows],
                preferred_element_type=jnp.float32,
            ).reshape(total_rows, key_width)
        ).astype(jnp.bfloat16)
        value_grad = (
            value_partial
            + jnp.einsum(
                "gaij,igad->jgd",
                softmax_half[:, :, :memory_rows],
                memory_upstream,
                preferred_element_type=jnp.float32,
            ).reshape(total_rows, key_width)
        ).astype(jnp.bfloat16)
        normed_grad = (
            contract_last(memory_query_grad, query_full)
            + contract_last(key_grad[:memory_rows], key_full)
            + contract_last(value_grad[:memory_rows], value_full)
        )
        memory_grad = norm_backward(
            incoming.astype(jnp.float32),
            normed_grad,
            hidden[:memory_rows],
            inverse_norm[:memory_rows],
            norm_gain,
        ).astype(jnp.bfloat16)
        return (memory_grad, key_grad, value_grad)

    chain_length = lax.axis_size("seg")
    position = lax.axis_index("seg")
    at_end = position == chain_length - 1

    def chain_turn(section, current):
        arrived = passed_along(current[0], "seg", -1)
        incoming = jnp.where(at_end, grad_last[0], arrived)
        active = position == chain_length - 1 - section

        def keep_state(unused):
            return current

        return lax.cond(active, chain_step, keep_state, incoming)

    start_state = (
        jnp.zeros((memory_rows, model_width), jnp.bfloat16),
        jnp.zeros((total_rows, key_width), jnp.bfloat16),
        jnp.zeros((total_rows, key_width), jnp.bfloat16),
    )
    memory_grad, key_grad, value_grad = lax.fori_loop(0, chain_length, chain_turn, start_state)
    token_normed_grad = (
        contract_last(token_query_grad, query_full)
        + contract_last(key_grad[memory_rows:], key_full)
        + contract_last(value_grad[memory_rows:], value_full)
    )
    token_grad = norm_backward(
        token_cotangent.astype(jnp.float32),
        token_normed_grad,
        hidden[memory_rows:],
        inverse_norm[memory_rows:],
        norm_gain,
    ).astype(jnp.bfloat16)
    key_gradient = contract_first(normed, key_grad)
    value_gradient = contract_first(normed, value_grad)
    documents = lax.axis_size("dp")
    shares = (
        lax.psum_scatter(
            key_gradient.astype(jnp.bfloat16), "dp", scatter_dimension=0, tiled=True
        ).astype(jnp.float32),
        lax.psum_scatter(
            value_gradient.astype(jnp.bfloat16), "dp", scatter_dimension=0, tiled=True
        ).astype(jnp.float32),
    )
    totals = (
        lax.psum(shares[0].astype(jnp.bfloat16), "seg").astype(jnp.float32),
        lax.psum(shares[1].astype(jnp.bfloat16), "seg").astype(jnp.float32),
    )
    return (token_grad[None], memory_grad[None, None], totals[0] / documents, totals[1] / documents)


def solution(mesh):
    in_specs = (
        P("dp", "seg", None),
        P("dp", "seg", None),
        P("dp", "seg", None, None),
        P("dp", None, None),
        P(),
        P("dp", None),
        P("dp", None),
        P("dp", None),
        P(None, "dp"),
    )
    out_specs = (P("dp", "seg", None), P("dp", "seg", None, None), P("dp", None), P("dp", None))
    return jax.shard_map(body, mesh=mesh, in_specs=in_specs, out_specs=out_specs, check_vma=False)
```

profile of v0, /device:TPU:2, one launch (start us, length us, event | category | flops | bytes accessed | tf_op | source)
XLA Modules:
  0.0 781.7 jit_solution(6831233496585554209)
XLA Ops:
  11.6 46.4 %all_gather.14 = bf16[1024,256]{1,0:T(8,128)(2,1)S(1)} all-gather(bf16[32,256]{1,0:T(8,128)(2,1)S(1)} %copy-done.12), channel_id=1, replica_groups=mesh['seg'=16,'dp'=32] {'dp'}, dimensions={0}, use_global_device_ids=true | all-gather | bytes 540672 | tf_op jit(solution)/shard_map/all_gather | solution.py:72
  59.0 43.4 %all_gather.12 = bf16[1024,256]{1,0:T(8,128)(2,1)S(1)} all-gather(bf16[32,256]{1,0:T(8,128)(2,1)S(1)} %copy-done.13), channel_id=1, replica_groups=mesh['seg'=16,'dp'=32] {'dp'}, dimensions={0}, use_global_device_ids=true | all-gather | bytes 540672 | tf_op jit(solution)/shard_map/all_gather | solution.py:71
  103.5 2.1 convolution_convert_fusion.4
  105.9 30.1 %all-gather.5.cloned.1.call-done = bf16[1024,1024]{0,1:T(8,128)(2,1)} async-done(((bf16[1024,32]{0,1:T(8,128)(2,1)}), bf16[1024,1024]{0,1:T(8,128)(2,1)}) %all-gather.5.cloned.1.call-update) | async-done | bytes 2097168 | tf_op jit(solution)/shard_map/all_gather | solution.py:100
  136.0 2.0 convolution_convert_fusion.6
  139.5 1.7 fusion.35
  141.3 2.1 fusion.56
  143.4 1.6 copy.51
  146.2 1.3 convolution_bitcast_fusion.1
  147.5 4.0 copy.48
  151.5 4.1 fusion.42
  155.6 4.1 copy.49
  161.7 359.4 %while.17 = (s32[]{:T(128)}, bf16[32,1024]{1,0:T(8,128)(2,1)}, bf16[160,256]{0,1:T(8,128)(2,1)}, bf16[160,256]{0,1:T(8,128)(2,1)}, s32[]{:T(128)}, /*index=5*/pr...) while((s32[]{:T(128)}, bf16[32,1024]{1,0:T(8,128)(2,1)}, ...), condition=%wide.region_8.9_spmd, body=%wide.region_3.8_spmd.sunk | while | flops 211256640 | bytes 15062437 | solution.py:208
  161.7 1.3 collective-permute-start
  163.0 5.1 collective-permute-done
  169.4 5.1 collective-permute-done
  174.4 1.3 collective-permute-start
  175.7 5.8 collective-permute-done
  182.8 6.0 collective-permute-done
  190.1 6.0 collective-permute-done
  197.3 6.4 collective-permute-done
  205.0 6.4 collective-permute-done
  211.4 1.3 collective-permute-start
  212.7 5.8 collective-permute-done
  219.8 6.0 collective-permute-done
  227.1 6.0 collective-permute-done
  234.3 6.0 collective-permute-done
  241.6 6.0 collective-permute-done
  248.8 6.0 collective-permute-done
  256.1 6.0 collective-permute-done
  263.4 7.2 collective-permute-done
  271.9 232.4 %collective-permute-done = bf16[32,1024]{1,0:T(8,128)(2,1)S(1)} collective-permute-done((bf16[32,1024]{1,0:T(8,128)(2,1)}, bf16[32,1024]{1,0:T(8,128)(2,1)S(1)}, u32[]{:S(2)}, u32[]{:S(2)}) %collective-permute-start) | collective-permute-done | bytes 65568 | tf_op jit(solution)/shard_map/while/body/eval_jaxpr/ppermute | solution.py:19
  504.3 16.8 %conditional.2 = ((bf16[32,1024]{1,0:T(8,128)(2,1)}, bf16[160,256]{0,1:T(8,128)(2,1)}, bf16[160,256]{0,1:T(8,128)(2,1)})) conditional(s32[]{:T(128)} %convert_element_type.156, (bf16[32,1024]{1,0:T(8,128)(2,1)}, bf16[160,256]{0,1:T(8,128)(2,1)}, bf16[160,256]{0,1:T(8,128)(2,1)}) %tuple.50, (pred[]{:T(512)}, bf16[1,32,1024]{2,1,0:T(8,128)(2,1)}, ...), branch_computations={%region_4.4_spmd, %region_5.7_spmd} | conditional | flops 211256640 | bytes 14799862 | solution.py:201
  504.3 2.4 convolution_convert_fusion.1
  508.0 1.9 convolution_bitcast_fusion
  509.9 2.6 fusion.7
  512.5 1.8 fusion.5
  514.3 1.9 fusion.16
  519.5 1.6 add_convert_fusion
  521.1 2.2 convolution_convert_fusion.2
  523.6 5.1 convolution_convert_fusion.5
  528.7 2.0 convolution_convert_fusion.3
  530.8 1.8 fusion.59
  532.7 1.3 convolution_add_fusion.3
  534.0 1.4 multiply_reduce_fusion.3
  536.3 75.7 %reduce-scatter.5.cloned.1.call-done = bf16[32,256]{1,0:T(8,128)(2,1)} async-done(((bf16[1024,256]{1,0:T(8,128)(2,1)}), bf16[32,256]{1,0:T(8,128)(2,1)}) %reduce-scatter.5.cloned.1.call-update) | async-done | bytes 16400 | tf_op jit(solution)/shard_map/reduce_scatter | solution.py:228
  612.0 98.5 %reduce-scatter.3.cloned.1.call-done = bf16[32,256]{1,0:T(8,128)(2,1)} async-done(((bf16[1024,256]{1,0:T(8,128)(2,1)}), bf16[32,256]{1,0:T(8,128)(2,1)}) %reduce-scatter.3.cloned.1.call-update) | async-done | bytes 16400 | tf_op jit(solution)/shard_map/reduce_scatter | solution.py:225
  710.5 64.1 %all-reduce = (bf16[32,256]{1,0:T(8,128)(2,1)S(1)}, bf16[32,256]{1,0:T(8,128)(2,1)S(1)}) all-reduce(bf16[32,256]{1,0:T(8,128)(2,1)} %reduce-scatter.3.cloned.1.call-done, bf16[32,256]{1,0:T(8,128)(2,1)} %reduce-scatter.5.cloned.1.call-done), channel_id=1, replica_groups=mesh['seg'=16,'dp'=32] {'seg'}, use_global_device_ids=true, to_apply=%region_11.12 | all-reduce | flops 16384 | bytes 65536 | tf_op jit(solution)/shard_map/psum | solution.py:233
  (98 shorter events, 34.4 us)
Async XLA Ops:
  7.2 4.4 copy-start.12
  7.2 96.3 %all-gather.3.cloned.1.call-start = ((), (), s32[]{:S(2)}) async-start(), calls=%async_computation.2 | async-start | bytes 2162688 | tf_op jit(solution)/shard_map/all_gather | solution.py:70
  7.9 128.1 %all-gather.5.cloned.1.call-start = ((), (), s32[]{:S(2)}) async-start(), calls=%async_computation.3 | async-start | bytes 2162688 | tf_op jit(solution)/shard_map/all_gather | solution.py:100
  8.7 603.3 %reduce-scatter.5.cloned.1.call-start = ((), (), s32[]{:S(2)}) async-start(), calls=%async_computation.5 | async-start | bytes 540672 | tf_op jit(solution)/shard_map/reduce_scatter | solution.py:228
  9.6 1.2 copy-start.1
  9.6 49.4 %copy-start.13 = (bf16[32,256]{1,0:T(8,128)(2,1)S(1)}, bf16[32,256]{1,0:T(8,128)(2,1)}, u32[]{:S(2)}) copy-start(bf16[32,256]{1,0:T(8,128)(2,1)} %param.19) | copy-start | bytes 49156
  11.6 94.0 %copy-start.3 = (bf16[160,1024]{1,0:T(8,128)(2,1)}, bf16[160,1024]{1,0:T(8,128)(2,1)S(1)}, u32[]{:S(2)}) copy-start(bf16[160,1024]{1,0:T(8,128)(2,1)S(1)} %multiply_convert_fusion) | copy-start | bytes 983044
  103.4 32.6 %copy-start.9 = (bf16[1,128,1024]{2,1,0:T(8,128)(2,1)S(1)}, bf16[1,128,1024]{2,1,0:T(8,128)(2,1)}, u32[]{:S(2)}) copy-start(bf16[1,128,1024]{2,1,0:T(8,128)(2,1)} %param.14) | copy-start | bytes 786436
  147.4 4.0 copy-start.8
  155.6 6.1 copy-start
  155.6 6.1 copy-start.11
  161.7 6.4 collective-permute-start
  168.1 6.4 collective-permute-start
  174.4 7.1 collective-permute-start
  181.5 7.3 collective-permute-start
  188.8 7.3 collective-permute-start
  196.0 7.7 collective-permute-start
  203.7 7.7 collective-permute-start
  211.4 7.1 collective-permute-start
  218.5 7.3 collective-permute-start
  225.8 7.3 collective-permute-start
  233.0 7.3 collective-permute-start
  240.3 7.3 collective-permute-start
  247.5 7.3 collective-permute-start
  254.8 7.3 collective-permute-start
  262.1 8.5 %collective-permute-start = (bf16[32,1024]{1,0:T(8,128)(2,1)}, bf16[32,1024]{1,0:T(8,128)(2,1)S(1)}, u32[]{:S(2)}, u32[]{:S(2)}) collective-permute-start(bf16[32,1024]{1,0:T(8,128)(2,1)} %get-tuple-element.694), channel_id=1, source_target_pairs={{32,0},{64,32},{96,64},{128,96},{160,128},{192,160},{224,192},{256... | collective-permute-start | bytes 196616 | tf_op jit(solution)/shard_map/while/body/eval_jaxpr/ppermute | solution.py:19
  270.6 233.7 %collective-permute-start = (bf16[32,1024]{1,0:T(8,128)(2,1)}, bf16[32,1024]{1,0:T(8,128)(2,1)S(1)}, u32[]{:S(2)}, u32[]{:S(2)}) collective-permute-start(bf16[32,1024]{1,0:T(8,128)(2,1)} %get-tuple-element.694), channel_id=1, source_target_pairs={{32,0},{64,32},{96,64},{128,96},{160,128},{192,160},{224,192},{256... | collective-permute-start | bytes 196616 | tf_op jit(solution)/shard_map/while/body/eval_jaxpr/ppermute | solution.py:19
  504.3 2.4 copy-start.5
  516.2 2.1 copy-start.2
  516.4 3.1 copy-start.6
  521.1 7.7 copy-start.4
  523.3 187.1 %reduce-scatter.3.cloned.1.call-start = ((), (), s32[]{:S(2)}) async-start(), calls=%async_computation.4 | async-start | bytes 540672 | tf_op jit(solution)/shard_map/reduce_scatter | solution.py:225
  530.8 3.2 copy-start.7
  532.6 2.7 copy-start.10
Sparse Core Ops, SparseCore 0:
  11.1 63.1 all-gather.2
  77.4 58.5 all-gather.4
  523.4 88.4 reduce-scatter.4
  616.1 94.2 reduce-scatter.2
where the time goes:
time: 783 us; the launch traced here: 782 us
  waiting for transfers between devices  528 us (67%)
  blocking collectives  154 us (20%)
  matrix products  39.7 us (5%)
  starting transfers between devices  20.8 us (3%)
  local copies, waits for them, and re-layouts  15.4 us (2%)
  between operations  14 us (2%)
  other arithmetic  10 us (1%)
    ppermute x16, waiting for transfers between devices, passed_along(): return lax.ppermute(block, axis, route)  322 us
    reduce_scatter x1, waiting for transfers between devices, body(): lax.psum_scatter(key_gradient.astype(jnp.bfloat16), 'dp', scatter_dimensi...  98.5 us
    reduce_scatter x1, waiting for transfers between devices, body(): lax.psum_scatter(value_gradient.astype(jnp.bfloat16), 'dp', scatter_dimen...  75.7 us
    psum x1, blocking collectives, body(): lax.psum(shares[0].astype(jnp.bfloat16), 'seg').astype(jnp.float32)  64.1 us
    all_gather x1, blocking collectives, body(): lax.all_gather(value_weight, 'dp', axis=0, tiled=True)  46.4 us
    all_gather x1, blocking collectives, body(): lax.all_gather(key_weight, 'dp', axis=0, tiled=True)  43.4 us
    all_gather x1, waiting for transfers between devices, body(): piece = lax.all_gather(out_weight, 'dp', axis=1, tiled=True)  30.1 us
    ppermute x16, starting transfers between devices, passed_along(): return lax.ppermute(block, axis, route)  20.5 us
  transfers between devices with their start and end apart: 20, of which 19 were waited for; matrix products, arithmetic and copies ran while one was open for 3% of the time, Pallas kernels for 0%

commit v1 on v0

v1 whole, which is shorter than its diff:
```python
import functools

import jax
import jax.numpy as jnp
from jax import lax
from jax.experimental import pallas as pl
from jax.experimental.pallas import tpu as pltpu
from jax.sharding import PartitionSpec as P

D = 1024
GROUPS = 4
PER_GROUP = 4
HEAD = 64
WIDE = PER_GROUP * HEAD
KV = GROUPS * HEAD
MEM = 32
TOK = 128
ROWS = MEM + TOK
SPAN = 4
EPS = 1e-05
SCALE = 0.125
BF = jnp.bfloat16
F32 = jnp.float32


def nn(a, b):
    return lax.dot_general(a, b, (((1,), (0,)), ((), ())), preferred_element_type=F32)


def nt(a, b):
    return lax.dot_general(a, b, (((1,), (1,)), ((), ())), preferred_element_type=F32)


def tn(a, b):
    return lax.dot_general(a, b, (((0,), (0,)), ((), ())), preferred_element_type=F32)


def normalised(rows, gain):
    inverse = lax.rsqrt(jnp.mean(rows * rows, axis=-1, keepdims=True) + EPS)
    return inverse, (rows * inverse * gain).astype(BF)


def norm_backward(cotangent, normed_grad, hidden, inverse, gain):
    scaled = normed_grad * gain
    mean = jnp.mean(scaled * hidden, axis=-1, keepdims=True)
    return cotangent + inverse * (scaled - hidden * (inverse * inverse * mean))


def repeated(rows, g):
    half = rows[:, (g // 2) * 128 : (g // 2) * 128 + 128].astype(F32)
    lane = lax.broadcasted_iota(jnp.int32, half.shape, 1)
    kept = jnp.where((lane < HEAD) == (g % 2 == 0), half, 0.0)
    both = kept + pltpu.roll(kept, HEAD, 1)
    return jnp.concatenate([both, both], axis=1).astype(BF)


def stacked(rows):
    rows = rows.astype(F32)
    lane = lax.broadcasted_iota(jnp.int32, rows.shape, 1) // HEAD
    return jnp.concatenate([jnp.where(lane == a, rows, 0.0) for a in range(PER_GROUP)], axis=0).astype(BF)


def unstacked(rows):
    n = rows.shape[0] // PER_GROUP
    lane = lax.broadcasted_iota(jnp.int32, (n, WIDE), 1) // HEAD
    total = jnp.zeros((n, WIDE), F32)
    for a in range(PER_GROUP):
        total = jnp.where(lane == a, rows[a * n : (a + 1) * n], total)
    return total


def folded(parts):
    sums = []
    for part in parts:
        half = part[:, :128] + part[:, 128:]
        sums.append(half + pltpu.roll(half, HEAD, 1))
    lane = lax.broadcasted_iota(jnp.int32, sums[0].shape, 1)
    return jnp.concatenate(
        [jnp.where(lane < HEAD, sums[0], sums[1]), jnp.where(lane < HEAD, sums[2], sums[3])], axis=1
    )


def softmax_grad(probs, prob_grad):
    centred = prob_grad - jnp.sum(probs * prob_grad, axis=0, keepdims=True)
    return (probs * centred * SCALE).astype(BF)


def token_kernel(mem, tok, gout, gain, w, normed_out, qg_out, part_out, kvp_out, wt_out):
    hidden = jnp.concatenate([mem[...].astype(F32), tok[...].astype(F32)], axis=0)
    _, normed = normalised(hidden, gain[...])
    normed_out[...] = normed
    q = nn(normed[MEM:], w[:, :D])
    kv = nn(normed, w[:, D : D + 2 * KV]).astype(BF)
    up = nn(gout[...], w[:, D + 2 * KV :])
    k, v = kv[:, :KV], kv[:, KV:]
    key_at = lax.broadcasted_iota(jnp.int32, (ROWS, PER_GROUP * TOK), 0)
    row_at = lax.broadcasted_iota(jnp.int32, (ROWS, PER_GROUP * TOK), 1) % TOK
    seen = key_at <= row_at + MEM
    key_parts, value_parts = [], []
    for g in range(GROUPS):
        cols = slice(g * WIDE, (g + 1) * WIDE)
        zq = stacked(q[:, cols])
        zu = stacked(up[:, cols])
        krep, vrep = repeated(k, g), repeated(v, g)
        raised = jnp.where(seen, jnp.exp(nt(krep, zq) * SCALE), 0.0)
        probs = raised * (1.0 / jnp.sum(raised, axis=0, keepdims=True))
        score_grad = softmax_grad(probs, nt(vrep, zu))
        key_parts.append(nn(score_grad, zq))
        value_parts.append(nn(probs.astype(BF), zu))
        qg_out[:, cols] = unstacked(tn(score_grad, krep)).astype(BF)
    part = jnp.concatenate([folded(key_parts), folded(value_parts)], axis=1)
    part_out[...] = part
    kvp_out[:MEM, :] = part[:MEM].astype(BF)
    kvp_out[MEM:, :] = kv[MEM:]
    wt_out[...] = w[:, : D + 2 * KV].T


def ready_kernel(mem4, gain, w, kvp4, probs_out, krep_out, vrep_out, zq_out):
    _, normed = normalised(mem4[...].astype(F32), gain[...])
    qkv = nn(normed, w[:, : D + 2 * KV])
    for s in range(SPAN):
        rows = slice(s * MEM, (s + 1) * MEM)
        later = slice(s * ROWS + MEM, (s + 1) * ROWS)
        k = jnp.concatenate([qkv[rows, D : D + KV].astype(BF), kvp4[later, :KV]], axis=0)
        v = jnp.concatenate([qkv[rows, D + KV :].astype(BF), kvp4[later, KV:]], axis=0)
        for g in range(GROUPS):
            zq = stacked(qkv[rows, g * WIDE : (g + 1) * WIDE])
            krep = repeated(k, g)
            raised = jnp.exp(nt(krep, zq) * SCALE)
            at = s * GROUPS + g
            probs_out[at] = raised * (1.0 / jnp.sum(raised, axis=0, keepdims=True))
            krep_out[at] = krep
            vrep_out[at] = repeated(v, g)
            zq_out[at] = zq


def chain_kernel(fresh, arrived, held, mem4, gain, wo, wt, probs, krep, vrep, zq, kvp4, out):
    start = jnp.where(fresh[0] == 1, arrived[...].astype(F32), held[...].astype(F32)).astype(BF)
    out[SPAN * MEM :, :] = start
    current = start
    for s in reversed(range(SPAN)):
        rows = slice(s * MEM, (s + 1) * MEM)
        hidden = mem4[rows, :].astype(F32)
        inverse, _ = normalised(hidden, gain[...])
        up = nn(current, wo[...])
        query_grads, key_parts, value_parts = [], [], []
        for g in range(GROUPS):
            at = s * GROUPS + g
            zu = stacked(up[:, g * WIDE : (g + 1) * WIDE])
            p = probs[at]
            score_grad = softmax_grad(p, nt(vrep[at], zu))
            query_grads.append(unstacked(tn(score_grad, krep[at])))
            key_parts.append(nn(score_grad[:MEM], zq[at]))
            value_parts.append(nn(p[:MEM].astype(BF), zu))
        own = kvp4[s * ROWS : s * ROWS + MEM, :].astype(F32)
        kv_grad = jnp.concatenate([folded(key_parts), folded(value_parts)], axis=1) + own
        grads = jnp.concatenate(query_grads + [kv_grad], axis=1).astype(BF)
        current = norm_backward(current.astype(F32), nn(grads, wt[...]), hidden, inverse, gain[...]).astype(BF)
        out[rows, :] = current


def weight_kernel(place, chain, wo, probs, krep, vrep, zq, part, normed, kv_out, grad_out):
    r = place[0]
    current = chain[pl.ds(pl.multiple_of((r + 1) * MEM, MEM), MEM), :]
    up = nn(current, wo[...])
    key_parts, value_parts = [], []
    for g in range(GROUPS):
        at = r * GROUPS + g
        zu = stacked(up[:, g * WIDE : (g + 1) * WIDE])
        p = probs[at]
        score_grad = softmax_grad(p, nt(vrep[at], zu))
        key_parts.append(nn(score_grad, zq[at]))
        value_parts.append(nn(p.astype(BF), zu))
    kv_grad = jnp.concatenate([folded(key_parts), folded(value_parts)], axis=1) + part[...]
    kv_grad = kv_grad.astype(BF)
    kv_out[...] = kv_grad
    grad_out[...] = tn(normed[...], kv_grad).astype(BF)


def rows_kernel(tok, gout, gain, wt, qg, kv_grad, out):
    hidden = tok[...].astype(F32)
    inverse, _ = normalised(hidden, gain[...])
    normed_grad = nn(qg[...], wt[:D, :]) + nn(kv_grad[MEM:, :], wt[D:, :])
    out[...] = norm_backward(gout[...].astype(F32), normed_grad, hidden, inverse, gain[...]).astype(BF)


def call(kernel, outs, args, flops, scalars=0):
    vmem = pl.BlockSpec(memory_space=pltpu.VMEM)
    smem = pl.BlockSpec(memory_space=pltpu.SMEM)
    moved = sum(a.size * a.dtype.itemsize for a in args) + sum(o.size * o.dtype.itemsize for o in outs)
    return pl.pallas_call(
        kernel,
        out_shape=outs,
        in_specs=[smem] * scalars + [vmem] * (len(args) - scalars),
        out_specs=[vmem] * len(outs),
        compiler_params=pltpu.CompilerParams(vmem_limit_bytes=48 * 1024 * 1024),
        cost_estimate=pl.CostEstimate(flops=flops, bytes_accessed=moved, transcendentals=0),
    )(*args)


def shape(dims, dtype=BF):
    return jax.ShapeDtypeStruct(dims, dtype)


def runs(axis_size, length, stride):
    block = length * stride
    return [
        [b + o + i * stride for i in range(length)] for b in range(0, axis_size, block) for o in range(stride)
    ]


def shared_out(block, length, stride):
    groups = runs(lax.axis_size("dp"), length, stride)
    got = lax.all_to_all(block, "dp", 0, 0, tiled=True, axis_index_groups=groups)
    got = got.reshape((length, block.shape[0] // length) + block.shape[1:])
    return jnp.sum(got.astype(F32), axis=0).astype(BF)


def summed(block, length, stride):
    groups = runs(lax.axis_size("seg"), length, stride)
    got = lax.all_gather(block, "seg", axis=0, axis_index_groups=groups)
    return jnp.sum(got.astype(F32), axis=0)


def reduced(grad):
    docs = lax.axis_size("dp")
    rows = D // docs
    core = lax.axis_index("dp") % 2
    halves = grad.reshape(docs // 2, 2, rows, 2 * KV)
    mine = lax.dynamic_index_in_dim(halves, core, 1, keepdims=False)
    other = lax.dynamic_index_in_dim(halves, 1 - core, 1, keepdims=False)
    got = lax.ppermute(other, "dp", [(i, i ^ 1) for i in range(docs)])
    block = (mine.astype(F32) + got.astype(F32)).astype(BF)
    if docs == 32:
        block = block.reshape(4, 4, rows, 2 * KV)
        block = shared_out(block, 4, 8)[0]
        block = shared_out(block, 4, 2)[0]
    else:
        block = block[0]
    block = summed(block, 4, 1).astype(BF)
    return summed(block, lax.axis_size("seg") // 4, 4)


def body(tokens, grad_output, memories, grad_last, norm_gain, query_weight, key_weight, value_weight, out_weight):
    position = lax.axis_index("seg")
    n_seg = lax.axis_size("seg")
    turns = n_seg // SPAN
    tok, gout, mem, gain = tokens[0], grad_output[0], memories[0, 0], norm_gain[None]

    shard = jnp.concatenate([query_weight, key_weight, value_weight, out_weight.T], axis=1)
    w = lax.all_gather(shard, "dp", axis=0, tiled=True)
    near = runs(n_seg, SPAN, 1)
    mem4 = lax.all_gather(mem, "seg", axis=0, tiled=True, axis_index_groups=near)

    normed, qg, part, kvp, wt = call(
        token_kernel,
        [shape((ROWS, D)), shape((TOK, D)), shape((ROWS, 2 * KV), F32), shape((ROWS, 2 * KV)), shape((D + 2 * KV, D))],
        (mem, tok, gout, gain, w),
        1_500_000_000,
    )
    kvp4 = lax.all_gather(kvp, "seg", axis=0, tiled=True, axis_index_groups=near)
    count = SPAN * GROUPS
    probs, krep, vrep, zq = call(
        ready_kernel,
        [
            shape((count, ROWS, PER_GROUP * MEM), F32),
            shape((count, ROWS, WIDE)),
            shape((count, ROWS, WIDE)),
            shape((count, PER_GROUP * MEM, WIDE)),
        ],
        (mem4, gain, w, kvp4),
        800_000_000,
    )
    wo = w[:, D + 2 * KV :]
    block = position // SPAN
    held = grad_last[0]
    arrived = held
    for turn in range(turns):
        fresh = (block == turns - 1 - turn).astype(jnp.int32)[None]
        (chain,) = call(
            chain_kernel,
            [shape(((SPAN + 1) * MEM, D))],
            (fresh, arrived, held, mem4, gain, wo, wt, probs, krep, vrep, zq, kvp4),
            1_000_000_000,
            scalars=1,
        )
        held = chain[SPAN * MEM :]
        if turn < turns - 1:
            route = [(i, i - SPAN) for i in range((turns - 1 - turn) * SPAN, (turns - turn) * SPAN)]
            arrived = lax.ppermute(chain[:MEM], "seg", route)
    place = (position % SPAN)[None].astype(jnp.int32)
    kv_grad, grad = call(
        weight_kernel,
        [shape((ROWS, 2 * KV)), shape((D, 2 * KV))],
        (place, chain, wo, probs, krep, vrep, zq, part, normed),
        400_000_000,
        scalars=1,
    )
    (grad_tokens,) = call(
        rows_kernel, [shape((TOK, D))], (tok, gout, gain, wt, qg, kv_grad), 500_000_000
    )
    grad_memories = lax.dynamic_slice_in_dim(chain, place[0] * MEM, MEM, 0)
    total = reduced(grad) / lax.axis_size("dp")
    return (grad_tokens[None], grad_memories[None, None], total[:, :KV], total[:, KV:])


def solution(mesh):
    in_specs = (
        P("dp", "seg", None),
        P("dp", "seg", None),
        P("dp", "seg", None, None),
        P("dp", None, None),
        P(),
        P("dp", None),
        P("dp", None),
        P("dp", None),
        P(None, "dp"),
    )
    out_specs = (P("dp", "seg", None), P("dp", "seg", None, None), P("dp", None), P("dp", None))
    return jax.shard_map(body, mesh=mesh, in_specs=in_specs, out_specs=out_specs, check_vma=False)
```

time: 783 us -> 273 us (0.35)
  the two profiles are of different devices: /device:TPU:2 before, /device:TPU:8 now
where the time goes in v1:
time: 273 us; the launch traced here: 272 us
  waiting for transfers between devices  95.9 us (35%)
  Pallas kernels  60.7 us (22%)
  blocking collectives  58.6 us (21%)
  local copies, waits for them, and re-layouts  22.5 us (8%)
  starting transfers between devices  14.4 us (5%)
  between operations  14.4 us (5%)
  other arithmetic  5.62 us (2%)
    pallas_call x8, Pallas kernels, call(): pl.pallas_call(kernel, out_shape=outs, in_specs=[smem] * scalars + [vmem]...  60.7 us
    all_gather x1, waiting for transfers between devices, body(): w = lax.all_gather(shard, 'dp', axis=0, tiled=True)  59 us
    all_gather x2, blocking collectives, summed(): got = lax.all_gather(block, 'seg', axis=0, axis_index_groups=groups)  25.6 us
    ppermute x3, waiting for transfers between devices, body(): arrived = lax.ppermute(chain[:MEM], 'seg', route)  18.3 us
    all_gather x1, blocking collectives, body(): lax.all_gather(kvp, 'seg', axis=0, tiled=True, axis_index_groups=near)  17.6 us
    all_to_all x2, waiting for transfers between devices, shared_out(): lax.all_to_all(block, 'dp', 0, 0, tiled=True, axis_index_groups=groups)  16.4 us
    all_gather x1, blocking collectives, body(): lax.all_gather(mem, 'seg', axis=0, tiled=True, axis_index_groups=near)  15.4 us
    unnamed x56, local copies, waits for them, and re-layouts  14.5 us
  transfers between devices with their start and end apart: 7, of which 5 were waited for; matrix products, arithmetic and copies ran while one was open for 1% of the time, Pallas kernels for 1%

profile of v1, /device:TPU:8, one launch (start us, length us, event | category | flops | bytes accessed | tf_op | source)
XLA Modules:
  0.0 272.1 jit_solution(16503879487156209880)
XLA Ops:
  7.2 1.6 pad_maximum_fusion
  8.8 15.4 %all-gather = bf16[1,1,128,1024]{3,2,1,0:T(8,128)(2,1)S(1)} all-gather(bf16[1,1,32,1024]{3,2,1,0:T(8,128)(2,1)} %param.11), channel_id=2, replica_groups={{0,32,64,96},{128,160,192,224},{256,288,320,352},{384,416,448,480},{1,3..., dimensions={2}, use_global_device_ids=true | all-gather | bytes 327680 | tf_op jit(solution)/shard_map/all_gather | solution.py:253
  24.3 59.0 %all-gather.5.cloned.1.call-done.w = bf16[1024,2560]{1,0:T(8,128)(2,1)} async-done(((bf16[32,2560]{1,0:T(8,128)(2,1)}), bf16[1024,2560]{1,0:T(8,128)(2,1)}) %all-gather.5.cloned.1.call-update) | async-done | bytes 5242896 | tf_op jit(solution)/shard_map/all_gather | solution.py:251
  83.3 0.9 copy-done.8
  84.2 0.9 copy-done.10
  85.2 0.8 copy-done.18
  86.0 0.7 copy-done.24
  86.7 5.5 %shard_map.120 = (bf16[160,1024]{1,0:T(8,128)(2,1)S(1)}, bf16[128,1024]{1,0:T(8,128)(2,1)S(1)}, f32[160,512]{1,0:T(8,128)S(1)}, bf16[160,512]{1,0:T(8,128)(2,1)S(1)}, bf16[1536,1024]{1,0:T(8,128)(2,1)S(1)}) custom-call(bf16[32,1024]{1,0:T(8,128)(2,1)S(1)} %bitcast.38, bf16[128,1024]{1,0:T(8,128)(2,1)S(1)} %bitcast.30, bf16[128,1024]{1,0:T(8,128)(2,1)S(1)} %bitcast.32, ...), custom_call_target="tpu_custom_call" | custom-call | flops 1500000000 | bytes 10063872 | tf_op jit(solution)/shard_map/pallas_call | solution.py:191
  92.3 17.6 %all_gather.20.kvp4 = bf16[640,512]{1,0:T(8,128)(2,1)S(1)} all-gather(bf16[160,512]{1,0:T(8,128)(2,1)S(1)} %get-tuple-element.17), channel_id=1, replica_groups={{0,32,64,96},{128,160,192,224},{256,288,320,352},{384,416,448,480},{1,3..., dimensions={0}, use_global_device_ids=true | all-gather | bytes 819200 | tf_op jit(solution)/shard_map/all_gather | solution.py:261
  109.8 3.1 %slice.36.wo = bf16[1024,1024]{1,0:T(8,128)(2,1)} slice(bf16[1024,2560]{1,0:T(8,128)(2,1)} %all-gather.5.cloned.1.call-done.w), slice={[0:1024], [1536:2560]} | slice | bytes 4194304 | tf_op jit(solution)/shard_map/slice | solution.py:274
  113.0 4.0 %shard_map.121 = (f32[16,160,128]{2,1,0:T(8,128)S(1)}, bf16[16,160,256]{2,1,0:T(8,128)(2,1)S(1)}, bf16[16,160,256]{2,1,0:T(8,128)(2,1)S(1)}, bf16[16,128,256]{2,1,0:T(8,128)(2,1)S(1)}) custom-call(bf16[128,1024]{1,0:T(8,128)(2,1)S(1)} %bitcast.25, f32[1,1024]{1,0:T(1,128)S(1)} %bitcast.40, bf16[1024,2560]{1,0:T(8,128)(2,1)} %all-gather.5.cloned.1.call-done.w, ...), custom_call_target="tpu_custom_call" | custom-call | flops 800000000 | bytes 11145216 | tf_op jit(solution)/shard_map/pallas_call | solution.py:191
  117.0 1.1 copy-done.2
  118.1 11.8 %shard_map.122 = bf16[160,1024]{1,0:T(8,128)(2,1)S(1)} custom-call(s32[1]{0:T(128)} %bitcast.9.fresh, bf16[32,1024]{1,0:T(8,128)(2,1)S(1)} %bitcast.36, bf16[32,1024]{1,0:T(8,128)(2,1)S(1)} %bitcast.37, bf16[128,1024]{1,0:T(8,128)(2,1)S(1)} %bitcast.26, f32[1,1024]{1,0:T(1,128)S(1)} %bitcast.41, bf16[1024,1024]{1,0:T(8,128)(2,1)} %slice.36.wo, ...), custom_call_target="tpu_custom_call" | custom-call | flops 1000000000 | bytes 11603972 | tf_op jit(solution)/shard_map/pallas_call | solution.py:191
  129.9 0.7 fusion.3
  130.5 1.3 collective-permute-start
  131.8 1.2 copy-done.4
  133.0 0.8 copy-done.20
  133.9 11.4 %shard_map.123 = bf16[160,1024]{1,0:T(8,128)(2,1)S(1)} custom-call(s32[1]{0:T(128)} %bitcast.8.fresh, bf16[32,1024]{1,0:T(8,128)(2,1)} %collective-permute-done.arrived, bf16[32,1024]{1,0:T(8,128)(2,1)S(1)} %copy-done.20, bf16[128,1024]{1,0:T(8,128)(2,1)S(1)} %bitcast.27, f32[1,1024]{1,0:T(1,128)S(1)} %bitcast.42, bf16[1024,1024]{1,0:T(8,128)(2,1)} %slice.36.wo, ...), custom_call_target="tpu_custom_call" | custom-call | flops 1000000000 | bytes 11603972 | tf_op jit(solution)/shard_map/pallas_call | solution.py:191
  145.3 0.7 fusion.2
  145.9 1.3 collective-permute-start.1
  147.2 1.2 copy-done.5
  148.5 0.8 copy-done.21
  149.3 11.4 %shard_map.124 = bf16[160,1024]{1,0:T(8,128)(2,1)S(1)} custom-call(s32[1]{0:T(128)} %bitcast.7.fresh, bf16[32,1024]{1,0:T(8,128)(2,1)} %collective-permute-done.1.arrived, bf16[32,1024]{1,0:T(8,128)(2,1)S(1)} %copy-done.21, bf16[128,1024]{1,0:T(8,128)(2,1)S(1)} %bitcast.28, f32[1,1024]{1,0:T(1,128)S(1)} %bitcast.43, bf16[1024,1024]{1,0:T(8,128)(2,1)} %slice.36.wo, ...), custom_call_target="tpu_custom_call" | custom-call | flops 1000000000 | bytes 11603972 | tf_op jit(solution)/shard_map/pallas_call | solution.py:191
  160.7 0.7 fusion.1
  161.3 1.5 collective-permute-start.2
  162.9 18.3 %collective-permute-done.2.arrived = bf16[32,1024]{1,0:T(8,128)(2,1)} collective-permute-done((bf16[32,1024]{1,0:T(8,128)(2,1)}, bf16[32,1024]{1,0:T(8,128)(2,1)}, u32[]{:S(2)}, u32[]{:S(2)}) %collective-permute-start.2) | collective-permute-done | bytes 65568 | tf_op jit(solution)/shard_map/ppermute | solution.py:290
  181.1 1.2 copy-done.6
  182.4 0.8 copy-done.19
  183.2 11.5 %shard_map.125.chain = bf16[160,1024]{1,0:T(8,128)(2,1)S(1)} custom-call(s32[1]{0:T(128)} %bitcast.6.fresh, bf16[32,1024]{1,0:T(8,128)(2,1)} %collective-permute-done.2.arrived, bf16[32,1024]{1,0:T(8,128)(2,1)S(1)} %copy-done.19, bf16[128,1024]{1,0:T(8,128)(2,1)S(1)} %bitcast.29, f32[1,1024]{1,0:T(1,128)S(1)} %bitcast.44, bf16[1024,1024]{1,0:T(8,128)(2,1)} %slice.36.wo, ...), custom_call_target="tpu_custom_call" | custom-call | flops 1000000000 | bytes 11603972 | tf_op jit(solution)/shard_map/pallas_call | solution.py:191
  194.7 3.8 %shard_map.126 = (bf16[160,512]{1,0:T(8,128)(2,1)S(1)}, bf16[1024,512]{1,0:T(8,128)(2,1)S(1)}) custom-call(s32[1]{0:T(128)} %bitcast.5.place, bf16[160,1024]{1,0:T(8,128)(2,1)S(1)} %shard_map.125.chain, bf16[1024,1024]{1,0:T(8,128)(2,1)} %slice.36.wo, f32[16,160,128]{2,1,0:T(8,128)S(1)} %get-tuple-element.18.probs, ...), custom_call_target="tpu_custom_call" | custom-call | flops 400000000 | bytes 9273348 | tf_op jit(solution)/shard_map/pallas_call | solution.py:191
  198.5 0.9 copy-done.12
  199.5 0.8 dynamic-slice_bitcast_fusion
  200.3 1.9 collective-permute-start.3
  202.2 2.2 collective-permute-done.3
  204.5 2.2 fusion
  206.6 4.1 %all-to-all-start = ((bf16[4,4,32,512]{3,2,1,0:T(8,128)(2,1)}), bf16[4,4,32,512]{3,2,1,0:T(8,128)(2,1)}, u32[]{:S(2)}, u32[]{:S(2)}) async-start(bf16[4,4,32,512]{3,2,1,0:T(8,128)(2,1)} %bitcast.46), calls=%async_computation | async-start | bytes 1048576 | tf_op jit(solution)/shard_map/all_to_all | solution.py:214
  210.8 0.9 copy-done.11
  211.7 0.9 copy-done.23
  212.7 0.9 copy-done.27
  213.6 1.5 shard_map.127
  215.1 11.9 %all-to-all-done = bf16[4,4,32,512]{3,2,1,0:T(8,128)(2,1)} async-done(((bf16[4,4,32,512]{3,2,1,0:T(8,128)(2,1)}), bf16[4,4,32,512]{3,2,1,0:T(8,128)(2,1)}, u32[]{:S(2)}, u32[]{:S(2)}) %all-to-all-start) | async-done | bytes 524320 | tf_op jit(solution)/shard_map/all_to_all | solution.py:214
  226.9 1.8 reduce_sum.47
  228.7 4.2 %all-to-all-start.1 = ((bf16[4,32,512]{2,1,0:T(8,128)(2,1)}), bf16[4,32,512]{2,1,0:T(8,128)(2,1)S(1)}, u32[]{:S(2)}, u32[]{:S(2)}) async-start(bf16[4,32,512]{2,1,0:T(8,128)(2,1)} %reduce_sum.47), calls=%async_computation.1 | async-start | bytes 262144 | tf_op jit(solution)/shard_map/all_to_all | solution.py:214
  233.0 1.5 dynamic-slice_bitcast_fusion.1
  234.5 4.5 %all-to-all-done.1 = bf16[4,32,512]{2,1,0:T(8,128)(2,1)S(1)} async-done(((bf16[4,32,512]{2,1,0:T(8,128)(2,1)}), bf16[4,32,512]{2,1,0:T(8,128)(2,1)S(1)}, u32[]{:S(2)}, u32[]{:S(2)}) %all-to-all-start.1) | async-done | bytes 131104 | tf_op jit(solution)/shard_map/all_to_all | solution.py:214
  239.0 11.7 %all-gather.1 = bf16[128,512]{1,0:T(8,128)(2,1)S(1)} all-gather(bf16[32,512]{1,0:T(8,128)(2,1)S(1)} %reduce_sum.48), channel_id=3, replica_groups={{0,32,64,96},{128,160,192,224},{256,288,320,352},{384,416,448,480},{1,3..., dimensions={0}, use_global_device_ids=true | all-gather | bytes 163840 | tf_op jit(solution)/shard_map/all_gather | solution.py:221
  250.8 13.9 %all-gather.2 = bf16[128,512]{1,0:T(8,128)(2,1)S(1)} all-gather(bf16[32,512]{1,0:T(8,128)(2,1)S(1)} %reduce_sum.50), channel_id=4, replica_groups={{0,128,256,384},{32,160,288,416},{64,192,320,448},{96,224,352,480},{1,1..., dimensions={0}, use_global_device_ids=true | all-gather | bytes 163840 | tf_op jit(solution)/shard_map/all_gather | solution.py:221
  264.7 0.6 fusion.4
  (49 shorter events, 0.2 us)
Async XLA Ops:
  7.2 76.1 %all-gather.5.cloned.1.call-start = ((), (), s32[]{:S(2)}) async-start(), calls=%async_computation.2 | async-start | bytes 5406720 | tf_op jit(solution)/shard_map/all_gather | solution.py:251
  83.3 0.9 copy-start.8
  84.2 0.9 copy-start.10
  85.2 0.8 copy-start.18
  86.0 0.7 copy-start.24
  92.2 20.8 %copy-start = (bf16[1536,1024]{1,0:T(8,128)(2,1)}, bf16[1536,1024]{1,0:T(8,128)(2,1)S(1)}, u32[]{:S(2)}) copy-start(bf16[1536,1024]{1,0:T(8,128)(2,1)S(1)} %get-tuple-element.15.wt) | copy-start | bytes 9437188
  92.2 20.8 %copy-start.13 = (bf16[160,1024]{1,0:T(8,128)(2,1)}, bf16[160,1024]{1,0:T(8,128)(2,1)S(1)}, u32[]{:S(2)}) copy-start(bf16[160,1024]{1,0:T(8,128)(2,1)S(1)} %get-tuple-element.23.normed) | copy-start | bytes 983044
  92.2 20.7 %copy-start.15 = (f32[160,512]{1,0:T(8,128)}, f32[160,512]{1,0:T(8,128)S(1)}, u32[]{:S(2)}) copy-start(f32[160,512]{1,0:T(8,128)S(1)} %get-tuple-element.22.part) | copy-start | bytes 983044
  92.2 20.7 %copy-start.22 = (bf16[128,1024]{1,0:T(8,128)(2,1)}, bf16[128,1024]{1,0:T(8,128)(2,1)S(1)}, u32[]{:S(2)}) copy-start(bf16[128,1024]{1,0:T(8,128)(2,1)S(1)} %get-tuple-element.16.qg) | copy-start | bytes 786436
  113.0 5.1 %copy-start.17 = (bf16[1,32,1024]{2,1,0:T(8,128)(2,1)S(1)}, bf16[1,32,1024]{2,1,0:T(8,128)(2,1)}, u32[]{:S(2)}) copy-start(bf16[1,32,1024]{2,1,0:T(8,128)(2,1)} %param.12) | copy-start | bytes 196612
  117.0 1.1 copy-start.2
  118.1 11.8 %copy-start.3 = (bf16[16,128,256]{2,1,0:T(8,128)(2,1)}, bf16[16,128,256]{2,1,0:T(8,128)(2,1)S(1)}, u32[]{:S(2)}) copy-start(bf16[16,128,256]{2,1,0:T(8,128)(2,1)S(1)} %get-tuple-element.21.zq) | copy-start | bytes 3145732
  118.1 13.7 %copy-start.25 = (f32[1024]{0:T(1024)S(1)}, f32[1024]{0:T(1024)}, u32[]{:S(2)}) copy-start(f32[1024]{0:T(1024)} %param.13) | copy-start | bytes 12292
  130.5 1.3 collective-permute-start
  131.8 1.2 copy-start.4
  133.0 0.8 copy-start.20
  145.9 1.3 collective-permute-start.1
  147.2 1.2 copy-start.5
  148.4 0.8 copy-start.21
  161.3 19.8 %collective-permute-start.2 = (bf16[32,1024]{1,0:T(8,128)(2,1)}, bf16[32,1024]{1,0:T(8,128)(2,1)}, u32[]{:S(2)}, u32[]{:S(2)}) collective-permute-start(bf16[32,1024]{1,0:T(8,128)(2,1)} %get-tuple-element.27), channel_id=1, source_target_pairs={{128,0},{160,32},{192,64},{224,96},{129,1},{161,33},{193,65},{225,... | collective-permute-start | bytes 196616 | tf_op jit(solution)/shard_map/ppermute | solution.py:290
  181.1 1.2 copy-start.6
  182.4 0.8 copy-start.19
  183.2 11.5 %copy-start.14 = (bf16[160,1024]{1,0:T(8,128)(2,1)S(1)}, bf16[160,1024]{1,0:T(8,128)(2,1)}, u32[]{:S(2)}) copy-start(bf16[160,1024]{1,0:T(8,128)(2,1)} %copy-done.13) | copy-start | bytes 983044
  183.2 11.5 %copy-start.16 = (f32[160,512]{1,0:T(8,128)S(1)}, f32[160,512]{1,0:T(8,128)}, u32[]{:S(2)}) copy-start(f32[160,512]{1,0:T(8,128)} %copy-done.15) | copy-start | bytes 983044
  194.7 3.8 %copy-start.7 = (bf16[160,1024]{1,0:T(8,128)(2,1)}, bf16[160,1024]{1,0:T(8,128)(2,1)S(1)}, u32[]{:S(2)}) copy-start(bf16[160,1024]{1,0:T(8,128)(2,1)S(1)} %shard_map.125.chain) | copy-start | bytes 983044
  198.5 1.0 copy-start.12
  198.5 1.8 copy-start.26
  198.5 12.3 %copy-start.1 = (bf16[1536,1024]{1,0:T(8,128)(2,1)S(1)}, bf16[1536,1024]{1,0:T(8,128)(2,1)}, u32[]{:S(2)}) copy-start(bf16[1536,1024]{1,0:T(8,128)(2,1)} %copy-done) | copy-start | bytes 9437188
  198.5 12.3 %copy-start.9 = (bf16[1,128,1024]{2,1,0:T(8,128)(2,1)S(1)}, bf16[1,128,1024]{2,1,0:T(8,128)(2,1)}, u32[]{:S(2)}) copy-start(bf16[1,128,1024]{2,1,0:T(8,128)(2,1)} %param.9) | copy-start | bytes 786436
  200.3 4.1 %collective-permute-start.3 = (bf16[16,32,512]{2,1,0:T(8,128)(2,1)}, bf16[16,32,512]{2,1,0:T(8,128)(2,1)}, u32[]{:S(2)}, u32[]{:S(2)}) collective-permute-start(bf16[16,32,512]{2,1,0:T(8,128)(2,1)} %dynamic-slice_bitcast_fusion), channel_id=1, source_target_pairs={{0,1},{1,0},{2,3},{3,2},{4,5},{5,4},{6,7},{7,6},{8,9},{9,8},{10,11... | collective-permute-start | bytes 1572872 | tf_op jit(solution)/shard_map/ppermute | solution.py:232
  206.6 20.3 %all-to-all-start = ((bf16[4,4,32,512]{3,2,1,0:T(8,128)(2,1)}), bf16[4,4,32,512]{3,2,1,0:T(8,128)(2,1)}, u32[]{:S(2)}, u32[]{:S(2)}) async-start(bf16[4,4,32,512]{3,2,1,0:T(8,128)(2,1)} %bitcast.46), calls=%async_computation | async-start | bytes 1048576 | tf_op jit(solution)/shard_map/all_to_all | solution.py:214
  210.8 1.0 copy-start.11
  211.7 0.9 copy-start.23
  212.7 0.9 copy-start.27
  228.7 10.2 %all-to-all-start.1 = ((bf16[4,32,512]{2,1,0:T(8,128)(2,1)}), bf16[4,32,512]{2,1,0:T(8,128)(2,1)S(1)}, u32[]{:S(2)}, u32[]{:S(2)}) async-start(bf16[4,32,512]{2,1,0:T(8,128)(2,1)} %reduce_sum.47), calls=%async_computation.1 | async-start | bytes 262144 | tf_op jit(solution)/shard_map/all_to_all | solution.py:214
Sparse Core Ops, SparseCore 0:
  11.7 71.5 all-gather.4

commit v2 on v1

v2 whole, which is shorter than its diff:
```python
import functools

import jax
import jax.numpy as jnp
from jax import lax
from jax.experimental import pallas as pl
from jax.experimental.pallas import tpu as pltpu
from jax.sharding import PartitionSpec as P

D = 1024
GROUPS = 4
PER_GROUP = 4
HEAD = 64
WIDE = PER_GROUP * HEAD
KV = GROUPS * HEAD
MEM = 32
TOK = 128
ROWS = MEM + TOK
SPAN = 4
EPS = 1e-05
SCALE = 0.125
BF = jnp.bfloat16
F32 = jnp.float32


def nn(a, b):
    return lax.dot_general(a, b, (((1,), (0,)), ((), ())), preferred_element_type=F32)


def nt(a, b):
    return lax.dot_general(a, b, (((1,), (1,)), ((), ())), preferred_element_type=F32)


def tn(a, b):
    return lax.dot_general(a, b, (((0,), (0,)), ((), ())), preferred_element_type=F32)


def normalised(rows, gain):
    inverse = lax.rsqrt(jnp.mean(rows * rows, axis=-1, keepdims=True) + EPS)
    return inverse, (rows * inverse * gain).astype(BF)


def norm_backward(cotangent, normed_grad, hidden, inverse, gain):
    scaled = normed_grad * gain
    mean = jnp.mean(scaled * hidden, axis=-1, keepdims=True)
    return cotangent + inverse * (scaled - hidden * (inverse * inverse * mean))


def repeated(rows, g):
    half = rows[:, (g // 2) * 128 : (g // 2) * 128 + 128].astype(F32)
    lane = lax.broadcasted_iota(jnp.int32, half.shape, 1)
    kept = jnp.where((lane < HEAD) == (g % 2 == 0), half, 0.0)
    both = kept + pltpu.roll(kept, HEAD, 1)
    return jnp.concatenate([both, both], axis=1).astype(BF)


def stacked(rows):
    rows = rows.astype(F32)
    lane = lax.broadcasted_iota(jnp.int32, rows.shape, 1) // HEAD
    return jnp.concatenate([jnp.where(lane == a, rows, 0.0) for a in range(PER_GROUP)], axis=0).astype(BF)


def unstacked(rows):
    n = rows.shape[0] // PER_GROUP
    lane = lax.broadcasted_iota(jnp.int32, (n, WIDE), 1) // HEAD
    total = jnp.zeros((n, WIDE), F32)
    for a in range(PER_GROUP):
        total = jnp.where(lane == a, rows[a * n : (a + 1) * n], total)
    return total


def folded(parts):
    sums = []
    for part in parts:
        half = part[:, :128] + part[:, 128:]
        sums.append(half + pltpu.roll(half, HEAD, 1))
    lane = lax.broadcasted_iota(jnp.int32, sums[0].shape, 1)
    return jnp.concatenate(
        [jnp.where(lane < HEAD, sums[0], sums[1]), jnp.where(lane < HEAD, sums[2], sums[3])], axis=1
    )


def centred(scores_sum_axis, probs, products):
    total = jnp.sum(products, axis=scores_sum_axis, keepdims=True)
    return ((products - probs * total) * SCALE).astype(BF)


def group_columns(g):
    return slice(g * WIDE, (g + 1) * WIDE)


def token_kernel(mem, tok, gout, gain, w, normed_out, qg_out, part_out, kvp_out, wt_out):
    hidden = jnp.concatenate([mem[...].astype(F32), tok[...].astype(F32)], axis=0)
    _, normed = normalised(hidden, gain[...])
    normed_out[...] = normed
    q = nn(normed[MEM:], w[:, :D])
    kv = nn(normed, w[:, D : D + 2 * KV]).astype(BF)
    up = nn(gout[...], w[:, D + 2 * KV :])
    k, v = kv[:, :KV], kv[:, KV:]
    key_at = lax.broadcasted_iota(jnp.int32, (ROWS, PER_GROUP * TOK), 0)
    row_at = lax.broadcasted_iota(jnp.int32, (ROWS, PER_GROUP * TOK), 1) % TOK
    seen = key_at <= row_at + MEM
    key_parts, value_parts = [], []
    for g in range(GROUPS):
        cols = group_columns(g)
        zq = stacked(q[:, cols])
        zu = stacked(up[:, cols])
        krep, vrep = repeated(k, g), repeated(v, g)
        raised = jnp.where(seen, jnp.exp(nt(krep, zq) * SCALE), 0.0)
        probs = raised * (1.0 / jnp.sum(raised, axis=0, keepdims=True))
        score_grad = centred(0, probs, probs * nt(vrep, zu))
        key_parts.append(nn(score_grad, zq))
        value_parts.append(nn(probs.astype(BF), zu))
        qg_out[:, cols] = unstacked(tn(score_grad, krep)).astype(BF)
    part = jnp.concatenate([folded(key_parts), folded(value_parts)], axis=1)
    part_out[...] = part
    for copy in range(SPAN):
        kvp_out[copy * ROWS : copy * ROWS + MEM, :] = part[:MEM].astype(BF)
        kvp_out[copy * ROWS + MEM : (copy + 1) * ROWS, :] = kv[MEM:]
    wt_out[...] = w[:, : D + 2 * KV].T


def mix_kernel(mem4, last, gain, w, wt, mixed_out, qkv_out, hw_out, inv_out, u_out):
    inverse, normed = normalised(mem4[...].astype(F32), gain[...])
    inv_out[...] = inverse
    hw_out[...] = nn(mem4[...], w[:, D + 2 * KV :])
    qkv_out[...] = nn(normed, w[:, : D + 2 * KV])
    u_out[...] = nn(last[...], w[:, D + 2 * KV :]).astype(BF)
    scaled = (wt[...].astype(F32) * gain[...]).astype(BF)
    mixed_out[...] = nn(scaled, w[:, D + 2 * KV :]).astype(BF)


def ready_kernel(qkv4, kvp4, probs_k_out, probs_q_out, krep_out, vrep_out, zq_out):
    for s in range(SPAN):
        rows = slice(s * MEM, (s + 1) * MEM)
        later = slice(s * ROWS + MEM, (s + 1) * ROWS)
        k = jnp.concatenate([qkv4[rows, D : D + KV].astype(BF), kvp4[later, :KV]], axis=0)
        v = jnp.concatenate([qkv4[rows, D + KV :].astype(BF), kvp4[later, KV:]], axis=0)
        zqs = [stacked(qkv4[rows, group_columns(g)]) for g in range(GROUPS)]
        kreps = [repeated(k, g) for g in range(GROUPS)]
        raised_k = [jnp.exp(nt(krep, zq) * SCALE) for krep, zq in zip(kreps, zqs)]
        raised_q = [jnp.exp(nt(zq, krep) * SCALE) for krep, zq in zip(kreps, zqs)]
        for g in range(GROUPS):
            at = s * GROUPS + g
            probs_k_out[at] = raised_k[g] * (1.0 / jnp.sum(raised_k[g], axis=0, keepdims=True))
            probs_q_out[at] = raised_q[g] * (1.0 / jnp.sum(raised_q[g], axis=1, keepdims=True))
            krep_out[at] = kreps[g]
            vrep_out[at] = repeated(v, g)
            zq_out[at] = zqs[g]


def chain_kernel(
    latched, fresh, arrived, before, mixed, probs_k, probs_q, krep, vrep, zq, qkv4, hw4, inv4, kvp4, send_out, u_out, grads_out
):
    up = arrived[...].astype(F32)
    if latched:
        up = jnp.where(fresh[0] == 1, up, before[(SPAN - 1) * MEM :, :].astype(F32))
    for s in reversed(range(SPAN)):
        rows = slice(s * MEM, (s + 1) * MEM)
        u_out[rows, :] = up.astype(BF)
        ats = range(s * GROUPS, (s + 1) * GROUPS)
        zus = [stacked(up[:, group_columns(g)]) for g in range(GROUPS)]
        by_query = [probs_q[at] * nt(zu, vrep[at]) for at, zu in zip(ats, zus)]
        by_key = [probs_k[at] * nt(vrep[at], zu) for at, zu in zip(ats, zus)]
        value_parts = [nn(probs_k[at, :MEM].astype(BF), zu) for at, zu in zip(ats, zus)]
        score_grads = [centred(1, probs_q[at], products) for at, products in zip(ats, by_query)]
        totals = [jnp.sum(products, axis=0, keepdims=True) for products in by_key]
        near_grads = [
            ((products[:MEM] - probs_k[at, :MEM] * total) * SCALE).astype(BF)
            for at, products, total in zip(ats, by_key, totals)
        ]
        query_grads = [unstacked(nn(grad, krep[at])) for at, grad in zip(ats, score_grads)]
        key_parts = [nn(grad, zq[at]) for at, grad in zip(ats, near_grads)]
        own = kvp4[s * ROWS : s * ROWS + MEM, :].astype(F32)
        kv_grad = jnp.concatenate([folded(key_parts), folded(value_parts)], axis=1) + own
        grads = jnp.concatenate(query_grads + [kv_grad], axis=1).astype(BF)
        grads_out[rows, :] = grads
        inverse = inv4[rows, :]
        along = jnp.sum(grads.astype(F32) * qkv4[rows, :], axis=-1, keepdims=True) * (inverse * inverse / D)
        up = up + inverse * nn(grads, mixed[...]) - along * hw4[rows, :]
    send_out[...] = up.astype(BF)


def weight_kernel(place, u4, probs, krep, vrep, zq, part, normed, kv_out, mine_out, other_out):
    r = place[0]
    up = u4[pl.ds(pl.multiple_of(r * MEM, MEM), MEM), :]
    ats = [r * GROUPS + g for g in range(GROUPS)]
    zus = [stacked(up[:, group_columns(g)]) for g in range(GROUPS)]
    ps = [probs[at] for at in ats]
    products = [p * nt(vrep[at], zu) for at, p, zu in zip(ats, ps, zus)]
    value_parts = [nn(p.astype(BF), zu) for p, zu in zip(ps, zus)]
    score_grads = [centred(0, p, product) for p, product in zip(ps, products)]
    key_parts = [nn(grad, zq[at]) for at, grad in zip(ats, score_grads)]
    kv_grad = jnp.concatenate([folded(key_parts), folded(value_parts)], axis=1) + part[...]
    kv_grad = kv_grad.astype(BF)
    kv_out[...] = kv_grad
    share = mine_out.shape[1]
    grad = tn(normed[...], kv_grad).reshape(mine_out.shape[0], 2, share, 2 * KV)
    first = place[1] == 0
    mine_out[...] = jnp.where(first, grad[:, 0], grad[:, 1]).astype(BF)
    other_out[...] = jnp.where(first, grad[:, 1], grad[:, 0]).astype(BF)


def memory_kernel(place, grads4, wt, mem4, inv4, gain, own_out, all_out):
    hidden, inverse = mem4[...].astype(F32), inv4[...]
    change = norm_backward(0.0, nn(grads4[...], wt[...]), hidden, inverse, gain[...])
    total = jnp.zeros((MEM, D), F32)
    own = jnp.zeros((MEM, D), F32)
    for s in reversed(range(SPAN)):
        total = total + change[s * MEM : (s + 1) * MEM]
        own = jnp.where(place[0] == s, total, own)
    own_out[...] = own
    for copy in range(all_out.shape[0]):
        all_out[copy] = total.astype(BF)


def rows_kernel(tok, gout, gain, wt, qg, kv_grad, out):
    hidden = tok[...].astype(F32)
    inverse, _ = normalised(hidden, gain[...])
    normed_grad = nn(qg[...], wt[:D, :]) + nn(kv_grad[MEM:, :], wt[D:, :])
    out[...] = norm_backward(gout[...].astype(F32), normed_grad, hidden, inverse, gain[...]).astype(BF)


def call(kernel, outs, args, flops, scalars=0):
    vmem = pl.BlockSpec(memory_space=pltpu.VMEM)
    smem = pl.BlockSpec(memory_space=pltpu.SMEM)
    moved = sum(a.size * a.dtype.itemsize for a in args) + sum(o.size * o.dtype.itemsize for o in outs)
    return pl.pallas_call(
        kernel,
        out_shape=outs,
        in_specs=[smem] * scalars + [vmem] * (len(args) - scalars),
        out_specs=[vmem] * len(outs),
        compiler_params=pltpu.CompilerParams(vmem_limit_bytes=20 * 1024 * 1024),
        cost_estimate=pl.CostEstimate(flops=flops, bytes_accessed=moved, transcendentals=0),
    )(*args)


def shape(dims, dtype=BF):
    return jax.ShapeDtypeStruct(dims, dtype)


def runs(axis_size, length, stride):
    block = length * stride
    return [
        [b + o + i * stride for i in range(length)] for b in range(0, axis_size, block) for o in range(stride)
    ]


def spread(block, axis, groups):
    return lax.all_to_all(block, axis, 0, 0, tiled=True, axis_index_groups=groups)


def reduced(mine, other):
    docs, n_seg = lax.axis_size("dp"), lax.axis_size("seg")
    got = lax.ppermute(other, "dp", [(i, i ^ 1) for i in range(docs)])
    block = (mine.astype(F32) + got.astype(F32)).astype(BF)
    if docs > 2:
        block = lax.all_to_all(block, "dp", 0, 0, tiled=True, axis_index_groups=runs(docs, docs // 2, 2))
    block = jnp.sum(block.astype(F32), axis=0).astype(BF)
    for length, stride in ((SPAN, 1), (n_seg // SPAN, SPAN)):
        copies = jnp.broadcast_to(block[None], (length,) + block.shape)
        got = spread(copies, "seg", runs(n_seg, length, stride))
        total = jnp.sum(got.astype(F32), axis=0)
        block = total.astype(BF)
    return total


def body(tokens, grad_output, memories, grad_last, norm_gain, query_weight, key_weight, value_weight, out_weight):
    position = lax.axis_index("seg")
    n_seg = lax.axis_size("seg")
    docs = lax.axis_size("dp")
    turns = n_seg // SPAN
    tok, gout, mem, last, gain = tokens[0], grad_output[0], memories[0, 0], grad_last[0], norm_gain[None]

    shard = jnp.concatenate([query_weight, key_weight, value_weight, out_weight.T], axis=1)
    w = lax.all_gather(shard, "dp", axis=0, tiled=True)
    near = runs(n_seg, SPAN, 1)
    mem4 = lax.all_gather(mem, "seg", axis=0, tiled=True, axis_index_groups=near)

    normed, qg, part, kvp, wt = call(
        token_kernel,
        [
            shape((ROWS, D)),
            shape((TOK, D)),
            shape((ROWS, 2 * KV), F32),
            shape((SPAN * ROWS, 2 * KV)),
            shape((D + 2 * KV, D)),
        ],
        (mem, tok, gout, gain, w),
        1_500_000_000,
    )
    kvp4 = spread(kvp, "seg", near)
    mixed, qkv4, hw4, inv4, arrived = call(
        mix_kernel,
        [
            shape((D + 2 * KV, D)),
            shape((SPAN * MEM, D + 2 * KV), F32),
            shape((SPAN * MEM, D), F32),
            shape((SPAN * MEM, 1), F32),
            shape((MEM, D)),
        ],
        (mem4, last, gain, w, wt),
        4_000_000_000,
    )
    count = SPAN * GROUPS
    probs_k, probs_q, krep, vrep, zq = call(
        ready_kernel,
        [
            shape((count, ROWS, PER_GROUP * MEM), F32),
            shape((count, PER_GROUP * MEM, ROWS), F32),
            shape((count, ROWS, WIDE)),
            shape((count, ROWS, WIDE)),
            shape((count, PER_GROUP * MEM, WIDE)),
        ],
        (qkv4, kvp4),
        400_000_000,
    )
    block = position // SPAN
    u4 = kvp4
    for turn in range(turns):
        fresh = (block == turns - 1 - turn).astype(jnp.int32)[None]
        send, u4, grads4 = call(
            functools.partial(chain_kernel, turn > 0),
            [shape((MEM, D)), shape((SPAN * MEM, D)), shape((SPAN * MEM, D + 2 * KV))],
            (fresh, arrived, u4, mixed, probs_k, probs_q, krep, vrep, zq, qkv4, hw4, inv4, kvp4),
            1_000_000_000,
            scalars=1,
        )
        if turn < turns - 1:
            route = [(i, i - SPAN) for i in range((turns - 1 - turn) * SPAN, (turns - turn) * SPAN)]
            arrived = lax.ppermute(send, "seg", route)
    place = jnp.stack([position % SPAN, lax.axis_index("dp") % 2]).astype(jnp.int32)
    half = (docs // 2, D // docs, 2 * KV)
    kv_grad, mine, other = call(
        weight_kernel,
        [shape((ROWS, 2 * KV)), shape(half), shape(half)],
        (place, u4, probs_k, krep, vrep, zq, part, normed),
        400_000_000,
        scalars=1,
    )
    total = reduced(mine, other) / docs
    own, change = call(
        memory_kernel,
        [shape((MEM, D), F32), shape((turns, MEM, D))],
        (place, grads4, wt, mem4, inv4, gain),
        400_000_000,
        scalars=1,
    )
    changes = spread(change, "seg", runs(n_seg, turns, SPAN))
    later = (jnp.arange(turns) > block)[:, None, None]
    after = jnp.sum(jnp.where(later, changes.astype(F32), 0.0), axis=0)
    grad_memories = (last.astype(F32) + after + own).astype(BF)
    (grad_tokens,) = call(rows_kernel, [shape((TOK, D))], (tok, gout, gain, wt, qg, kv_grad), 500_000_000)
    return (grad_tokens[None], grad_memories[None, None], total[:, :KV], total[:, KV:])


def solution(mesh):
    in_specs = (
        P("dp", "seg", None),
        P("dp", "seg", None),
        P("dp", "seg", None, None),
        P("dp", None, None),
        P(),
        P("dp", None),
        P("dp", None),
        P("dp", None),
        P(None, "dp"),
    )
    out_specs = (P("dp", "seg", None), P("dp", "seg", None, None), P("dp", None), P("dp", None))
    return jax.shard_map(body, mesh=mesh, in_specs=in_specs, out_specs=out_specs, check_vma=False)
```

time: 273 us -> 288 us (1.055)
  blocking collectives: 58.6 us -> 17.2 us
  local copies, waits for them, and re-layouts: 22.5 us -> 51.5 us
  waiting for transfers between devices: 95.9 us -> 122 us
  Pallas kernels: 60.7 us -> 39.1 us
  starting transfers between devices: 14.4 us -> 35 us
    all_gather x3 -> x0, blocking collectives: 43.2 us -> none  [the longest x2 25.6 us: summed(): got = lax.all_gather(block, 'seg', axis=0, axis_index_groups=groups)]
    unnamed x56 -> x118, local copies, waits for them, and re-layouts: 14.5 us -> 49.5 us
    pallas_call x8 -> x10, Pallas kernels: 60.7 us -> 39.1 us  [call(): pl.pallas_call(kernel, out_shape=outs, in_specs=[smem] * scalars + [vmem]...]
    all_to_all x2 -> x5, starting transfers between devices: 8.38 us -> 29.2 us  [the longest x4 23 us: spread(): lax.all_to_all(block, axis, 0, 0, tiled=True, axis_index_groups=groups)]
    all_gather x1, waiting for transfers between devices: 59 us -> 74.5 us  [body(): w = lax.all_gather(shard, 'dp', axis=0, tiled=True)]
    all_to_all x2 -> x5, waiting for transfers between devices: 16.4 us -> 27 us  [the longest x4 15.8 us: spread(): lax.all_to_all(block, axis, 0, 0, tiled=True, axis_index_groups=groups)]
    slice x4 -> x0, local copies, waits for them, and re-layouts: 5.09 us -> none  [the longest x1 3.13 us: body(): wo = w[:, D + 2 * KV:]]
  transfers between devices with their start and end apart: 7 -> 10, of which waited for: 5 -> 6; matrix products, arithmetic and copies ran while one was open for 1% -> 1% of each run, Pallas kernels for 1% -> 3%
where the time goes in v2:
time: 288 us; the launch traced here: 286 us
  waiting for transfers between devices  122 us (42%)
  local copies, waits for them, and re-layouts  51.5 us (18%)
  Pallas kernels  39.1 us (14%)
  starting transfers between devices  35 us (12%)
  blocking collectives  17.2 us (6%)
  between operations  14.3 us (5%)
  other arithmetic  7.35 us (3%)
    all_gather x1, waiting for transfers between devices, body(): w = lax.all_gather(shard, 'dp', axis=0, tiled=True)  74.5 us
    unnamed x118, local copies, waits for them, and re-layouts  49.5 us
    pallas_call x10, Pallas kernels, call(): pl.pallas_call(kernel, out_shape=outs, in_specs=[smem] * scalars + [vmem]...  39.1 us
    all_to_all x4, starting transfers between devices, spread(): lax.all_to_all(block, axis, 0, 0, tiled=True, axis_index_groups=groups)  23 us
    ppermute x3, waiting for transfers between devices, body(): arrived = lax.ppermute(send, 'seg', route)  18.4 us
    all_gather x1, blocking collectives, body(): lax.all_gather(mem, 'seg', axis=0, tiled=True, axis_index_groups=near)  17.2 us
    all_to_all x4, waiting for transfers between devices, spread(): lax.all_to_all(block, axis, 0, 0, tiled=True, axis_index_groups=groups)  15.8 us
    all_to_all x1, waiting for transfers between devices, reduced(): lax.all_to_all(block, 'dp', 0, 0, tiled=True, axis_index_groups=runs(docs...  11.2 us
  transfers between devices with their start and end apart: 10, of which 6 were waited for; matrix products, arithmetic and copies ran while one was open for 1% of the time, Pallas kernels for 3%

profile of v2, /device:TPU:8, one launch (start us, length us, event | category | flops | bytes accessed | tf_op | source)
XLA Modules:
  0.0 286.1 jit_solution(1093383453842440670)
XLA Ops:
  7.2 1.6 pad_maximum_fusion
  8.8 74.5 %all-gather.3.cloned.1.call-done.w = bf16[1024,2560]{1,0:T(8,128)(2,1)} async-done(((bf16[32,2560]{1,0:T(8,128)(2,1)}), bf16[1024,2560]{1,0:T(8,128)(2,1)}) %all-gather.3.cloned.1.call-update) | async-done | bytes 5242896 | tf_op jit(solution)/shard_map/all_gather | solution.py:276
  83.3 2.5 copy-done.29
  89.2 3.9 %shard_map.120 = (bf16[160,1024]{1,0:T(8,128)(2,1)S(1)}, bf16[128,1024]{1,0:T(8,128)(2,1)S(1)}, f32[160,512]{1,0:T(8,128)S(1)}, bf16[640,512]{1,0:T(8,128)(2,1)}, bf16[1536,1024]{1,0:T(8,128)(2,1)S(1)}) custom-call(bf16[32,1024]{1,0:T(8,128)(2,1)S(1)} %bitcast.25, bf16[128,1024]{1,0:T(8,128)(2,1)S(1)} %bitcast.19, bf16[128,1024]{1,0:T(8,128)(2,1)S(1)} %bitcast.21, ...), custom_call_target="tpu_custom_call" | custom-call | flops 1500000000 | bytes 10555392 | tf_op jit(solution)/shard_map/pallas_call | solution.py:228
  93.1 1.7 copy-done.21
  96.3 7.0 %all-to-all-start = ((bf16[4,160,512]{2,1,0:T(8,128)(2,1)}), bf16[4,160,512]{2,1,0:T(8,128)(2,1)}, u32[]{:S(2)}, u32[]{:S(2)}) async-start(bf16[4,160,512]{2,1,0:T(8,128)(2,1)} %bitcast.13), calls=%async_computation | async-start | bytes 1310720 | tf_op jit(solution)/shard_map/all_to_all | solution.py:250
  103.3 17.2 %all-gather = bf16[1,1,128,1024]{3,2,1,0:T(8,128)(2,1)S(1)} all-gather(bf16[1,1,32,1024]{3,2,1,0:T(8,128)(2,1)S(1)} %copy-done.42), channel_id=2, replica_groups={{0,32,64,96},{128,160,192,224},{256,288,320,352},{384,416,448,480},{1,3..., dimensions={2}, use_global_device_ids=true | all-gather | bytes 327680 | tf_op jit(solution)/shard_map/all_gather | solution.py:278
  120.5 1.9 copy-done.22
  122.4 2.5 copy-done.30
  125.7 4.6 %shard_map.121 = (bf16[1536,1024]{1,0:T(8,128)(2,1)S(1)}, f32[128,1536]{1,0:T(8,128)S(1)}, f32[128,1024]{1,0:T(8,128)S(1)}, f32[128,1]{1,0:T(8,128)S(1)}, bf16[32,1024]{1,0:T(8,128)(2,1)S(1)}) custom-call(bf16[128,1024]{1,0:T(8,128)(2,1)S(1)} %bitcast.23, bf16[32,1024]{1,0:T(8,128)(2,1)S(1)} %bitcast.26, f32[1,1024]{1,0:T(1,128)S(1)} %bitcast.28, ...), custom_call_target="tpu_custom_call" | custom-call | flops 4000000000 | bytes 13242880 | tf_op jit(solution)/shard_map/pallas_call | solution.py:228
  133.3 1.1 copy-done.17
  134.5 2.8 shard_map.122
  137.3 1.4 copy-done.25
  139.7 6.1 %shard_map.123 = (bf16[32,1024]{1,0:T(8,128)(2,1)}, bf16[128,1024]{1,0:T(8,128)(2,1)S(1)}, bf16[128,1536]{1,0:T(8,128)(2,1)}) custom-call(s32[1]{0:T(128)} %bitcast.10.fresh, bf16[32,1024]{1,0:T(8,128)(2,1)S(1)} %copy-done.54, bf16[640,512]{1,0:T(8,128)(2,1)} %bitcast.14.kvp4.before, bf16[1536,1024]{1,0:T(8,128)(2,1)S(1)} %get-tuple-element.36.mixed, ...), custom_call_target="tpu_custom_call" | custom-call | flops 1000000000 | bytes 12845572 | tf_op jit(solution)/shard_map/pallas_call | solution.py:228
  146.5 1.3 collective-permute-start
  147.8 1.6 copy-done.1
  149.4 1.3 copy-done.4
  150.7 1.3 copy-done.8
  152.0 1.3 copy-done.11
  153.3 1.2 copy-done.14
  154.5 1.1 copy-done.18
  157.7 5.8 %shard_map.124 = (bf16[32,1024]{1,0:T(8,128)(2,1)}, bf16[128,1024]{1,0:T(8,128)(2,1)S(1)}, bf16[128,1536]{1,0:T(8,128)(2,1)}) custom-call(s32[1]{0:T(128)} %bitcast.9.fresh, bf16[32,1024]{1,0:T(8,128)(2,1)} %collective-permute-done.arrived, bf16[128,1024]{1,0:T(8,128)(2,1)S(1)} %copy-done.48, bf16[1536,1024]{1,0:T(8,128)(2,1)S(1)} %get-tuple-element.36.mixed, ...), custom_call_target="tpu_custom_call" | custom-call | flops 1000000000 | bytes 12452356 | tf_op jit(solution)/shard_map/pallas_call | solution.py:228
  164.1 1.3 collective-permute-start.1
  165.4 1.6 copy-done.2
  167.0 1.3 copy-done.5
  168.3 1.3 copy-done.9
  169.6 1.3 copy-done.12
  170.9 1.2 copy-done.15
  172.2 1.1 copy-done.19
  175.3 5.8 %shard_map.125 = (bf16[32,1024]{1,0:T(8,128)(2,1)S(1)}, bf16[128,1024]{1,0:T(8,128)(2,1)S(1)}, bf16[128,1536]{1,0:T(8,128)(2,1)}) custom-call(s32[1]{0:T(128)} %bitcast.8.fresh, bf16[32,1024]{1,0:T(8,128)(2,1)} %collective-permute-done.1.arrived, bf16[128,1024]{1,0:T(8,128)(2,1)S(1)} %copy-done.46, bf16[1536,1024]{1,0:T(8,128)(2,1)S(1)} %get-tuple-element.36.mixed, ...), custom_call_target="tpu_custom_call" | custom-call | flops 1000000000 | bytes 12452356 | tf_op jit(solution)/shard_map/pallas_call | solution.py:228
  181.1 1.3 collective-permute-start.2
  182.5 18.4 %collective-permute-done.2.arrived = bf16[32,1024]{1,0:T(8,128)(2,1)S(1)} collective-permute-done((bf16[32,1024]{1,0:T(8,128)(2,1)S(1)}, bf16[32,1024]{1,0:T(8,128)(2,1)S(1)}, u32[]{:S(2)}, u32[]{:S(2)}) %collective-permute-start.2) | collective-permute-done | bytes 65568 | tf_op jit(solution)/shard_map/ppermute | solution.py:331
  200.9 5.8 %shard_map.126 = (bf16[32,1024]{1,0:T(8,128)(2,1)}, bf16[128,1024]{1,0:T(8,128)(2,1)S(1)}, bf16[128,1536]{1,0:T(8,128)(2,1)S(1)}) custom-call(s32[1]{0:T(128)} %bitcast.7.fresh, bf16[32,1024]{1,0:T(8,128)(2,1)S(1)} %collective-permute-done.2.arrived, bf16[128,1024]{1,0:T(8,128)(2,1)S(1)} %get-tuple-element.50.before, ...), custom_call_target="tpu_custom_call" | custom-call | flops 1000000000 | bytes 12452356 | tf_op jit(solution)/shard_map/pallas_call | solution.py:228
  207.5 1.5 shard_map.127
  209.7 1.9 collective-permute-start.3
  211.6 1.9 collective-permute-done.3
  214.4 6.2 %all-to-all-start.2 = ((bf16[16,32,512]{2,1,0:T(8,128)(2,1)}), bf16[16,32,512]{2,1,0:T(8,128)(2,1)}, u32[]{:S(2)}, u32[]{:S(2)}) async-start(bf16[16,32,512]{2,1,0:T(8,128)(2,1)} %add_convert_fusion), calls=%async_computation.2 | async-start | bytes 1048576 | tf_op jit(solution)/shard_map/all_to_all | solution.py:258
  222.6 1.4 shard_map.129
  225.3 11.2 %all-to-all-done.2 = bf16[16,32,512]{2,1,0:T(8,128)(2,1)} async-done(((bf16[16,32,512]{2,1,0:T(8,128)(2,1)}), bf16[16,32,512]{2,1,0:T(8,128)(2,1)}, u32[]{:S(2)}, u32[]{:S(2)}) %all-to-all-start.2) | async-done | bytes 524320 | tf_op jit(solution)/shard_map/all_to_all | solution.py:258
  236.5 4.0 %all-to-all-start.1 = ((bf16[4,32,1024]{2,1,0:T(8,128)(2,1)}), bf16[4,32,1024]{2,1,0:T(8,128)(2,1)}, u32[]{:S(2)}, u32[]{:S(2)}) async-start(bf16[4,32,1024]{2,1,0:T(8,128)(2,1)} %copy-done.49), calls=%async_computation.1 | async-start | bytes 524288 | tf_op jit(solution)/shard_map/all_to_all | solution.py:250
  240.6 1.1 reduce_sum.43
  241.7 8.3 %all-to-all-done.1 = bf16[4,32,1024]{2,1,0:T(8,128)(2,1)} async-done(((bf16[4,32,1024]{2,1,0:T(8,128)(2,1)}), bf16[4,32,1024]{2,1,0:T(8,128)(2,1)}, u32[]{:S(2)}, u32[]{:S(2)}) %all-to-all-start.1) | async-done | bytes 262176 | tf_op jit(solution)/shard_map/all_to_all | solution.py:250
  250.7 8.6 %all-to-all-start.3 = ((bf16[4,32,512]{2,1,0:T(8,128)(2,1)}), bf16[4,32,512]{2,1,0:T(8,128)(2,1)}, u32[]{:S(2)}, u32[]{:S(2)}) async-start(bf16[4,32,512]{2,1,0:T(8,128)(2,1)} %broadcast_in_dim.67), calls=%async_computation.3 | async-start | bytes 262144 | tf_op jit(solution)/shard_map/all_to_all | solution.py:250
  262.1 1.4 shard_map.128
  263.5 1.1 select_reduce_fusion
  266.2 3.3 %all-to-all-start.4 = ((bf16[4,32,512]{2,1,0:T(8,128)(2,1)}), bf16[4,32,512]{2,1,0:T(8,128)(2,1)S(1)}, u32[]{:S(2)}, u32[]{:S(2)}) async-start(bf16[4,32,512]{2,1,0:T(8,128)(2,1)} %broadcast_in_dim.68), calls=%async_computation.4 | async-start | bytes 262144 | tf_op jit(solution)/shard_map/all_to_all | solution.py:250
  269.6 1.6 fusion
  271.1 7.5 %all-to-all-done.4 = bf16[4,32,512]{2,1,0:T(8,128)(2,1)S(1)} async-done(((bf16[4,32,512]{2,1,0:T(8,128)(2,1)}), bf16[4,32,512]{2,1,0:T(8,128)(2,1)S(1)}, u32[]{:S(2)}, u32[]{:S(2)}) %all-to-all-start.4) | async-done | bytes 131104 | tf_op jit(solution)/shard_map/all_to_all | solution.py:250
  (115 shorter events, 26.6 us)
Async XLA Ops:
  7.2 76.1 %all-gather.3.cloned.1.call-start = ((), (), s32[]{:S(2)}) async-start(), calls=%async_computation.5 | async-start | bytes 5406720 | tf_op jit(solution)/shard_map/all_gather | solution.py:276
  83.3 2.5 copy-start.29
  85.8 0.9 copy-start.31
  89.2 14.1 %copy-start.42 = (bf16[1,1,32,1024]{3,2,1,0:T(8,128)(2,1)S(1)}, bf16[1,1,32,1024]{3,2,1,0:T(8,128)(2,1)}, u32[]{:S(2)}) copy-start(bf16[1,1,32,1024]{3,2,1,0:T(8,128)(2,1)} %param.11) | copy-start | bytes 196612
  89.2 31.3 %copy-start.58 = (f32[1024]{0:T(1024)S(1)}, f32[1024]{0:T(1024)}, u32[]{:S(2)}) copy-start(f32[1024]{0:T(1024)} %param.13) | copy-start | bytes 12292
  93.1 1.7 copy-start.21
  96.3 37.1 %all-to-all-start = ((bf16[4,160,512]{2,1,0:T(8,128)(2,1)}), bf16[4,160,512]{2,1,0:T(8,128)(2,1)}, u32[]{:S(2)}, u32[]{:S(2)}) async-start(bf16[4,160,512]{2,1,0:T(8,128)(2,1)} %bitcast.13), calls=%async_computation | async-start | bytes 1310720 | tf_op jit(solution)/shard_map/all_to_all | solution.py:250
  120.5 1.9 copy-start.22
  122.4 2.5 copy-start.30
  133.3 1.1 copy-start.17
  137.3 8.5 %copy-start = (f32[16,128,160]{2,1,0:T(8,128)}, f32[16,128,160]{2,1,0:T(8,128)S(1)}, u32[]{:S(2)}) copy-start(f32[16,128,160]{2,1,0:T(8,128)S(1)} %get-tuple-element.39.probs_q) | copy-start | bytes 3932164
  137.3 8.5 %copy-start.3 = (f32[16,160,128]{2,1,0:T(8,128)}, f32[16,160,128]{2,1,0:T(8,128)S(1)}, u32[]{:S(2)}) copy-start(f32[16,160,128]{2,1,0:T(8,128)S(1)} %get-tuple-element.38.probs_k.probs) | copy-start | bytes 3932164
  137.3 8.4 %copy-start.7 = (bf16[16,160,256]{2,1,0:T(8,128)(2,1)}, bf16[16,160,256]{2,1,0:T(8,128)(2,1)S(1)}, u32[]{:S(2)}) copy-start(bf16[16,160,256]{2,1,0:T(8,128)(2,1)S(1)} %get-tuple-element.40.krep) | copy-start | bytes 3932164
  137.3 8.4 %copy-start.10 = (bf16[16,160,256]{2,1,0:T(8,128)(2,1)}, bf16[16,160,256]{2,1,0:T(8,128)(2,1)S(1)}, u32[]{:S(2)}) copy-start(bf16[16,160,256]{2,1,0:T(8,128)(2,1)S(1)} %get-tuple-element.41.vrep) | copy-start | bytes 3932164
  137.3 8.4 %copy-start.13 = (bf16[16,128,256]{2,1,0:T(8,128)(2,1)}, bf16[16,128,256]{2,1,0:T(8,128)(2,1)S(1)}, u32[]{:S(2)}) copy-start(bf16[16,128,256]{2,1,0:T(8,128)(2,1)S(1)} %get-tuple-element.42.zq) | copy-start | bytes 3145732
  137.3 1.4 copy-start.25
  146.5 1.3 collective-permute-start
  147.8 1.6 copy-start.1
  149.4 1.3 copy-start.4
  150.7 1.3 copy-start.8
  152.0 1.3 copy-start.11
  153.3 1.2 copy-start.14
  154.5 1.1 copy-start.18
  155.7 1.0 copy-start.26
  164.1 1.3 collective-permute-start.1
  165.4 1.6 copy-start.2
  167.0 1.3 copy-start.5
  168.3 1.3 copy-start.9
  169.6 1.3 copy-start.12
  170.9 1.2 copy-start.15
  172.2 1.1 copy-start.19
  173.3 1.0 copy-start.27
  175.3 25.6 %copy-start.20 = (f32[128,1536]{1,0:T(8,128)S(1)}, f32[128,1536]{1,0:T(8,128)}, u32[]{:S(2)}) copy-start(f32[128,1536]{1,0:T(8,128)} %copy-done.16) | copy-start | bytes 2359300
  175.3 25.6 %copy-start.28 = (f32[128,1024]{1,0:T(8,128)S(1)}, f32[128,1024]{1,0:T(8,128)}, u32[]{:S(2)}) copy-start(f32[128,1024]{1,0:T(8,128)} %copy-done.24) | copy-start | bytes 1572868
  181.1 19.8 %collective-permute-start.2 = (bf16[32,1024]{1,0:T(8,128)(2,1)S(1)}, bf16[32,1024]{1,0:T(8,128)(2,1)S(1)}, u32[]{:S(2)}, u32[]{:S(2)}) collective-permute-start(bf16[32,1024]{1,0:T(8,128)(2,1)S(1)} %get-tuple-element.49), channel_id=1, source_target_pairs={{128,0},{160,32},{192,64},{224,96},{129,1},{161,33},{193,65},{225,... | collective-permute-start | bytes 196616 | tf_op jit(solution)/shard_map/ppermute | solution.py:331
  200.9 6.6 %copy-start.6 = (f32[16,160,128]{2,1,0:T(8,128)S(1)}, f32[16,160,128]{2,1,0:T(8,128)}, u32[]{:S(2)}) copy-start(f32[16,160,128]{2,1,0:T(8,128)} %copy-done.3) | copy-start | bytes 3932164
  200.9 6.6 %copy-start.40 = (f32[160,512]{1,0:T(8,128)S(1)}, f32[160,512]{1,0:T(8,128)}, u32[]{:S(2)}) copy-start(f32[160,512]{1,0:T(8,128)} %copy-done.39) | copy-start | bytes 983044
  207.5 13.1 %copy-start.23 = (bf16[1536,1024]{1,0:T(8,128)(2,1)S(1)}, bf16[1536,1024]{1,0:T(8,128)(2,1)}, u32[]{:S(2)}) copy-start(bf16[1536,1024]{1,0:T(8,128)(2,1)} %copy-done.21) | copy-start | bytes 9437188
  209.7 3.8 %collective-permute-start.3 = (bf16[16,32,512]{2,1,0:T(8,128)(2,1)S(1)}, bf16[16,32,512]{2,1,0:T(8,128)(2,1)S(1)}, u32[]{:S(2)}, u32[]{:S(2)}) collective-permute-start(bf16[16,32,512]{2,1,0:T(8,128)(2,1)S(1)} %get-tuple-element.59), channel_id=1, source_target_pairs={{0,1},{1,0},{2,3},{3,2},{4,5},{5,4},{6,7},{7,6},{8,9},{9,8},{10,11... | collective-permute-start | bytes 1572872 | tf_op jit(solution)/shard_map/ppermute | solution.py:255
  214.4 22.1 %all-to-all-start.2 = ((bf16[16,32,512]{2,1,0:T(8,128)(2,1)}), bf16[16,32,512]{2,1,0:T(8,128)(2,1)}, u32[]{:S(2)}, u32[]{:S(2)}) async-start(bf16[16,32,512]{2,1,0:T(8,128)(2,1)} %add_convert_fusion), calls=%async_computation.2 | async-start | bytes 1048576 | tf_op jit(solution)/shard_map/all_to_all | solution.py:258
  220.7 1.0 copy-start.36
  221.6 1.0 copy-start.38
  222.6 36.6 %copy-start.32 = (bf16[1,128,1024]{2,1,0:T(8,128)(2,1)S(1)}, bf16[1,128,1024]{2,1,0:T(8,128)(2,1)}, u32[]{:S(2)}) copy-start(bf16[1,128,1024]{2,1,0:T(8,128)(2,1)} %param.9) | copy-start | bytes 786436
  236.5 13.5 %all-to-all-start.1 = ((bf16[4,32,1024]{2,1,0:T(8,128)(2,1)}), bf16[4,32,1024]{2,1,0:T(8,128)(2,1)}, u32[]{:S(2)}, u32[]{:S(2)}) async-start(bf16[4,32,1024]{2,1,0:T(8,128)(2,1)} %copy-done.49), calls=%async_computation.1 | async-start | bytes 524288 | tf_op jit(solution)/shard_map/all_to_all | solution.py:250
  250.7 14.0 %all-to-all-start.3 = ((bf16[4,32,512]{2,1,0:T(8,128)(2,1)}), bf16[4,32,512]{2,1,0:T(8,128)(2,1)}, u32[]{:S(2)}, u32[]{:S(2)}) async-start(bf16[4,32,512]{2,1,0:T(8,128)(2,1)} %broadcast_in_dim.67), calls=%async_computation.3 | async-start | bytes 262144 | tf_op jit(solution)/shard_map/all_to_all | solution.py:250
  259.3 1.0 copy-start.34
  262.1 7.5 %copy-start.56 = (bf16[1,32,1024]{2,1,0:T(8,128)(2,1)S(1)}, bf16[1,32,1024]{2,1,0:T(8,128)(2,1)}, u32[]{:S(2)}) copy-start(bf16[1,32,1024]{2,1,0:T(8,128)(2,1)} %param.12) | copy-start | bytes 196612
  266.2 12.4 %all-to-all-start.4 = ((bf16[4,32,512]{2,1,0:T(8,128)(2,1)}), bf16[4,32,512]{2,1,0:T(8,128)(2,1)S(1)}, u32[]{:S(2)}, u32[]{:S(2)}) async-start(bf16[4,32,512]{2,1,0:T(8,128)(2,1)} %broadcast_in_dim.68), calls=%async_computation.4 | async-start | bytes 262144 | tf_op jit(solution)/shard_map/all_to_all | solution.py:250
  (21 other events, 16.6 us)
Sparse Core Ops, SparseCore 0:
  11.7 71.5 all-gather.2

commit v3 on v2

--- a/solution.py
+++ b/solution.py
@@ -89,12 +89,38 @@
     return slice(g * WIDE, (g + 1) * WIDE)
 
 
-def token_kernel(mem, tok, gout, gain, w, normed_out, qg_out, part_out, kvp_out, wt_out):
+def loads(pairs, sems):
+    copies = [pltpu.make_async_copy(src, dst, sems.at[i]) for i, (src, dst) in enumerate(pairs)]
+    for copy in copies:
+        copy.start()
+    return copies
+
+
+def token_kernel(
+    mem_hbm, tok_hbm, gout_hbm, gain_hbm, w_hbm, normed_out, qg_out, part_out, kvp_out, wt_out, w, mem, tok, gout, gain, sems
+):
+    first, second = slice(0, D + 2 * KV), slice(D + 2 * KV, 2 * D + 2 * KV)
+    copies = loads(
+        [
+            (mem_hbm, mem),
+            (tok_hbm, tok),
+            (gain_hbm, gain),
+            (w_hbm.at[:, first], w.at[:, first]),
+            (gout_hbm, gout),
+            (w_hbm.at[:, second], w.at[:, second]),
+        ],
+        sems,
+    )
+    for copy in copies[:3]:
+        copy.wait()
     hidden = jnp.concatenate([mem[...].astype(F32), tok[...].astype(F32)], axis=0)
     _, normed = normalised(hidden, gain[...])
     normed_out[...] = normed
+    copies[3].wait()
     q = nn(normed[MEM:], w[:, :D])
     kv = nn(normed, w[:, D : D + 2 * KV]).astype(BF)
+    copies[4].wait()
+    copies[5].wait()
     up = nn(gout[...], w[:, D + 2 * KV :])
     k, v = kv[:, :KV], kv[:, KV:]
     key_at = lax.broadcasted_iota(jnp.int32, (ROWS, PER_GROUP * TOK), 0)
@@ -114,13 +140,14 @@
         qg_out[:, cols] = unstacked(tn(score_grad, krep)).astype(BF)
     part = jnp.concatenate([folded(key_parts), folded(value_parts)], axis=1)
     part_out[...] = part
-    for copy in range(SPAN):
-        kvp_out[copy * ROWS : copy * ROWS + MEM, :] = part[:MEM].astype(BF)
-        kvp_out[copy * ROWS + MEM : (copy + 1) * ROWS, :] = kv[MEM:]
+    kvp_out[:MEM, :] = part[:MEM].astype(BF)
+    kvp_out[MEM:, :] = kv[MEM:]
     wt_out[...] = w[:, : D + 2 * KV].T
 
 
-def mix_kernel(mem4, last, gain, w, wt, mixed_out, qkv_out, hw_out, inv_out, u_out):
+def mix_kernel(mem4_hbm, last_hbm, gain_hbm, w, wt, mixed_out, qkv_out, hw_out, inv_out, u_out, mem4, last, gain, sems):
+    for copy in loads([(mem4_hbm, mem4), (last_hbm, last), (gain_hbm, gain)], sems):
+        copy.wait()
     inverse, normed = normalised(mem4[...].astype(F32), gain[...])
     inv_out[...] = inverse
     hw_out[...] = nn(mem4[...], w[:, D + 2 * KV :])
@@ -130,13 +157,16 @@
     mixed_out[...] = nn(scaled, w[:, D + 2 * KV :]).astype(BF)
 
 
-def ready_kernel(qkv4, kvp4, probs_k_out, probs_q_out, krep_out, vrep_out, zq_out):
-    for s in range(SPAN):
-        rows = slice(s * MEM, (s + 1) * MEM)
-        later = slice(s * ROWS + MEM, (s + 1) * ROWS)
-        k = jnp.concatenate([qkv4[rows, D : D + KV].astype(BF), kvp4[later, :KV]], axis=0)
-        v = jnp.concatenate([qkv4[rows, D + KV :].astype(BF), kvp4[later, KV:]], axis=0)
-        zqs = [stacked(qkv4[rows, group_columns(g)]) for g in range(GROUPS)]
+def ready_kernel(place, qkv4, *refs):
+    parts, (probs_k_out, probs_q_out, krep_out, vrep_out, zq_out, near_out) = refs[:SPAN], refs[SPAN:]
+    for ahead, kvp in enumerate(parts):
+        s = (place[0] + ahead) % SPAN
+        rows = pl.ds(pl.multiple_of(s * MEM, MEM), MEM)
+        qkv = qkv4[rows, :]
+        near_out[rows, :] = kvp[:MEM, :].astype(F32)
+        k = jnp.concatenate([qkv[:, D : D + KV].astype(BF), kvp[MEM:, :KV]], axis=0)
+        v = jnp.concatenate([qkv[:, D + KV :].astype(BF), kvp[MEM:, KV:]], axis=0)
+        zqs = [stacked(qkv[:, group_columns(g)]) for g in range(GROUPS)]
         kreps = [repeated(k, g) for g in range(GROUPS)]
         raised_k = [jnp.exp(nt(krep, zq) * SCALE) for krep, zq in zip(kreps, zqs)]
         raised_q = [jnp.exp(nt(zq, krep) * SCALE) for krep, zq in zip(kreps, zqs)]
@@ -150,11 +180,11 @@
 
 
 def chain_kernel(
-    latched, fresh, arrived, before, mixed, probs_k, probs_q, krep, vrep, zq, qkv4, hw4, inv4, kvp4, send_out, u_out, grads_out
+    turn, place, arrived, before, mixed, probs_k, probs_q, krep, vrep, zq, qkv4, hw4, inv4, near, send_out, u_out, grads_out
 ):
     up = arrived[...].astype(F32)
-    if latched:
-        up = jnp.where(fresh[0] == 1, up, before[(SPAN - 1) * MEM :, :].astype(F32))
+    if turn > 0:
+        up = jnp.where(place[2] == turn, up, before[(SPAN - 1) * MEM :, :].astype(F32))
     for s in reversed(range(SPAN)):
         rows = slice(s * MEM, (s + 1) * MEM)
         u_out[rows, :] = up.astype(BF)
@@ -171,8 +201,7 @@
         ]
         query_grads = [unstacked(nn(grad, krep[at])) for at, grad in zip(ats, score_grads)]
         key_parts = [nn(grad, zq[at]) for at, grad in zip(ats, near_grads)]
-        own = kvp4[s * ROWS : s * ROWS + MEM, :].astype(F32)
-        kv_grad = jnp.concatenate([folded(key_parts), folded(value_parts)], axis=1) + own
+        kv_grad = jnp.concatenate([folded(key_parts), folded(value_parts)], axis=1) + near[rows, :]
         grads = jnp.concatenate(query_grads + [kv_grad], axis=1).astype(BF)
         grads_out[rows, :] = grads
         inverse = inv4[rows, :]
@@ -211,7 +240,8 @@
         own = jnp.where(place[0] == s, total, own)
     own_out[...] = own
     for copy in range(all_out.shape[0]):
-        all_out[copy] = total.astype(BF)
+        all_out[copy, :MEM, :] = total[:, : 2 * KV].astype(BF)
+        all_out[copy, MEM:, :] = total[:, 2 * KV :].astype(BF)
 
 
 def rows_kernel(tok, gout, gain, wt, qg, kv_grad, out):
@@ -221,15 +251,20 @@
     out[...] = norm_backward(gout[...].astype(F32), normed_grad, hidden, inverse, gain[...]).astype(BF)
 
 
-def call(kernel, outs, args, flops, scalars=0):
+def call(kernel, outs, args, flops, scalars=0, far=0, scratch=()):
     vmem = pl.BlockSpec(memory_space=pltpu.VMEM)
     smem = pl.BlockSpec(memory_space=pltpu.SMEM)
+    hbm = pl.BlockSpec(memory_space=pltpu.HBM)
+    args = [
+        pltpu.with_memory_space_constraint(a, pltpu.HBM) if scalars <= i < scalars + far else a for i, a in enumerate(args)
+    ]
     moved = sum(a.size * a.dtype.itemsize for a in args) + sum(o.size * o.dtype.itemsize for o in outs)
     return pl.pallas_call(
         kernel,
         out_shape=outs,
-        in_specs=[smem] * scalars + [vmem] * (len(args) - scalars),
+        in_specs=[smem] * scalars + [hbm] * far + [vmem] * (len(args) - scalars - far),
         out_specs=[vmem] * len(outs),
+        scratch_shapes=list(scratch),
         compiler_params=pltpu.CompilerParams(vmem_limit_bytes=20 * 1024 * 1024),
         cost_estimate=pl.CostEstimate(flops=flops, bytes_accessed=moved, transcendentals=0),
     )(*args)
@@ -250,19 +285,24 @@
     return lax.all_to_all(block, axis, 0, 0, tiled=True, axis_index_groups=groups)
 
 
-def reduced(mine, other):
+def copies_of(block, count):
+    return jnp.broadcast_to(block[None], (count,) + block.shape)
+
+
+def reduced(mine, other, change):
     docs, n_seg = lax.axis_size("dp"), lax.axis_size("seg")
+    turns = n_seg // SPAN
     got = lax.ppermute(other, "dp", [(i, i ^ 1) for i in range(docs)])
     block = (mine.astype(F32) + got.astype(F32)).astype(BF)
     if docs > 2:
         block = lax.all_to_all(block, "dp", 0, 0, tiled=True, axis_index_groups=runs(docs, docs // 2, 2))
     block = jnp.sum(block.astype(F32), axis=0).astype(BF)
-    for length, stride in ((SPAN, 1), (n_seg // SPAN, SPAN)):
-        copies = jnp.broadcast_to(block[None], (length,) + block.shape)
-        got = spread(copies, "seg", runs(n_seg, length, stride))
-        total = jnp.sum(got.astype(F32), axis=0)
-        block = total.astype(BF)
-    return total
+    got = spread(copies_of(block, SPAN), "seg", runs(n_seg, SPAN, 1))
+    block = jnp.sum(got.astype(F32), axis=0).astype(BF)
+    got = spread(jnp.concatenate([copies_of(block, turns), change], axis=1), "seg", runs(n_seg, turns, SPAN))
+    rows = block.shape[0]
+    changes = jnp.concatenate([got[:, rows : rows + MEM], got[:, rows + MEM :]], axis=2)
+    return jnp.sum(got[:, :rows].astype(F32), axis=0), changes
 
 
 def body(tokens, grad_output, memories, grad_last, norm_gain, query_weight, key_weight, value_weight, out_weight):
@@ -271,25 +311,40 @@
     docs = lax.axis_size("dp")
     turns = n_seg // SPAN
     tok, gout, mem, last, gain = tokens[0], grad_output[0], memories[0, 0], grad_last[0], norm_gain[None]
+    block = position // SPAN
+    place = jnp.stack([position % SPAN, lax.axis_index("dp") % 2, turns - 1 - block]).astype(jnp.int32)
 
     shard = jnp.concatenate([query_weight, key_weight, value_weight, out_weight.T], axis=1)
     w = lax.all_gather(shard, "dp", axis=0, tiled=True)
-    near = runs(n_seg, SPAN, 1)
-    mem4 = lax.all_gather(mem, "seg", axis=0, tiled=True, axis_index_groups=near)
-
-    normed, qg, part, kvp, wt = call(
+    mem4 = lax.all_gather(mem, "seg", axis=0, tiled=True, axis_index_groups=runs(n_seg, SPAN, 1))
+    w, mem4, place = lax.optimization_barrier((w, mem4, place))
+
+    dma = pltpu.SemaphoreType.DMA
+    normed, qg, part, kvp, wt, w = call(
         token_kernel,
         [
             shape((ROWS, D)),
             shape((TOK, D)),
             shape((ROWS, 2 * KV), F32),
-            shape((SPAN * ROWS, 2 * KV)),
+            shape((ROWS, 2 * KV)),
             shape((D + 2 * KV, D)),
+            shape((D, 2 * D + 2 * KV)),
         ],
         (mem, tok, gout, gain, w),
         1_500_000_000,
-    )
-    kvp4 = spread(kvp, "seg", near)
+        far=5,
+        scratch=(
+            pltpu.VMEM((MEM, D), BF),
+            pltpu.VMEM((TOK, D), BF),
+            pltpu.VMEM((TOK, D), BF),
+            pltpu.VMEM((1, D), F32),
+            dma((6,)),
+        ),
+    )
+    kvps = [kvp]
+    for ahead in range(1, SPAN):
+        route = [(i, i // SPAN * SPAN + (i - ahead) % SPAN) for i in range(n_seg)]
+        kvps.append(lax.ppermute(kvp, "seg", route))
     mixed, qkv4, hw4, inv4, arrived = call(
         mix_kernel,
         [
@@ -301,9 +356,11 @@
         ],
         (mem4, last, gain, w, wt),
         4_000_000_000,
+        far=3,
+        scratch=(pltpu.VMEM((SPAN * MEM, D), BF), pltpu.VMEM((MEM, D), BF), pltpu.VMEM((1, D), F32), dma((3,))),
     )
     count = SPAN * GROUPS
-    probs_k, probs_q, krep, vrep, zq = call(
+    probs_k, probs_q, krep, vrep, zq, near = call(
         ready_kernel,
         [
             shape((count, ROWS, PER_GROUP * MEM), F32),
@@ -311,25 +368,24 @@
             shape((count, ROWS, WIDE)),
             shape((count, ROWS, WIDE)),
             shape((count, PER_GROUP * MEM, WIDE)),
+            shape((SPAN * MEM, 2 * KV), F32),
         ],
-        (qkv4, kvp4),
+        (place, qkv4, *kvps),
         400_000_000,
-    )
-    block = position // SPAN
-    u4 = kvp4
+        scalars=1,
+    )
+    u4 = arrived
     for turn in range(turns):
-        fresh = (block == turns - 1 - turn).astype(jnp.int32)[None]
         send, u4, grads4 = call(
-            functools.partial(chain_kernel, turn > 0),
+            functools.partial(chain_kernel, turn),
             [shape((MEM, D)), shape((SPAN * MEM, D)), shape((SPAN * MEM, D + 2 * KV))],
-            (fresh, arrived, u4, mixed, probs_k, probs_q, krep, vrep, zq, qkv4, hw4, inv4, kvp4),
+            (place, arrived, u4, mixed, probs_k, probs_q, krep, vrep, zq, qkv4, hw4, inv4, near),
             1_000_000_000,
             scalars=1,
         )
         if turn < turns - 1:
             route = [(i, i - SPAN) for i in range((turns - 1 - turn) * SPAN, (turns - turn) * SPAN)]
             arrived = lax.ppermute(send, "seg", route)
-    place = jnp.stack([position % SPAN, lax.axis_index("dp") % 2]).astype(jnp.int32)
     half = (docs // 2, D // docs, 2 * KV)
     kv_grad, mine, other = call(
         weight_kernel,
@@ -338,19 +394,19 @@
         400_000_000,
         scalars=1,
     )
-    total = reduced(mine, other) / docs
     own, change = call(
         memory_kernel,
-        [shape((MEM, D), F32), shape((turns, MEM, D))],
+        [shape((MEM, D), F32), shape((turns, 2 * MEM, 2 * KV))],
         (place, grads4, wt, mem4, inv4, gain),
         400_000_000,
         scalars=1,
     )
-    changes = spread(change, "seg", runs(n_seg, turns, SPAN))
+    (grad_tokens,) = call(rows_kernel, [shape((TOK, D))], (tok, gout, gain, wt, qg, kv_grad), 500_000_000)
+    total, changes = reduced(mine, other, change)
+    total = total / docs
     later = (jnp.arange(turns) > block)[:, None, None]
     after = jnp.sum(jnp.where(later, changes.astype(F32), 0.0), axis=0)
     grad_memories = (last.astype(F32) + after + own).astype(BF)
-    (grad_tokens,) = call(rows_kernel, [shape((TOK, D))], (tok, gout, gain, wt, qg, kv_grad), 500_000_000)
     return (grad_tokens[None], grad_memories[None, None], total[:, :KV], total[:, KV:])
 
 

time: 288 us -> 223 us (0.77)
  local copies, waits for them, and re-layouts: 51.5 us -> 9.1 us
  waiting for transfers between devices: 122 us -> 87 us
  blocking collectives: 17.2 us -> 41.9 us
  starting transfers between devices: 35 us -> 23.5 us
    unnamed x118 -> x26, local copies, waits for them, and re-layouts: 49.5 us -> 6.82 us
    all_to_all x0 -> x1, blocking collectives: none -> 24.2 us  [reduced(): lax.all_to_all(block, 'dp', 0, 0, tiled=True, axis_index_groups=runs(docs...]
    all_gather x1, waiting for transfers between devices: 74.5 us -> 56.7 us  [body(): w = lax.all_gather(shard, 'dp', axis=0, tiled=True)]
    all_to_all x4 -> x2, starting transfers between devices: 23 us -> 8.18 us  [spread(): lax.all_to_all(block, axis, 0, 0, tiled=True, axis_index_groups=groups)]
    all_to_all x1 -> x0, waiting for transfers between devices: 11.2 us -> none  [reduced(): lax.all_to_all(block, 'dp', 0, 0, tiled=True, axis_index_groups=runs(docs...]
    ppermute x0 -> x3, starting transfers between devices: none -> 10.4 us  [body(): kvps.append(lax.ppermute(kvp, 'seg', route))]
    all_to_all x4 -> x2, waiting for transfers between devices: 15.8 us -> 8.49 us  [spread(): lax.all_to_all(block, axis, 0, 0, tiled=True, axis_index_groups=groups)]
    all_to_all x1 -> x0, starting transfers between devices: 6.22 us -> none  [reduced(): lax.all_to_all(block, 'dp', 0, 0, tiled=True, axis_index_groups=runs(docs...]
  transfers between devices with their start and end apart: 10 -> 10, of which waited for: 6 -> 5; matrix products, arithmetic and copies ran while one was open for 1% -> 0% of each run, Pallas kernels for 3% -> 4%
where the time goes in v3:
time: 223 us; the launch traced here: 222 us
  waiting for transfers between devices  87 us (39%)
  blocking collectives  41.9 us (19%)
  Pallas kernels  37.5 us (17%)
  starting transfers between devices  23.5 us (11%)
  between operations  14.3 us (6%)
  local copies, waits for them, and re-layouts  9.1 us (4%)
  other arithmetic  8.22 us (4%)
    all_gather x1, waiting for transfers between devices, body(): w = lax.all_gather(shard, 'dp', axis=0, tiled=True)  56.7 us
    pallas_call x10, Pallas kernels, call(): pl.pallas_call(kernel, out_shape=outs, in_specs=[smem] * scalars + [hbm]...  37.5 us
    all_to_all x1, blocking collectives, reduced(): lax.all_to_all(block, 'dp', 0, 0, tiled=True, axis_index_groups=runs(docs...  24.2 us
    ppermute x3, waiting for transfers between devices, body(): arrived = lax.ppermute(send, 'seg', route)  18.6 us
    all_gather x1, blocking collectives, body(): lax.all_gather(mem, 'seg', axis=0, tiled=True, axis_index_groups=runs(n_s...  17.7 us
    ppermute x3, starting transfers between devices, body(): kvps.append(lax.ppermute(kvp, 'seg', route))  10.4 us
    all_to_all x2, waiting for transfers between devices, spread(): lax.all_to_all(block, axis, 0, 0, tiled=True, axis_index_groups=groups)  8.49 us
    all_to_all x2, starting transfers between devices, spread(): lax.all_to_all(block, axis, 0, 0, tiled=True, axis_index_groups=groups)  8.18 us
  transfers between devices with their start and end apart: 10, of which 5 were waited for; matrix products, arithmetic and copies ran while one was open for 0% of the time, Pallas kernels for 4%

profile of v3, /device:TPU:8, one launch (start us, length us, event | category | flops | bytes accessed | tf_op | source)
XLA Modules:
  0.0 221.6 jit_solution(6176007183140763128)
XLA Ops:
  7.2 0.0 all-gather.3.cloned.1.call-start
  7.2 1.6 pad_maximum_fusion.1
  8.8 0.0 all-gather.3.cloned.1.call-update
  8.9 17.7 %all-gather = bf16[1,1,128,1024]{3,2,1,0:T(8,128)(2,1)} all-gather(bf16[1,1,32,1024]{3,2,1,0:T(8,128)(2,1)} %param.11), channel_id=2, replica_groups={{0,32,64,96},{128,160,192,224},{256,288,320,352},{384,416,448,480},{1,3..., dimensions={2}, use_global_device_ids=true | all-gather | bytes 327680 | tf_op jit(solution)/shard_map/all_gather | solution.py:319
  26.5 0.1 pad_add_fusion.place
  26.6 56.7 %all-gather.3.cloned.1.call-done.w_hbm = bf16[1024,2560]{1,0:T(8,128)(2,1)} async-done(((bf16[32,2560]{1,0:T(8,128)(2,1)}), bf16[1024,2560]{1,0:T(8,128)(2,1)}) %all-gather.3.cloned.1.call-update) | async-done | bytes 5242896 | tf_op jit(solution)/shard_map/all_gather | solution.py:318
  83.3 5.3 %shard_map.120 = (bf16[160,1024]{1,0:T(8,128)(2,1)S(1)}, bf16[128,1024]{1,0:T(8,128)(2,1)S(1)}, f32[160,512]{1,0:T(8,128)S(1)}, bf16[160,512]{1,0:T(8,128)(2,1)S...) custom-call(bf16[32,1024]{1,0:T(8,128)(2,1)} %bitcast.24, bf16[128,1024]{1,0:T(8,128)(2,1)} %bitcast.14, ...), custom_call_target="tpu_custom_call" | custom-call | flops 1500000000 | bytes 15306752 | tf_op jit(solution)/shard_map/pallas_call | solution.py:262
  88.6 0.7 copy-done.5
  89.3 5.9 %collective-permute-start.2 = (bf16[160,512]{1,0:T(8,128)(2,1)S(1)}, bf16[160,512]{1,0:T(8,128)(2,1)S(1)}, u32[]{:S(2)}, u32[]{:S(2)}) collective-permute-start(bf16[160,512]{1,0:T(8,128)(2,1)S(1)} %get-tuple-element.46.refs_0_), channel_id=1, source_target_pairs={{0,32},{32,64},{64,96},{96,0},{128,160},{160,192},{192,224},{224,1... | collective-permute-start | bytes 491528 | tf_op jit(solution)/shard_map/ppermute | solution.py:347
  95.2 2.3 %collective-permute-start.1 = (bf16[160,512]{1,0:T(8,128)(2,1)S(1)}, bf16[160,512]{1,0:T(8,128)(2,1)S(1)}, u32[]{:S(2)}, u32[]{:S(2)}) collective-permute-start(bf16[160,512]{1,0:T(8,128)(2,1)S(1)} %get-tuple-element.46.refs_0_), channel_id=1, source_target_pairs={{0,64},{32,96},{64,0},{96,32},{128,192},{160,224},{192,128},{224,1... | collective-permute-start | bytes 491528 | tf_op jit(solution)/shard_map/ppermute | solution.py:347
  97.5 2.3 %collective-permute-start = (bf16[160,512]{1,0:T(8,128)(2,1)S(1)}, bf16[160,512]{1,0:T(8,128)(2,1)S(1)}, u32[]{:S(2)}, u32[]{:S(2)}) collective-permute-start(bf16[160,512]{1,0:T(8,128)(2,1)S(1)} %get-tuple-element.46.refs_0_), channel_id=1, source_target_pairs={{0,96},{32,0},{64,32},{96,64},{128,224},{160,128},{192,160},{224,1... | collective-permute-start | bytes 491528 | tf_op jit(solution)/shard_map/ppermute | solution.py:347
  99.8 5.5 %shard_map.121 = (bf16[1536,1024]{1,0:T(8,128)(2,1)S(1)}, f32[128,1536]{1,0:T(8,128)S(1)}, f32[128,1024]{1,0:T(8,128)S(1)}, f32[128,1]{1,0:T(8,128)S(1)}, bf16[32,1024]{1,0:T(8,128)(2,1)S(1)}) custom-call(bf16[128,1024]{1,0:T(8,128)(2,1)} %bitcast.18, bf16[32,1024]{1,0:T(8,128)(2,1)} %bitcast.27, f32[1,1024]{1,0:T(1,128)} %bitcast.21, ...), custom_call_target="tpu_custom_call" | custom-call | flops 4000000000 | bytes 13242880 | tf_op jit(solution)/shard_map/pallas_call | solution.py:262
  105.3 1.4 collective-permute-done.1.refs_2_
  106.7 2.3 %shard_map.122 = (f32[16,160,128]{2,1,0:T(8,128)S(1)}, f32[16,128,160]{2,1,0:T(8,128)S(1)}, bf16[16,160,256]{2,1,0:T(8,128)(2,1)S(1)}, bf16[16,160,256]{2,1,0:T(...) custom-call(s32[3]{0:T(128)S(1)} %pad_add_fusion.place, ...), custom_call_target="tpu_custom_call" | custom-call | flops 400000000 | bytes 7995404 | tf_op jit(solution)/shard_map/pallas_call | solution.py:262
  109.0 5.0 %shard_map.123 = (bf16[32,1024]{1,0:T(8,128)(2,1)S(1)}, bf16[128,1024]{1,0:T(8,128)(2,1)S(1)}, bf16[128,1536]{1,0:T(8,128)(2,1)}) custom-call(s32[3]{0:T(128)S(1)} %pad_add_fusion.place, bf16[32,1024]{1,0:T(8,128)(2,1)S(1)} %get-tuple-element.43.arrived.before, bf16[32,1024]{1,0:T(8,128)(2,1)S(1)} %get-tuple-element.43.arrived.before, ...), custom_call_target="tpu_custom_call" | custom-call | flops 1000000000 | bytes 11862540 | tf_op jit(solution)/shard_map/pallas_call | solution.py:262
  114.0 0.7 collective-permute-start.3
  114.7 5.1 %shard_map.124 = (bf16[32,1024]{1,0:T(8,128)(2,1)S(1)}, bf16[128,1024]{1,0:T(8,128)(2,1)S(1)}, bf16[128,1536]{1,0:T(8,128)(2,1)}) custom-call(s32[3]{0:T(128)S(1)} %pad_add_fusion.place, bf16[32,1024]{1,0:T(8,128)(2,1)S(1)} %collective-permute-done.3.arrived, bf16[128,1024]{1,0:T(8,128)(2,1)S(1)} %get-tuple-element.56.before, ...), custom_call_target="tpu_custom_call" | custom-call | flops 1000000000 | bytes 12059148 | tf_op jit(solution)/shard_map/pallas_call | solution.py:262
  119.7 0.9 collective-permute-start.4
  120.6 5.1 %shard_map.125 = (bf16[32,1024]{1,0:T(8,128)(2,1)S(1)}, bf16[128,1024]{1,0:T(8,128)(2,1)S(1)}, bf16[128,1536]{1,0:T(8,128)(2,1)}) custom-call(s32[3]{0:T(128)S(1)} %pad_add_fusion.place, bf16[32,1024]{1,0:T(8,128)(2,1)S(1)} %collective-permute-done.4.arrived, bf16[128,1024]{1,0:T(8,128)(2,1)S(1)} %get-tuple-element.58.before, ...), custom_call_target="tpu_custom_call" | custom-call | flops 1000000000 | bytes 12059148 | tf_op jit(solution)/shard_map/pallas_call | solution.py:262
  125.7 1.3 collective-permute-start.5
  127.0 18.6 %collective-permute-done.5.arrived = bf16[32,1024]{1,0:T(8,128)(2,1)S(1)} collective-permute-done((bf16[32,1024]{1,0:T(8,128)(2,1)S(1)}, bf16[32,1024]{1,0:T(8,128)(2,1)S(1)}, u32[]{:S(2)}, u32[]{:S(2)}) %collective-permute-start.5) | collective-permute-done | bytes 65568 | tf_op jit(solution)/shard_map/ppermute | solution.py:388
  145.5 5.1 %shard_map.126 = (bf16[32,1024]{1,0:T(8,128)(2,1)}, bf16[128,1024]{1,0:T(8,128)(2,1)S(1)}, bf16[128,1536]{1,0:T(8,128)(2,1)S(1)}) custom-call(s32[3]{0:T(128)S(1)} %pad_add_fusion.place, bf16[32,1024]{1,0:T(8,128)(2,1)S(1)} %collective-permute-done.5.arrived, bf16[128,1024]{1,0:T(8,128)(2,1)S(1)} %get-tuple-element.60.before, ...), custom_call_target="tpu_custom_call" | custom-call | flops 1000000000 | bytes 12059148 | tf_op jit(solution)/shard_map/pallas_call | solution.py:262
  150.6 1.4 shard_map.127
  152.0 2.1 collective-permute-start.6
  154.1 1.9 collective-permute-done.6
  156.0 0.2 add_convert_fusion
  156.2 24.2 %all_to_all.15 = bf16[16,32,512]{2,1,0:T(8,128)(2,1)} all-to-all(bf16[16,32,512]{2,1,0:T(8,128)(2,1)S(1)} %add_convert_fusion), channel_id=1, replica_groups={{0,2,4,6,8,10,12,14,16,18,20,22,24,26,28,30},{1,3,5,7,9,11,13,15,17,19,..., dimensions={0} | all-to-all | bytes 1048576 | tf_op jit(solution)/shard_map/all_to_all | solution.py:298
  180.4 1.1 reduce_sum.42
  181.6 0.7 broadcast_in_dim.37
  182.2 3.9 %all-to-all-start.1 = ((bf16[4,32,512]{2,1,0:T(8,128)(2,1)}), bf16[4,32,512]{2,1,0:T(8,128)(2,1)}, u32[]{:S(2)}, u32[]{:S(2)}) async-start(bf16[4,32,512]{2,1,0:T(8,128)(2,1)} %broadcast_in_dim.37), calls=%async_computation.1 | async-start | bytes 262144 | tf_op jit(solution)/shard_map/all_to_all | solution.py:285
  186.2 0.9 copy-done.2
  187.1 1.0 copy-done.4
  188.1 1.4 shard_map.129
  189.5 0.7 copy-done.7
  190.2 0.7 copy-done.10
  190.8 0.9 reduce_sum.43
  191.8 1.7 pad_maximum_fusion
  193.5 4.3 %all-to-all-start.2 = ((bf16[4,96,512]{2,1,0:T(8,128)(2,1)}), bf16[4,96,512]{2,1,0:T(8,128)(2,1)}, u32[]{:S(2)}, u32[]{:S(2)}) async-start(bf16[4,96,512]{2,1,0:T(8,128)(2,1)} %pad_maximum_fusion), calls=%async_computation.2 | async-start | bytes 786432 | tf_op jit(solution)/shard_map/all_to_all | solution.py:285
  197.8 0.9 copy-done.1
  198.7 0.9 copy-done.6
  199.7 0.9 copy-done.9
  200.6 1.4 shard_map.128
  202.1 8.5 %all-to-all-done.2 = bf16[4,96,512]{2,1,0:T(8,128)(2,1)} async-done(((bf16[4,96,512]{2,1,0:T(8,128)(2,1)}), bf16[4,96,512]{2,1,0:T(8,128)(2,1)}, u32[]{:S(2)}, u32[]{:S(2)}) %all-to-all-start.2) | async-done | bytes 393248 | tf_op jit(solution)/shard_map/all_to_all | solution.py:285
  210.5 0.9 convert_reduce_fusion
  211.5 0.6 fusion.2
  212.1 1.0 fusion.1
  213.1 0.1 select_reduce_fusion
  213.2 1.6 fusion
  (26 shorter events, 0.1 us)
Async XLA Ops:
  7.2 76.1 %all-gather.3.cloned.1.call-start = ((), (), s32[]{:S(2)}) async-start(), calls=%async_computation.3 | async-start | bytes 5406720 | tf_op jit(solution)/shard_map/all_gather | solution.py:318
  88.6 0.7 copy-start.5
  89.3 16.0 %collective-permute-start.2 = (bf16[160,512]{1,0:T(8,128)(2,1)S(1)}, bf16[160,512]{1,0:T(8,128)(2,1)S(1)}, u32[]{:S(2)}, u32[]{:S(2)}) collective-permute-start(bf16[160,512]{1,0:T(8,128)(2,1)S(1)} %get-tuple-element.46.refs_0_), channel_id=1, source_target_pairs={{0,32},{32,64},{64,96},{96,0},{128,160},{160,192},{192,224},{224,1... | collective-permute-start | bytes 491528 | tf_op jit(solution)/shard_map/ppermute | solution.py:347
  95.2 11.5 %collective-permute-start.1 = (bf16[160,512]{1,0:T(8,128)(2,1)S(1)}, bf16[160,512]{1,0:T(8,128)(2,1)S(1)}, u32[]{:S(2)}, u32[]{:S(2)}) collective-permute-start(bf16[160,512]{1,0:T(8,128)(2,1)S(1)} %get-tuple-element.46.refs_0_), channel_id=1, source_target_pairs={{0,64},{32,96},{64,0},{96,32},{128,192},{160,224},{192,128},{224,1... | collective-permute-start | bytes 491528 | tf_op jit(solution)/shard_map/ppermute | solution.py:347
  97.5 9.2 %collective-permute-start = (bf16[160,512]{1,0:T(8,128)(2,1)S(1)}, bf16[160,512]{1,0:T(8,128)(2,1)S(1)}, u32[]{:S(2)}, u32[]{:S(2)}) collective-permute-start(bf16[160,512]{1,0:T(8,128)(2,1)S(1)} %get-tuple-element.46.refs_0_), channel_id=1, source_target_pairs={{0,96},{32,0},{64,32},{96,64},{128,224},{160,128},{192,160},{224,1... | collective-permute-start | bytes 491528 | tf_op jit(solution)/shard_map/ppermute | solution.py:347
  114.0 0.7 collective-permute-start.3
  119.7 0.9 collective-permute-start.4
  125.7 19.8 %collective-permute-start.5 = (bf16[32,1024]{1,0:T(8,128)(2,1)S(1)}, bf16[32,1024]{1,0:T(8,128)(2,1)S(1)}, u32[]{:S(2)}, u32[]{:S(2)}) collective-permute-start(bf16[32,1024]{1,0:T(8,128)(2,1)S(1)} %get-tuple-element.59), channel_id=1, source_target_pairs={{128,0},{160,32},{192,64},{224,96},{129,1},{161,33},{193,65},{225,... | collective-permute-start | bytes 196616 | tf_op jit(solution)/shard_map/ppermute | solution.py:388
  150.6 5.6 %copy-start.3 = (bf16[128,1536]{1,0:T(8,128)(2,1)}, bf16[128,1536]{1,0:T(8,128)(2,1)S(1)}, u32[]{:S(2)}) copy-start(bf16[128,1536]{1,0:T(8,128)(2,1)S(1)} %get-tuple-element.67.grads4) | copy-start | bytes 1179652
  152.0 4.1 %copy-start.8 = (bf16[160,512]{1,0:T(8,128)(2,1)}, bf16[160,512]{1,0:T(8,128)(2,1)S(1)}, u32[]{:S(2)}) copy-start(bf16[160,512]{1,0:T(8,128)(2,1)S(1)} %get-tuple-element.64.kv_grad) | copy-start | bytes 491524
  152.0 34.1 %copy-start.11 = (f32[1024]{0:T(1024)S(1)}, f32[1024]{0:T(1024)}, u32[]{:S(2)}) copy-start(f32[1024]{0:T(1024)} %param.13) | copy-start | bytes 12292
  152.0 3.9 %collective-permute-start.6 = (bf16[16,32,512]{2,1,0:T(8,128)(2,1)S(1)}, bf16[16,32,512]{2,1,0:T(8,128)(2,1)S(1)}, u32[]{:S(2)}, u32[]{:S(2)}) collective-permute-start(bf16[16,32,512]{2,1,0:T(8,128)(2,1)S(1)} %get-tuple-element.66), channel_id=1, source_target_pairs={{0,1},{1,0},{2,3},{3,2},{4,5},{5,4},{6,7},{7,6},{8,9},{9,8},{10,11... | collective-permute-start | bytes 1572872 | tf_op jit(solution)/shard_map/ppermute | solution.py:295
  181.5 16.2 %copy-start = (bf16[1,128,1024]{2,1,0:T(8,128)(2,1)S(1)}, bf16[1,128,1024]{2,1,0:T(8,128)(2,1)}, u32[]{:S(2)}) copy-start(bf16[1,128,1024]{2,1,0:T(8,128)(2,1)} %param.9) | copy-start | bytes 786436
  182.2 8.6 %all-to-all-start.1 = ((bf16[4,32,512]{2,1,0:T(8,128)(2,1)}), bf16[4,32,512]{2,1,0:T(8,128)(2,1)}, u32[]{:S(2)}, u32[]{:S(2)}) async-start(bf16[4,32,512]{2,1,0:T(8,128)(2,1)} %broadcast_in_dim.37), calls=%async_computation.1 | async-start | bytes 262144 | tf_op jit(solution)/shard_map/all_to_all | solution.py:285
  186.2 1.0 copy-start.2
  187.1 1.0 copy-start.4
  189.5 0.7 copy-start.7
  190.2 0.7 copy-start.10
  193.5 19.7 %copy-start.12 = (bf16[1,32,1024]{2,1,0:T(8,128)(2,1)S(1)}, bf16[1,32,1024]{2,1,0:T(8,128)(2,1)}, u32[]{:S(2)}) copy-start(bf16[1,32,1024]{2,1,0:T(8,128)(2,1)} %param.12) | copy-start | bytes 196612
  193.5 17.0 %all-to-all-start.2 = ((bf16[4,96,512]{2,1,0:T(8,128)(2,1)}), bf16[4,96,512]{2,1,0:T(8,128)(2,1)}, u32[]{:S(2)}, u32[]{:S(2)}) async-start(bf16[4,96,512]{2,1,0:T(8,128)(2,1)} %pad_maximum_fusion), calls=%async_computation.2 | async-start | bytes 786432 | tf_op jit(solution)/shard_map/all_to_all | solution.py:285
  197.8 1.0 copy-start.1
  198.7 0.9 copy-start.6
  199.7 0.9 copy-start.9
Sparse Core Ops, SparseCore 0:
  11.7 71.5 all-gather.2

commit v4 on v3

--- a/solution.py
+++ b/solution.py
@@ -223,25 +223,30 @@
     kv_grad = jnp.concatenate([folded(key_parts), folded(value_parts)], axis=1) + part[...]
     kv_grad = kv_grad.astype(BF)
     kv_out[...] = kv_grad
-    share = mine_out.shape[1]
-    grad = tn(normed[...], kv_grad).reshape(mine_out.shape[0], 2, share, 2 * KV)
+    grad = tn(normed[...], kv_grad)
+    grad = grad.reshape(mine_out.shape[0], 2, mine_out.shape[1], 2 * KV)
     first = place[1] == 0
     mine_out[...] = jnp.where(first, grad[:, 0], grad[:, 1]).astype(BF)
     other_out[...] = jnp.where(first, grad[:, 1], grad[:, 0]).astype(BF)
 
 
-def memory_kernel(place, grads4, wt, mem4, inv4, gain, own_out, all_out):
+def memory_kernel(turn, place, arrived, held, grads4, wt, mem4, inv4, gain, *outs):
+    current = arrived[...].astype(F32)
+    if turn > 0:
+        current = jnp.where(place[2] == turn, current, held[...].astype(F32))
     hidden, inverse = mem4[...].astype(F32), inv4[...]
     change = norm_backward(0.0, nn(grads4[...], wt[...]), hidden, inverse, gain[...])
-    total = jnp.zeros((MEM, D), F32)
-    own = jnp.zeros((MEM, D), F32)
+    if len(outs) > 1:
+        outs[1][...] = current.astype(BF)
+        for s in range(SPAN):
+            current = current + change[s * MEM : (s + 1) * MEM]
+        outs[0][...] = current.astype(BF)
+        return
+    own = current
     for s in reversed(range(SPAN)):
-        total = total + change[s * MEM : (s + 1) * MEM]
-        own = jnp.where(place[0] == s, total, own)
-    own_out[...] = own
-    for copy in range(all_out.shape[0]):
-        all_out[copy, :MEM, :] = total[:, : 2 * KV].astype(BF)
-        all_out[copy, MEM:, :] = total[:, 2 * KV :].astype(BF)
+        current = current + change[s * MEM : (s + 1) * MEM]
+        own = jnp.where(place[0] == s, current, own)
+    outs[0][...] = own.astype(BF)
 
 
 def rows_kernel(tok, gout, gain, wt, qg, kv_grad, out):
@@ -281,28 +286,19 @@
     ]
 
 
-def spread(block, axis, groups):
-    return lax.all_to_all(block, axis, 0, 0, tiled=True, axis_index_groups=groups)
-
-
-def copies_of(block, count):
-    return jnp.broadcast_to(block[None], (count,) + block.shape)
-
-
-def reduced(mine, other, change):
-    docs, n_seg = lax.axis_size("dp"), lax.axis_size("seg")
-    turns = n_seg // SPAN
+def summed_over_documents(mine, other):
+    docs = lax.axis_size("dp")
     got = lax.ppermute(other, "dp", [(i, i ^ 1) for i in range(docs)])
     block = (mine.astype(F32) + got.astype(F32)).astype(BF)
     if docs > 2:
         block = lax.all_to_all(block, "dp", 0, 0, tiled=True, axis_index_groups=runs(docs, docs // 2, 2))
-    block = jnp.sum(block.astype(F32), axis=0).astype(BF)
-    got = spread(copies_of(block, SPAN), "seg", runs(n_seg, SPAN, 1))
-    block = jnp.sum(got.astype(F32), axis=0).astype(BF)
-    got = spread(jnp.concatenate([copies_of(block, turns), change], axis=1), "seg", runs(n_seg, turns, SPAN))
-    rows = block.shape[0]
-    changes = jnp.concatenate([got[:, rows : rows + MEM], got[:, rows + MEM :]], axis=2)
-    return jnp.sum(got[:, :rows].astype(F32), axis=0), changes
+    return jnp.sum(block.astype(F32), axis=0).astype(BF)
+
+
+def summed_over_segments(block):
+    n_seg = lax.axis_size("seg")
+    copies = jnp.broadcast_to(block[None], (n_seg,) + block.shape)
+    return jnp.sum(lax.all_to_all(copies, "seg", 0, 0, tiled=True).astype(F32), axis=0)
 
 
 def body(tokens, grad_output, memories, grad_last, norm_gain, query_weight, key_weight, value_weight, out_weight):
@@ -375,6 +371,7 @@
         scalars=1,
     )
     u4 = arrived
+    memory_arrived = memory_held = last
     for turn in range(turns):
         send, u4, grads4 = call(
             functools.partial(chain_kernel, turn),
@@ -386,6 +383,15 @@
         if turn < turns - 1:
             route = [(i, i - SPAN) for i in range((turns - 1 - turn) * SPAN, (turns - turn) * SPAN)]
             arrived = lax.ppermute(send, "seg", route)
+            memory_send, memory_held = call(
+                functools.partial(memory_kernel, turn),
+                [shape((MEM, D)), shape((MEM, D))],
+                (place, memory_arrived, memory_held, grads4, wt, mem4, inv4, gain),
+                400_000_000,
+                scalars=1,
+            )
+            arrived, memory_send = lax.optimization_barrier((arrived, memory_send))
+            memory_arrived = lax.ppermute(memory_send, "seg", route)
     half = (docs // 2, D // docs, 2 * KV)
     kv_grad, mine, other = call(
         weight_kernel,
@@ -394,19 +400,17 @@
         400_000_000,
         scalars=1,
     )
-    own, change = call(
-        memory_kernel,
-        [shape((MEM, D), F32), shape((turns, 2 * MEM, 2 * KV))],
-        (place, grads4, wt, mem4, inv4, gain),
+    (grad_memories,) = call(
+        functools.partial(memory_kernel, turns - 1),
+        [shape((MEM, D))],
+        (place, memory_arrived, memory_held, grads4, wt, mem4, inv4, gain),
         400_000_000,
         scalars=1,
     )
     (grad_tokens,) = call(rows_kernel, [shape((TOK, D))], (tok, gout, gain, wt, qg, kv_grad), 500_000_000)
-    total, changes = reduced(mine, other, change)
-    total = total / docs
-    later = (jnp.arange(turns) > block)[:, None, None]
-    after = jnp.sum(jnp.where(later, changes.astype(F32), 0.0), axis=0)
-    grad_memories = (last.astype(F32) + after + own).astype(BF)
+    block = summed_over_documents(mine, other)
+    block, grad_tokens, grad_memories = lax.optimization_barrier((block, grad_tokens, grad_memories))
+    total = summed_over_segments(block) / docs
     return (grad_tokens[None], grad_memories[None, None], total[:, :KV], total[:, KV:])
 
 

time: 223 us -> 215 us (0.964)
  other arithmetic: 8.22 us -> 3.84 us
  Pallas kernels: 37.5 us -> 41 us
  local copies, waits for them, and re-layouts: 9.1 us -> 6.41 us
    pallas_call x10 -> x13, Pallas kernels: 37.5 us -> 41 us  [call(): pl.pallas_call(kernel, out_shape=outs, in_specs=[smem] * scalars + [hbm]...]
    ppermute x3, waiting for transfers between devices: 18.6 us -> 15.3 us  [body(): arrived = lax.ppermute(send, 'seg', route)]
    ppermute x1 -> x4, starting transfers between devices: 2.05 us -> 4.75 us  [the longest x3 2.84 us: body(): memory_arrived = lax.ppermute(memory_send, 'seg', route)]
    all_to_all x2 -> x1, starting transfers between devices: 8.18 us -> 6.2 us  [summed_over_documents(): lax.all_to_all(block, 'dp', 0, 0, tiled=True, axis_index_groups=runs(docs...]
    unnamed x26 -> x24, local copies, waits for them, and re-layouts: 6.82 us -> 5.74 us
    all_to_all x2 -> x1, waiting for transfers between devices: 8.49 us -> 8.69 us  [summed_over_documents(): lax.all_to_all(block, 'dp', 0, 0, tiled=True, axis_index_groups=runs(docs...]
  transfers between devices with their start and end apart: 10 -> 12, of which waited for: 5 -> 6; matrix products, arithmetic and copies ran while one was open for 0% -> 0% of each run, Pallas kernels for 4% -> 10%
where the time goes in v4:
time: 215 us; the launch traced here: 214 us
  waiting for transfers between devices  84.9 us (39%)
  Pallas kernels  41 us (19%)
  blocking collectives  39.8 us (19%)
  starting transfers between devices  24 us (11%)
  between operations  14.4 us (7%)
  local copies, waits for them, and re-layouts  6.41 us (3%)
  other arithmetic  3.84 us (2%)
    all_gather x1, waiting for transfers between devices, body(): w = lax.all_gather(shard, 'dp', axis=0, tiled=True)  56.7 us
    pallas_call x13, Pallas kernels, call(): pl.pallas_call(kernel, out_shape=outs, in_specs=[smem] * scalars + [hbm]...  41 us
    all_to_all x1, blocking collectives, summed_over_segments(): lax.all_to_all(copies, 'seg', 0, 0, tiled=True).astype(F32)  22.1 us
    all_gather x1, blocking collectives, body(): lax.all_gather(mem, 'seg', axis=0, tiled=True, axis_index_groups=runs(n_s...  17.7 us
    ppermute x3, waiting for transfers between devices, body(): arrived = lax.ppermute(send, 'seg', route)  15.3 us
    ppermute x3, starting transfers between devices, body(): kvps.append(lax.ppermute(kvp, 'seg', route))  10.4 us
    all_to_all x1, waiting for transfers between devices, summed_over_documents(): lax.all_to_all(block, 'dp', 0, 0, tiled=True, axis_index_groups=runs(docs...  8.69 us
    all_to_all x1, starting transfers between devices, summed_over_documents(): lax.all_to_all(block, 'dp', 0, 0, tiled=True, axis_index_groups=runs(docs...  6.2 us
  transfers between devices with their start and end apart: 12, of which 6 were waited for; matrix products, arithmetic and copies ran while one was open for 0% of the time, Pallas kernels for 10%

profile of v4, /device:TPU:8, one launch (start us, length us, event | category | flops | bytes accessed | tf_op | source)
XLA Modules:
  0.0 214.5 jit_solution(13779429164912427771)
XLA Ops:
  7.2 0.0 all-gather.3.cloned.1.call-start
  7.2 1.6 pad_maximum_fusion
  8.8 0.0 all-gather.3.cloned.1.call-update
  8.9 17.7 %all-gather = bf16[1,1,128,1024]{3,2,1,0:T(8,128)(2,1)} all-gather(bf16[1,1,32,1024]{3,2,1,0:T(8,128)(2,1)} %param.11), channel_id=2, replica_groups={{0,32,64,96},{128,160,192,224},{256,288,320,352},{384,416,448,480},{1,3..., dimensions={2}, use_global_device_ids=true | all-gather | bytes 327680 | tf_op jit(solution)/shard_map/all_gather | solution.py:315
  26.5 0.1 pad_add_fusion.place
  26.6 56.7 %all-gather.3.cloned.1.call-done.w_hbm = bf16[1024,2560]{1,0:T(8,128)(2,1)} async-done(((bf16[32,2560]{1,0:T(8,128)(2,1)}), bf16[1024,2560]{1,0:T(8,128)(2,1)}) %all-gather.3.cloned.1.call-update) | async-done | bytes 5242896 | tf_op jit(solution)/shard_map/all_gather | solution.py:314
  83.3 5.4 %shard_map.120 = (bf16[160,1024]{1,0:T(8,128)(2,1)S(1)}, bf16[128,1024]{1,0:T(8,128)(2,1)S(1)}, f32[160,512]{1,0:T(8,128)S(1)}, bf16[160,512]{1,0:T(8,128)(2,1)S...) custom-call(bf16[32,1024]{1,0:T(8,128)(2,1)} %bitcast.31, bf16[128,1024]{1,0:T(8,128)(2,1)} %bitcast.17, ...), custom_call_target="tpu_custom_call" | custom-call | flops 1500000000 | bytes 15306752 | tf_op jit(solution)/shard_map/pallas_call | solution.py:267
  88.7 0.7 copy-done.6
  89.4 5.9 %collective-permute-start.2 = (bf16[160,512]{1,0:T(8,128)(2,1)S(1)}, bf16[160,512]{1,0:T(8,128)(2,1)S(1)}, u32[]{:S(2)}, u32[]{:S(2)}) collective-permute-start(bf16[160,512]{1,0:T(8,128)(2,1)S(1)} %get-tuple-element.61.refs_0_), channel_id=1, source_target_pairs={{0,32},{32,64},{64,96},{96,0},{128,160},{160,192},{192,224},{224,1... | collective-permute-start | bytes 491528 | tf_op jit(solution)/shard_map/ppermute | solution.py:343
  95.3 2.3 %collective-permute-start.1 = (bf16[160,512]{1,0:T(8,128)(2,1)S(1)}, bf16[160,512]{1,0:T(8,128)(2,1)S(1)}, u32[]{:S(2)}, u32[]{:S(2)}) collective-permute-start(bf16[160,512]{1,0:T(8,128)(2,1)S(1)} %get-tuple-element.61.refs_0_), channel_id=1, source_target_pairs={{0,64},{32,96},{64,0},{96,32},{128,192},{160,224},{192,128},{224,1... | collective-permute-start | bytes 491528 | tf_op jit(solution)/shard_map/ppermute | solution.py:343
  97.6 2.3 %collective-permute-start = (bf16[160,512]{1,0:T(8,128)(2,1)S(1)}, bf16[160,512]{1,0:T(8,128)(2,1)S(1)}, u32[]{:S(2)}, u32[]{:S(2)}) collective-permute-start(bf16[160,512]{1,0:T(8,128)(2,1)S(1)} %get-tuple-element.61.refs_0_), channel_id=1, source_target_pairs={{0,96},{32,0},{64,32},{96,64},{128,224},{160,128},{192,160},{224,1... | collective-permute-start | bytes 491528 | tf_op jit(solution)/shard_map/ppermute | solution.py:343
  99.9 5.6 %shard_map.121 = (bf16[1536,1024]{1,0:T(8,128)(2,1)S(1)}, f32[128,1536]{1,0:T(8,128)S(1)}, f32[128,1024]{1,0:T(8,128)S(1)}, f32[128,1]{1,0:T(8,128)S(1)}, bf16[32,1024]{1,0:T(8,128)(2,1)S(1)}) custom-call(bf16[128,1024]{1,0:T(8,128)(2,1)} %bitcast.12, bf16[32,1024]{1,0:T(8,128)(2,1)} %bitcast.21, f32[1,1024]{1,0:T(1,128)} %bitcast.25, ...), custom_call_target="tpu_custom_call" | custom-call | flops 4000000000 | bytes 13242880 | tf_op jit(solution)/shard_map/pallas_call | solution.py:267
  105.5 1.3 collective-permute-done.1.refs_2_
  106.8 2.3 %shard_map.122 = (f32[16,160,128]{2,1,0:T(8,128)S(1)}, f32[16,128,160]{2,1,0:T(8,128)S(1)}, bf16[16,160,256]{2,1,0:T(8,128)(2,1)S(1)}, bf16[16,160,256]{2,1,0:T(...) custom-call(s32[3]{0:T(128)S(1)} %pad_add_fusion.place, ...), custom_call_target="tpu_custom_call" | custom-call | flops 400000000 | bytes 7995404 | tf_op jit(solution)/shard_map/pallas_call | solution.py:267
  109.1 0.0 copy-start.5
  109.1 4.5 %shard_map.123 = (bf16[32,1024]{1,0:T(8,128)(2,1)S(1)}, bf16[128,1024]{1,0:T(8,128)(2,1)S(1)}, bf16[128,1536]{1,0:T(8,128)(2,1)S(1)}) custom-call(s32[3]{0:T(128)S(1)} %pad_add_fusion.place, bf16[32,1024]{1,0:T(8,128)(2,1)S(1)} %get-tuple-element.58.arrived.before, bf16[32,1024]{1,0:T(8,128)(2,1)S(1)} %get-tuple-element.58.arrived.before, ...), custom_call_target="tpu_custom_call" | custom-call | flops 1000000000 | bytes 11862540 | tf_op jit(solution)/shard_map/pallas_call | solution.py:267
  113.6 0.7 collective-permute-start.3
  114.4 1.3 shard_map.124
  115.7 0.9 collective-permute-start.5
  116.6 4.6 %shard_map.125 = (bf16[32,1024]{1,0:T(8,128)(2,1)S(1)}, bf16[128,1024]{1,0:T(8,128)(2,1)S(1)}, bf16[128,1536]{1,0:T(8,128)(2,1)S(1)}) custom-call(s32[3]{0:T(128)S(1)} %pad_add_fusion.place, bf16[32,1024]{1,0:T(8,128)(2,1)S(1)} %collective-permute-done.3.arrived, bf16[128,1024]{1,0:T(8,128)(2,1)S(1)} %get-tuple-element.74.before, ...), custom_call_target="tpu_custom_call" | custom-call | flops 1000000000 | bytes 12059148 | tf_op jit(solution)/shard_map/pallas_call | solution.py:267
  121.2 0.7 collective-permute-start.4
  121.8 1.3 shard_map.126
  123.2 0.7 collective-permute-start.7
  123.9 4.6 %shard_map.127 = (bf16[32,1024]{1,0:T(8,128)(2,1)S(1)}, bf16[128,1024]{1,0:T(8,128)(2,1)S(1)}, bf16[128,1536]{1,0:T(8,128)(2,1)S(1)}) custom-call(s32[3]{0:T(128)S(1)} %pad_add_fusion.place, bf16[32,1024]{1,0:T(8,128)(2,1)S(1)} %collective-permute-done.4.arrived, bf16[128,1024]{1,0:T(8,128)(2,1)S(1)} %get-tuple-element.81.before, ...), custom_call_target="tpu_custom_call" | custom-call | flops 1000000000 | bytes 12059148 | tf_op jit(solution)/shard_map/pallas_call | solution.py:267
  128.4 1.3 collective-permute-start.6
  129.7 1.3 shard_map.128
  131.1 0.6 copy-done.11
  131.7 15.3 %collective-permute-done.6.arrived = bf16[32,1024]{1,0:T(8,128)(2,1)S(1)} collective-permute-done((bf16[32,1024]{1,0:T(8,128)(2,1)S(1)}, bf16[32,1024]{1,0:T(8,128)(2,1)S(1)}, u32[]{:S(2)}, u32[]{:S(2)}) %collective-permute-start.6) | collective-permute-done | bytes 65568 | tf_op jit(solution)/shard_map/ppermute | solution.py:385
  147.0 5.2 %shard_map.129 = (bf16[32,1024]{1,0:T(8,128)(2,1)}, bf16[128,1024]{1,0:T(8,128)(2,1)S(1)}, bf16[128,1536]{1,0:T(8,128)(2,1)S(1)}) custom-call(s32[3]{0:T(128)S(1)} %pad_add_fusion.place, bf16[32,1024]{1,0:T(8,128)(2,1)S(1)} %collective-permute-done.6.arrived, bf16[128,1024]{1,0:T(8,128)(2,1)S(1)} %get-tuple-element.88.before, ...), custom_call_target="tpu_custom_call" | custom-call | flops 1000000000 | bytes 12059148 | tf_op jit(solution)/shard_map/pallas_call | solution.py:267
  152.2 1.5 shard_map.130
  153.7 0.6 copy-done.8
  154.3 1.9 collective-permute-start.8
  156.3 1.9 collective-permute-done.8
  158.1 1.0 add_convert_fusion
  159.1 6.2 %all-to-all-start = ((bf16[16,32,512]{2,1,0:T(8,128)(2,1)}), bf16[16,32,512]{2,1,0:T(8,128)(2,1)}, u32[]{:S(2)}, u32[]{:S(2)}) async-start(bf16[16,32,512]{2,1,0:T(8,128)(2,1)} %add_convert_fusion), calls=%async_computation | async-start | bytes 1048576 | tf_op jit(solution)/shard_map/all_to_all | solution.py:294
  165.3 1.3 collective-permute-start.9
  166.6 0.9 copy-done.1
  167.6 0.9 copy-done.2
  168.5 0.9 copy-done.7
  169.5 0.9 copy-done.9
  170.4 1.4 shard_map.131
  171.8 1.0 collective-permute-done.9.arrived
  172.9 2.0 shard_map.132
  174.9 8.7 %all-to-all-done = bf16[16,32,512]{2,1,0:T(8,128)(2,1)} async-done(((bf16[16,32,512]{2,1,0:T(8,128)(2,1)}), bf16[16,32,512]{2,1,0:T(8,128)(2,1)}, u32[]{:S(2)}, u32[]{:S(2)}) %all-to-all-start) | async-done | bytes 524320 | tf_op jit(solution)/shard_map/all_to_all | solution.py:294
  183.6 1.1 reduce_sum.21
  184.7 22.1 %all_to_all.10 = bf16[16,32,512]{2,1,0:T(8,128)(2,1)S(1)} all-to-all(bf16[16,32,512]{2,1,0:T(8,128)(2,1)S(1)} %broadcast_in_dim.18), channel_id=1, replica_groups=mesh['seg'=16,'dp'=32] {'seg'}, dimensions={0} | all-to-all | bytes 1048576 | tf_op jit(solution)/shard_map/all_to_all | solution.py:301
  206.9 0.1 convert_reduce_fusion
  207.0 0.6 fusion
  (24 shorter events, 0.1 us)
Async XLA Ops:
  7.2 76.1 %all-gather.3.cloned.1.call-start = ((), (), s32[]{:S(2)}) async-start(), calls=%async_computation.2 | async-start | bytes 5406720 | tf_op jit(solution)/shard_map/all_gather | solution.py:314
  88.7 0.7 copy-start.6
  89.4 16.1 %collective-permute-start.2 = (bf16[160,512]{1,0:T(8,128)(2,1)S(1)}, bf16[160,512]{1,0:T(8,128)(2,1)S(1)}, u32[]{:S(2)}, u32[]{:S(2)}) collective-permute-start(bf16[160,512]{1,0:T(8,128)(2,1)S(1)} %get-tuple-element.61.refs_0_), channel_id=1, source_target_pairs={{0,32},{32,64},{64,96},{96,0},{128,160},{160,192},{192,224},{224,1... | collective-permute-start | bytes 491528 | tf_op jit(solution)/shard_map/ppermute | solution.py:343
  95.3 11.5 %collective-permute-start.1 = (bf16[160,512]{1,0:T(8,128)(2,1)S(1)}, bf16[160,512]{1,0:T(8,128)(2,1)S(1)}, u32[]{:S(2)}, u32[]{:S(2)}) collective-permute-start(bf16[160,512]{1,0:T(8,128)(2,1)S(1)} %get-tuple-element.61.refs_0_), channel_id=1, source_target_pairs={{0,64},{32,96},{64,0},{96,32},{128,192},{160,224},{192,128},{224,1... | collective-permute-start | bytes 491528 | tf_op jit(solution)/shard_map/ppermute | solution.py:343
  97.6 9.2 %collective-permute-start = (bf16[160,512]{1,0:T(8,128)(2,1)S(1)}, bf16[160,512]{1,0:T(8,128)(2,1)S(1)}, u32[]{:S(2)}, u32[]{:S(2)}) collective-permute-start(bf16[160,512]{1,0:T(8,128)(2,1)S(1)} %get-tuple-element.61.refs_0_), channel_id=1, source_target_pairs={{0,96},{32,0},{64,32},{96,64},{128,224},{160,128},{192,160},{224,1... | collective-permute-start | bytes 491528 | tf_op jit(solution)/shard_map/ppermute | solution.py:343
  109.1 5.3 %copy-start = (bf16[1,1,128,1024]{3,2,1,0:T(8,128)(2,1)S(1)}, bf16[1,1,128,1024]{3,2,1,0:T(8,128)(2,1)}, u32[]{:S(2)}) copy-start(bf16[1,1,128,1024]{3,2,1,0:T(8,128)(2,1)} %all-gather) | copy-start | bytes 786436
  109.1 5.3 %copy-start.5 = (bf16[1,32,1024]{2,1,0:T(8,128)(2,1)S(1)}, bf16[1,32,1024]{2,1,0:T(8,128)(2,1)}, u32[]{:S(2)}) copy-start(bf16[1,32,1024]{2,1,0:T(8,128)(2,1)} %param.12) | copy-start | bytes 196612
  109.1 5.3 %copy-start.10 = (f32[1024]{0:T(1024)S(1)}, f32[1024]{0:T(1024)}, u32[]{:S(2)}) copy-start(f32[1024]{0:T(1024)} %param.13) | copy-start | bytes 12292
  113.6 2.1 collective-permute-start.3
  115.7 6.1 %collective-permute-start.5 = (bf16[32,1024]{1,0:T(8,128)(2,1)S(1)}, bf16[32,1024]{1,0:T(8,128)(2,1)S(1)}, u32[]{:S(2)}, u32[]{:S(2)}) collective-permute-start(bf16[32,1024]{1,0:T(8,128)(2,1)S(1)} %get-tuple-element.76), channel_id=1, source_target_pairs={{384,256},{416,288},{448,320},{480,352},{385,257},{417,289},{449,3... | collective-permute-start | bytes 196616 | tf_op jit(solution)/shard_map/ppermute | solution.py:394
  121.2 2.0 collective-permute-start.4
  123.2 6.5 %collective-permute-start.7 = (bf16[32,1024]{1,0:T(8,128)(2,1)S(1)}, bf16[32,1024]{1,0:T(8,128)(2,1)S(1)}, u32[]{:S(2)}, u32[]{:S(2)}) collective-permute-start(bf16[32,1024]{1,0:T(8,128)(2,1)S(1)} %get-tuple-element.83), channel_id=1, source_target_pairs={{256,128},{288,160},{320,192},{352,224},{257,129},{289,161},{321,1... | collective-permute-start | bytes 196616 | tf_op jit(solution)/shard_map/ppermute | solution.py:394
  128.4 18.6 %collective-permute-start.6 = (bf16[32,1024]{1,0:T(8,128)(2,1)S(1)}, bf16[32,1024]{1,0:T(8,128)(2,1)S(1)}, u32[]{:S(2)}, u32[]{:S(2)}) collective-permute-start(bf16[32,1024]{1,0:T(8,128)(2,1)S(1)} %get-tuple-element.82), channel_id=1, source_target_pairs={{128,0},{160,32},{192,64},{224,96},{129,1},{161,33},{193,65},{225,... | collective-permute-start | bytes 196616 | tf_op jit(solution)/shard_map/ppermute | solution.py:385
  131.1 0.6 copy-start.11
  152.2 1.5 copy-start.3
  153.7 0.7 copy-start.8
  154.3 3.8 %collective-permute-start.8 = (bf16[16,32,512]{2,1,0:T(8,128)(2,1)S(1)}, bf16[16,32,512]{2,1,0:T(8,128)(2,1)S(1)}, u32[]{:S(2)}, u32[]{:S(2)}) collective-permute-start(bf16[16,32,512]{2,1,0:T(8,128)(2,1)S(1)} %get-tuple-element.93), channel_id=1, source_target_pairs={{0,1},{1,0},{2,3},{3,2},{4,5},{5,4},{6,7},{7,6},{8,9},{9,8},{10,11... | collective-permute-start | bytes 1572872 | tf_op jit(solution)/shard_map/ppermute | solution.py:291
  159.1 24.5 %all-to-all-start = ((bf16[16,32,512]{2,1,0:T(8,128)(2,1)}), bf16[16,32,512]{2,1,0:T(8,128)(2,1)}, u32[]{:S(2)}, u32[]{:S(2)}) async-start(bf16[16,32,512]{2,1,0:T(8,128)(2,1)} %add_convert_fusion), calls=%async_computation | async-start | bytes 1048576 | tf_op jit(solution)/shard_map/all_to_all | solution.py:294
  165.3 7.6 %collective-permute-start.9 = (bf16[32,1024]{1,0:T(8,128)(2,1)}, bf16[32,1024]{1,0:T(8,128)(2,1)S(1)}, u32[]{:S(2)}, u32[]{:S(2)}) collective-permute-start(bf16[32,1024]{1,0:T(8,128)(2,1)} %copy-done.11), channel_id=1, source_target_pairs={{128,0},{160,32},{192,64},{224,96},{129,1},{161,33},{193,65},{225,... | collective-permute-start | bytes 196616 | tf_op jit(solution)/shard_map/ppermute | solution.py:394
  166.6 1.0 copy-start.1
  167.6 0.9 copy-start.2
  168.5 0.9 copy-start.7
  169.5 0.9 copy-start.9
  170.4 2.5 %copy-start.4 = (bf16[128,1536]{1,0:T(8,128)(2,1)S(1)}, bf16[128,1536]{1,0:T(8,128)(2,1)}, u32[]{:S(2)}) copy-start(bf16[128,1536]{1,0:T(8,128)(2,1)} %copy-done.3) | copy-start | bytes 1179652
Sparse Core Ops, SparseCore 0:
  11.7 71.5 all-gather.2

commit v5 on v4

--- a/solution.py
+++ b/solution.py
@@ -97,31 +97,33 @@
 
 
 def token_kernel(
-    mem_hbm, tok_hbm, gout_hbm, gain_hbm, w_hbm, normed_out, qg_out, part_out, kvp_out, wt_out, w, mem, tok, gout, gain, sems
+    place, mem_hbm, tok_hbm, gout_hbm, gain_hbm, own_hbm, other_hbm,
+    normed_out, qg_out, part_out, kvp_out, wt_out, w, wo, mem, tok, gout, gain, sems
 ):
-    first, second = slice(0, D + 2 * KV), slice(D + 2 * KV, 2 * D + 2 * KV)
-    copies = loads(
-        [
-            (mem_hbm, mem),
-            (tok_hbm, tok),
-            (gain_hbm, gain),
-            (w_hbm.at[:, first], w.at[:, first]),
-            (gout_hbm, gout),
-            (w_hbm.at[:, second], w.at[:, second]),
-        ],
-        sems,
-    )
+    core = place[1]
+    across, along, rows, _ = own_hbm.shape
+    pieces, later = [], []
+    inner, outer = slice(0, D + 2 * KV), slice(D + 2 * KV, 2 * D + 2 * KV)
+    for source, side in ((own_hbm, core), (other_hbm, 1 - core)):
+        for i in range(across):
+            for j in range(along):
+                start = pl.multiple_of((j * across + i) * 2 * rows + side * rows, rows)
+                pieces.append((source.at[i, j, :, inner], w.at[pl.ds(start, rows), :]))
+                later.append((source.at[i, j, :, outer], wo.at[pl.ds(start, rows), :]))
+    pairs = [(mem_hbm, mem), (tok_hbm, tok), (gain_hbm, gain)] + pieces + [(gout_hbm, gout)] + later
+    copies = loads(pairs, sems)
     for copy in copies[:3]:
         copy.wait()
     hidden = jnp.concatenate([mem[...].astype(F32), tok[...].astype(F32)], axis=0)
     _, normed = normalised(hidden, gain[...])
     normed_out[...] = normed
-    copies[3].wait()
+    for copy in copies[3 : 3 + len(pieces)]:
+        copy.wait()
     q = nn(normed[MEM:], w[:, :D])
     kv = nn(normed, w[:, D : D + 2 * KV]).astype(BF)
-    copies[4].wait()
-    copies[5].wait()
-    up = nn(gout[...], w[:, D + 2 * KV :])
+    for copy in copies[3 + len(pieces) :]:
+        copy.wait()
+    up = nn(gout[...], wo[...])
     k, v = kv[:, :KV], kv[:, KV:]
     key_at = lax.broadcasted_iota(jnp.int32, (ROWS, PER_GROUP * TOK), 0)
     row_at = lax.broadcasted_iota(jnp.int32, (ROWS, PER_GROUP * TOK), 1) % TOK
@@ -141,31 +143,36 @@
     part = jnp.concatenate([folded(key_parts), folded(value_parts)], axis=1)
     part_out[...] = part
     kvp_out[:MEM, :] = part[:MEM].astype(BF)
-    kvp_out[MEM:, :] = kv[MEM:]
-    wt_out[...] = w[:, : D + 2 * KV].T
-
-
-def mix_kernel(mem4_hbm, last_hbm, gain_hbm, w, wt, mixed_out, qkv_out, hw_out, inv_out, u_out, mem4, last, gain, sems):
-    for copy in loads([(mem4_hbm, mem4), (last_hbm, last), (gain_hbm, gain)], sems):
+    kvp_out[MEM:ROWS, :] = kv[MEM:]
+    kvp_out[ROWS : ROWS + MEM, :] = mem[:, : D // 2]
+    kvp_out[ROWS + MEM :, :] = mem[:, D // 2 :]
+    wt_out[...] = w[...].T
+
+
+def mix_kernel(last_hbm, gain_hbm, wo, wt, mixed_out, u_out, last, gain, sems):
+    for copy in loads([(last_hbm, last), (gain_hbm, gain)], sems):
         copy.wait()
-    inverse, normed = normalised(mem4[...].astype(F32), gain[...])
+    u_out[...] = nn(last[...], wo[...]).astype(BF)
+    scaled = (wt[...].astype(F32) * gain[...]).astype(BF)
+    mixed_out[...] = nn(scaled, wo[...]).astype(BF)
+
+
+def ready_kernel(place, gain, w, wo, *refs):
+    parts, refs = refs[:SPAN], refs[SPAN:]
+    probs_k_out, probs_q_out, krep_out, vrep_out, zq_out, near_out, mem_out, qkv_out, hw_out, inv_out = refs
+    slots = [(place[0] + ahead) % SPAN for ahead in range(SPAN)]
+    spans = [pl.ds(pl.multiple_of(s * MEM, MEM), MEM) for s in slots]
+    for rows, kvp in zip(spans, parts):
+        mem_out[rows, :] = jnp.concatenate([kvp[ROWS : ROWS + MEM, :], kvp[ROWS + MEM :, :]], axis=1)
+        near_out[rows, :] = kvp[:MEM, :].astype(F32)
+    inverse, normed = normalised(mem_out[...].astype(F32), gain[...])
     inv_out[...] = inverse
-    hw_out[...] = nn(mem4[...], w[:, D + 2 * KV :])
-    qkv_out[...] = nn(normed, w[:, : D + 2 * KV])
-    u_out[...] = nn(last[...], w[:, D + 2 * KV :]).astype(BF)
-    scaled = (wt[...].astype(F32) * gain[...]).astype(BF)
-    mixed_out[...] = nn(scaled, w[:, D + 2 * KV :]).astype(BF)
-
-
-def ready_kernel(place, qkv4, *refs):
-    parts, (probs_k_out, probs_q_out, krep_out, vrep_out, zq_out, near_out) = refs[:SPAN], refs[SPAN:]
-    for ahead, kvp in enumerate(parts):
-        s = (place[0] + ahead) % SPAN
-        rows = pl.ds(pl.multiple_of(s * MEM, MEM), MEM)
-        qkv = qkv4[rows, :]
-        near_out[rows, :] = kvp[:MEM, :].astype(F32)
-        k = jnp.concatenate([qkv[:, D : D + KV].astype(BF), kvp[MEM:, :KV]], axis=0)
-        v = jnp.concatenate([qkv[:, D + KV :].astype(BF), kvp[MEM:, KV:]], axis=0)
+    hw_out[...] = nn(mem_out[...], wo[...])
+    qkv_out[...] = nn(normed, w[...])
+    for s, rows, kvp in zip(slots, spans, parts):
+        qkv = qkv_out[rows, :]
+        k = jnp.concatenate([qkv[:, D : D + KV].astype(BF), kvp[MEM:ROWS, :KV]], axis=0)
+        v = jnp.concatenate([qkv[:, D + KV :].astype(BF), kvp[MEM:ROWS, KV:]], axis=0)
         zqs = [stacked(qkv[:, group_columns(g)]) for g in range(GROUPS)]
         kreps = [repeated(k, g) for g in range(GROUPS)]
         raised_k = [jnp.exp(nt(krep, zq) * SCALE) for krep, zq in zip(kreps, zqs)]
@@ -286,6 +293,14 @@
     ]
 
 
+def gathered(shard):
+    docs = lax.axis_size("dp")
+    block = lax.all_gather(shard, "dp", axis=0, axis_index_groups=runs(docs, docs // 8, 8))
+    copies = jnp.broadcast_to(block[None], (4,) + block.shape)
+    own = lax.all_to_all(copies, "dp", 0, 0, tiled=True, axis_index_groups=runs(docs, 4, 2))
+    return own, lax.ppermute(own, "dp", [(i, i ^ 1) for i in range(docs)])
+
+
 def summed_over_documents(mine, other):
     docs = lax.axis_size("dp")
     got = lax.ppermute(other, "dp", [(i, i ^ 1) for i in range(docs)])
@@ -310,53 +325,47 @@
     block = position // SPAN
     place = jnp.stack([position % SPAN, lax.axis_index("dp") % 2, turns - 1 - block]).astype(jnp.int32)
 
-    shard = jnp.concatenate([query_weight, key_weight, value_weight, out_weight.T], axis=1)
-    w = lax.all_gather(shard, "dp", axis=0, tiled=True)
-    mem4 = lax.all_gather(mem, "seg", axis=0, tiled=True, axis_index_groups=runs(n_seg, SPAN, 1))
-    w, mem4, place = lax.optimization_barrier((w, mem4, place))
+    near_w, far_w = gathered(jnp.concatenate([query_weight, key_weight, value_weight, out_weight.T], axis=1))
+    near_w, far_w, place = lax.optimization_barrier((near_w, far_w, place))
 
     dma = pltpu.SemaphoreType.DMA
-    normed, qg, part, kvp, wt, w = call(
+    normed, qg, part, kvp, wt, w, wo = call(
         token_kernel,
         [
             shape((ROWS, D)),
             shape((TOK, D)),
             shape((ROWS, 2 * KV), F32),
-            shape((ROWS, 2 * KV)),
+            shape((ROWS + 2 * MEM, 2 * KV)),
             shape((D + 2 * KV, D)),
-            shape((D, 2 * D + 2 * KV)),
+            shape((D, D + 2 * KV)),
+            shape((D, D)),
         ],
-        (mem, tok, gout, gain, w),
+        (place, mem, tok, gout, gain, near_w, far_w),
         1_500_000_000,
-        far=5,
+        scalars=1,
+        far=6,
         scratch=(
             pltpu.VMEM((MEM, D), BF),
             pltpu.VMEM((TOK, D), BF),
             pltpu.VMEM((TOK, D), BF),
             pltpu.VMEM((1, D), F32),
-            dma((6,)),
+            dma((4 + 2 * docs,)),
         ),
     )
     kvps = [kvp]
     for ahead in range(1, SPAN):
         route = [(i, i // SPAN * SPAN + (i - ahead) % SPAN) for i in range(n_seg)]
         kvps.append(lax.ppermute(kvp, "seg", route))
-    mixed, qkv4, hw4, inv4, arrived = call(
+    mixed, arrived = call(
         mix_kernel,
-        [
-            shape((D + 2 * KV, D)),
-            shape((SPAN * MEM, D + 2 * KV), F32),
-            shape((SPAN * MEM, D), F32),
-            shape((SPAN * MEM, 1), F32),
-            shape((MEM, D)),
-        ],
-        (mem4, last, gain, w, wt),
+        [shape((D + 2 * KV, D)), shape((MEM, D))],
+        (last, gain, wo, wt),
         4_000_000_000,
-        far=3,
-        scratch=(pltpu.VMEM((SPAN * MEM, D), BF), pltpu.VMEM((MEM, D), BF), pltpu.VMEM((1, D), F32), dma((3,))),
+        far=2,
+        scratch=(pltpu.VMEM((MEM, D), BF), pltpu.VMEM((1, D), F32), dma((2,))),
     )
     count = SPAN * GROUPS
-    probs_k, probs_q, krep, vrep, zq, near = call(
+    probs_k, probs_q, krep, vrep, zq, near, mem4, qkv4, hw4, inv4 = call(
         ready_kernel,
         [
             shape((count, ROWS, PER_GROUP * MEM), F32),
@@ -365,8 +374,12 @@
             shape((count, ROWS, WIDE)),
             shape((count, PER_GROUP * MEM, WIDE)),
             shape((SPAN * MEM, 2 * KV), F32),
+            shape((SPAN * MEM, D)),
+            shape((SPAN * MEM, D + 2 * KV), F32),
+            shape((SPAN * MEM, D), F32),
+            shape((SPAN * MEM, 1), F32),
         ],
-        (place, qkv4, *kvps),
+        (place, gain, w, wo, *kvps),
         400_000_000,
         scalars=1,
     )

time: 215 us -> 189 us (0.88)
  waiting for transfers between devices: 84.9 us -> 32.6 us
  blocking collectives: 39.8 us -> 78.5 us
  between operations: 14.4 us -> 1 us
    all_gather x1 -> x0, waiting for transfers between devices: 56.7 us -> none  [body(): w = lax.all_gather(shard, 'dp', axis=0, tiled=True)]
    all_to_all x0 -> x1, blocking collectives: none -> 31.8 us  [gathered(): lax.all_to_all(copies, 'dp', 0, 0, tiled=True, axis_index_groups=runs(doc...]
    ppermute x0 -> x1, waiting for transfers between devices: none -> 4.9 us  [gathered(): return (own, lax.ppermute(own, 'dp', [(i, i ^ 1) for i in range(docs)]))]
    all_to_all x1, blocking collectives: 22.1 us -> 26 us  [summed_over_segments(): lax.all_to_all(copies, 'seg', 0, 0, tiled=True).astype(F32)]
    all_gather x1, blocking collectives: 17.7 us -> 20.6 us  [gathered(): lax.all_gather(shard, 'dp', axis=0, axis_index_groups=runs(docs, docs //...]
    ppermute x3, waiting for transfers between devices: 15.3 us -> 18.2 us  [body(): arrived = lax.ppermute(send, 'seg', route)]
    all_to_all x1, waiting for transfers between devices: 8.69 us -> 6.23 us  [summed_over_documents(): lax.all_to_all(block, 'dp', 0, 0, tiled=True, axis_index_groups=runs(docs...]
  transfers between devices with their start and end apart: 12 -> 12, of which waited for: 6 -> 6; matrix products, arithmetic and copies ran while one was open for 0% -> 0% of each run, Pallas kernels for 10% -> 11%
where the time goes in v5:
time: 189 us
  blocking collectives  78.5 us (42%)
  Pallas kernels  41.8 us (22%)
  waiting for transfers between devices  32.6 us (17%)
  starting transfers between devices  25.5 us (13%)
  local copies, waits for them, and re-layouts  5.98 us (3%)
  other arithmetic  3.19 us (2%)
    pallas_call x13, Pallas kernels, call(): pl.pallas_call(kernel, out_shape=outs, in_specs=[smem] * scalars + [hbm]...  41.8 us
    all_to_all x1, blocking collectives, gathered(): lax.all_to_all(copies, 'dp', 0, 0, tiled=True, axis_index_groups=runs(doc...  31.8 us
    all_to_all x1, blocking collectives, summed_over_segments(): lax.all_to_all(copies, 'seg', 0, 0, tiled=True).astype(F32)  26 us
    all_gather x1, blocking collectives, gathered(): lax.all_gather(shard, 'dp', axis=0, axis_index_groups=runs(docs, docs //...  20.6 us
    ppermute x3, waiting for transfers between devices, body(): arrived = lax.ppermute(send, 'seg', route)  18.2 us
    ppermute x3, starting transfers between devices, body(): kvps.append(lax.ppermute(kvp, 'seg', route))  11.2 us
    all_to_all x1, waiting for transfers between devices, summed_over_documents(): lax.all_to_all(block, 'dp', 0, 0, tiled=True, axis_index_groups=runs(docs...  6.23 us
    unnamed x24, local copies, waits for them, and re-layouts  5.06 us
  transfers between devices with their start and end apart: 12, of which 6 were waited for; matrix products, arithmetic and copies ran while one was open for 0% of the time, Pallas kernels for 11%

profile of v5, /device:TPU:8, one launch (start us, length us, event | category | flops | bytes accessed | tf_op | source)
XLA Modules:
  0.0 188.7 jit_solution(11229253503788950430)
XLA Ops:
  0.6 0.9 pad_maximum_fusion
  1.6 20.6 %all-gather = bf16[128,2560]{1,0:T(8,128)(2,1)S(1)} all-gather(bf16[32,2560]{1,0:T(8,128)(2,1)S(1)} %pad_maximum_fusion), channel_id=2, replica_groups={{0,8,16,24},{1,9,17,25},{2,10,18,26},{3,11,19,27},{4,12,20,28},{5,13,21..., dimensions={0}, use_global_device_ids=true | all-gather | bytes 819200 | tf_op jit(solution)/shard_map/all_gather | solution.py:298
  22.2 0.2 broadcast_in_dim.10
  22.5 31.8 %all_to_all.15.own_hbm = bf16[4,4,32,2560]{3,2,1,0:T(8,128)(2,1)S(1)} all-to-all(bf16[4,4,32,2560]{3,2,1,0:T(8,128)(2,1)S(1)} %broadcast_in_dim.10), channel_id=1, replica_groups={{0,2,4,6},{1,3,5,7},{8,10,12,14},{9,11,13,15},{16,18,20,22},{17,19,21,2..., dimensions={0} | all-to-all | bytes 5242880 | tf_op jit(solution)/shard_map/all_to_all | solution.py:300
  54.3 1.9 %collective-permute-start = (bf16[4,4,32,2560]{3,2,1,0:T(8,128)(2,1)S(1)}, bf16[4,4,32,2560]{3,2,1,0:T(8,128)(2,1)}, u32[]{:S(2)}, u32[]{:S(2)}) collective-permute-start(bf16[4,4,32,2560]{3,2,1,0:T(8,128)(2,1)S(1)} %all_to_all.15.own_hbm), channel_id=1, source_target_pairs={{0,1},{1,0},{2,3},{3,2},{4,5},{5,4},{6,7},{7,6},{8,9},{9,8},{10,11... | collective-permute-start | bytes 7864328 | tf_op jit(solution)/shard_map/ppermute | solution.py:301
  56.2 0.1 pad_add_fusion.place
  56.3 4.9 %collective-permute-done.other_hbm = bf16[4,4,32,2560]{3,2,1,0:T(8,128)(2,1)} collective-permute-done((bf16[4,4,32,2560]{3,2,1,0:T(8,128)(2,1)S(1)}, bf16[4,4,32,2560]{3,2,1,0:T(8,128)(2,1)}, u32[]{:S(2)}, u32[]{:S(2)}) %collective-permute-start) | collective-permute-done | bytes 2621472 | tf_op jit(solution)/shard_map/ppermute | solution.py:301
  61.2 6.4 %shard_map.120 = (bf16[160,1024]{1,0:T(8,128)(2,1)S(1)}, bf16[128,1024]{1,0:T(8,128)(2,1)S(1)}, f32[160,512]{1,0:T(8,128)S(1)}, bf16[224,512]{1,0:T(8,128)(2,1)S...) custom-call(s32[3]{0:T(128)S(1)} %pad_add_fusion.place, ...), custom_call_target="tpu_custom_call" | custom-call | flops 1500000000 | bytes 15372300 | tf_op jit(solution)/shard_map/pallas_call | solution.py:274
  67.6 0.0 copy-start.5
  67.6 2.2 %collective-permute-start.1 = (bf16[224,512]{1,0:T(8,128)(2,1)S(1)}, bf16[224,512]{1,0:T(8,128)(2,1)S(1)}, u32[]{:S(2)}, u32[]{:S(2)}) collective-permute-start(bf16[224,512]{1,0:T(8,128)(2,1)S(1)} %get-tuple-element.63.refs_0_), channel_id=1, source_target_pairs={{0,96},{32,0},{64,32},{96,64},{128,224},{160,128},{192,160},{224,1... | collective-permute-start | bytes 688136 | tf_op jit(solution)/shard_map/ppermute | solution.py:358
  69.8 4.3 %collective-permute-start.2 = (bf16[224,512]{1,0:T(8,128)(2,1)S(1)}, bf16[224,512]{1,0:T(8,128)(2,1)S(1)}, u32[]{:S(2)}, u32[]{:S(2)}) collective-permute-start(bf16[224,512]{1,0:T(8,128)(2,1)S(1)} %get-tuple-element.63.refs_0_), channel_id=1, source_target_pairs={{0,64},{32,96},{64,0},{96,32},{128,192},{160,224},{192,128},{224,1... | collective-permute-start | bytes 688136 | tf_op jit(solution)/shard_map/ppermute | solution.py:358
  74.1 4.7 %collective-permute-start.3 = (bf16[224,512]{1,0:T(8,128)(2,1)S(1)}, bf16[224,512]{1,0:T(8,128)(2,1)S(1)}, u32[]{:S(2)}, u32[]{:S(2)}) collective-permute-start(bf16[224,512]{1,0:T(8,128)(2,1)S(1)} %get-tuple-element.63.refs_0_), channel_id=1, source_target_pairs={{0,32},{32,64},{64,96},{96,0},{128,160},{160,192},{192,224},{224,1... | collective-permute-start | bytes 688136 | tf_op jit(solution)/shard_map/ppermute | solution.py:358
  78.8 4.7 %shard_map.121 = (bf16[1536,1024]{1,0:T(8,128)(2,1)S(1)}, bf16[32,1024]{1,0:T(8,128)(2,1)S(1)}) custom-call(bf16[32,1024]{1,0:T(8,128)(2,1)} %bitcast.16, f32[1,1024]{1,0:T(1,128)} %bitcast.20, bf16[1024,1024]{1,0:T(8,128)(2,1)S(1)} %get-tuple-element.58.wo, bf16[1536,1024]{1,0:T(8,128)(2,1)S(1)} %get-tuple-element.59.wt), custom_call_target="tpu_custom_call" | custom-call | flops 4000000000 | bytes 8523776 | tf_op jit(solution)/shard_map/pallas_call | solution.py:274
  83.6 0.3 collective-permute-done.3.refs_3_
  83.9 3.0 %shard_map.122 = (f32[16,160,128]{2,1,0:T(8,128)S(1)}, f32[16,128,160]{2,1,0:T(8,128)S(1)}, bf16[16,160,256]{2,1,0:T(8,128)(2,1)S(1)}, bf16[16,160,256]{2,1,0:T(...) custom-call(s32[3]{0:T(128)S(1)} %pad_add_fusion.place, ...), custom_call_target="tpu_custom_call" | custom-call | flops 400000000 | bytes 14291468 | tf_op jit(solution)/shard_map/pallas_call | solution.py:274
  86.9 4.6 %shard_map.123 = (bf16[32,1024]{1,0:T(8,128)(2,1)S(1)}, bf16[128,1024]{1,0:T(8,128)(2,1)S(1)}, bf16[128,1536]{1,0:T(8,128)(2,1)S(1)}) custom-call(s32[3]{0:T(128)S(1)} %pad_add_fusion.place, bf16[32,1024]{1,0:T(8,128)(2,1)S(1)} %get-tuple-element.60.arrived.before, bf16[32,1024]{1,0:T(8,128)(2,1)S(1)} %get-tuple-element.60.arrived.before, ...), custom_call_target="tpu_custom_call" | custom-call | flops 1000000000 | bytes 11862540 | tf_op jit(solution)/shard_map/pallas_call | solution.py:274
  91.4 0.7 collective-permute-start.4
  92.1 1.3 shard_map.124
  93.5 0.9 collective-permute-start.6
  94.4 4.6 %shard_map.125 = (bf16[32,1024]{1,0:T(8,128)(2,1)S(1)}, bf16[128,1024]{1,0:T(8,128)(2,1)S(1)}, bf16[128,1536]{1,0:T(8,128)(2,1)S(1)}) custom-call(s32[3]{0:T(128)S(1)} %pad_add_fusion.place, bf16[32,1024]{1,0:T(8,128)(2,1)S(1)} %collective-permute-done.4.arrived, bf16[128,1024]{1,0:T(8,128)(2,1)S(1)} %get-tuple-element.78.before, ...), custom_call_target="tpu_custom_call" | custom-call | flops 1000000000 | bytes 12059148 | tf_op jit(solution)/shard_map/pallas_call | solution.py:274
  98.9 0.7 collective-permute-start.5
  99.6 1.3 shard_map.126
  101.0 0.7 collective-permute-start.8
  101.7 4.6 %shard_map.127 = (bf16[32,1024]{1,0:T(8,128)(2,1)S(1)}, bf16[128,1024]{1,0:T(8,128)(2,1)S(1)}, bf16[128,1536]{1,0:T(8,128)(2,1)S(1)}) custom-call(s32[3]{0:T(128)S(1)} %pad_add_fusion.place, bf16[32,1024]{1,0:T(8,128)(2,1)S(1)} %collective-permute-done.5.arrived, bf16[128,1024]{1,0:T(8,128)(2,1)S(1)} %get-tuple-element.85.before, ...), custom_call_target="tpu_custom_call" | custom-call | flops 1000000000 | bytes 12059148 | tf_op jit(solution)/shard_map/pallas_call | solution.py:274
  106.2 1.3 collective-permute-start.7
  107.5 1.3 shard_map.128
  108.9 0.6 copy-done.10
  109.5 18.2 %collective-permute-done.7.arrived = bf16[32,1024]{1,0:T(8,128)(2,1)S(1)} collective-permute-done((bf16[32,1024]{1,0:T(8,128)(2,1)S(1)}, bf16[32,1024]{1,0:T(8,128)(2,1)S(1)}, u32[]{:S(2)}, u32[]{:S(2)}) %collective-permute-start.7) | collective-permute-done | bytes 65568 | tf_op jit(solution)/shard_map/ppermute | solution.py:398
  127.7 5.2 %shard_map.129 = (bf16[32,1024]{1,0:T(8,128)(2,1)}, bf16[128,1024]{1,0:T(8,128)(2,1)S(1)}, bf16[128,1536]{1,0:T(8,128)(2,1)S(1)}) custom-call(s32[3]{0:T(128)S(1)} %pad_add_fusion.place, bf16[32,1024]{1,0:T(8,128)(2,1)S(1)} %collective-permute-done.7.arrived, bf16[128,1024]{1,0:T(8,128)(2,1)S(1)} %get-tuple-element.92.before, ...), custom_call_target="tpu_custom_call" | custom-call | flops 1000000000 | bytes 12059148 | tf_op jit(solution)/shard_map/pallas_call | solution.py:274
  133.0 1.5 shard_map.130
  134.4 0.6 copy-done.8
  135.1 1.9 %collective-permute-start.9 = (bf16[16,32,512]{2,1,0:T(8,128)(2,1)S(1)}, bf16[16,32,512]{2,1,0:T(8,128)(2,1)S(1)}, u32[]{:S(2)}, u32[]{:S(2)}) collective-permute-start(bf16[16,32,512]{2,1,0:T(8,128)(2,1)S(1)} %get-tuple-element.97), channel_id=1, source_target_pairs={{0,1},{1,0},{2,3},{3,2},{4,5},{5,4},{6,7},{7,6},{8,9},{9,8},{10,11... | collective-permute-start | bytes 1572872 | tf_op jit(solution)/shard_map/ppermute | solution.py:306
  137.0 1.9 collective-permute-done.9
  138.9 1.0 add_convert_fusion
  139.9 5.1 %all-to-all-start.1 = ((bf16[16,32,512]{2,1,0:T(8,128)(2,1)}), bf16[16,32,512]{2,1,0:T(8,128)(2,1)}, u32[]{:S(2)}, u32[]{:S(2)}) async-start(bf16[16,32,512]{2,1,0:T(8,128)(2,1)} %add_convert_fusion), calls=%async_computation.1 | async-start | bytes 1048576 | tf_op jit(solution)/shard_map/all_to_all | solution.py:309
  144.9 1.3 collective-permute-start.10
  146.2 0.9 copy-done
  147.2 0.9 copy-done.1
  148.1 0.9 copy-done.6
  149.1 0.9 copy-done.9
  150.0 1.4 shard_map.131
  151.5 1.0 collective-permute-done.10.arrived
  152.5 2.0 %shard_map.132 = bf16[32,1024]{1,0:T(8,128)(2,1)} custom-call(s32[3]{0:T(128)S(1)} %pad_add_fusion.place, bf16[32,1024]{1,0:T(8,128)(2,1)S(1)} %collective-permute-done.10.arrived, bf16[32,1024]{1,0:T(8,128)(2,1)S(1)} %get-tuple-element.101.held, bf16[128,1536]{1,0:T(8,128)(2,1)S(1)} %copy-done.3, bf16[1536,1024]{1,0:T(8,128)(2,1)S(1)} %get-tuple-element.59.wt, ...), custom_call_target="tpu_custom_call" | custom-call | flops 400000000 | bytes 4002316 | tf_op jit(solution)/shard_map/pallas_call | solution.py:274
  154.5 6.2 %all-to-all-done.1 = bf16[16,32,512]{2,1,0:T(8,128)(2,1)} async-done(((bf16[16,32,512]{2,1,0:T(8,128)(2,1)}), bf16[16,32,512]{2,1,0:T(8,128)(2,1)}, u32[]{:S(2)}, u32[]{:S(2)}) %all-to-all-start.1) | async-done | bytes 524320 | tf_op jit(solution)/shard_map/all_to_all | solution.py:309
  160.7 1.1 reduce_sum.21
  161.9 26.0 %all_to_all.16 = bf16[16,32,512]{2,1,0:T(8,128)(2,1)S(1)} all-to-all(bf16[16,32,512]{2,1,0:T(8,128)(2,1)S(1)} %broadcast_in_dim.25), channel_id=1, replica_groups=mesh['seg'=16,'dp'=32] {'seg'}, dimensions={0} | all-to-all | bytes 1048576 | tf_op jit(solution)/shard_map/all_to_all | solution.py:316
  187.9 0.1 convert_reduce_fusion
  188.0 0.6 fusion
  (25 shorter events, 0.1 us)
Async XLA Ops:
  54.3 6.9 %copy-start.11 = (bf16[4,4,32,2560]{3,2,1,0:T(8,128)(2,1)}, bf16[4,4,32,2560]{3,2,1,0:T(8,128)(2,1)S(1)}, u32[]{:S(2)}) copy-start(bf16[4,4,32,2560]{3,2,1,0:T(8,128)(2,1)S(1)} %all_to_all.15.own_hbm) | copy-start | bytes 7864324
  54.3 6.9 %collective-permute-start = (bf16[4,4,32,2560]{3,2,1,0:T(8,128)(2,1)S(1)}, bf16[4,4,32,2560]{3,2,1,0:T(8,128)(2,1)}, u32[]{:S(2)}, u32[]{:S(2)}) collective-permute-start(bf16[4,4,32,2560]{3,2,1,0:T(8,128)(2,1)S(1)} %all_to_all.15.own_hbm), channel_id=1, source_target_pairs={{0,1},{1,0},{2,3},{3,2},{4,5},{5,4},{6,7},{7,6},{8,9},{9,8},{10,11... | collective-permute-start | bytes 7864328 | tf_op jit(solution)/shard_map/ppermute | solution.py:301
  67.6 16.0 %copy-start.5 = (bf16[128,1024]{1,0:T(8,128)(2,1)}, bf16[128,1024]{1,0:T(8,128)(2,1)S(1)}, u32[]{:S(2)}) copy-start(bf16[128,1024]{1,0:T(8,128)(2,1)S(1)} %get-tuple-element.98.qg) | copy-start | bytes 786436
  67.6 16.0 %collective-permute-start.1 = (bf16[224,512]{1,0:T(8,128)(2,1)S(1)}, bf16[224,512]{1,0:T(8,128)(2,1)S(1)}, u32[]{:S(2)}, u32[]{:S(2)}) collective-permute-start(bf16[224,512]{1,0:T(8,128)(2,1)S(1)} %get-tuple-element.63.refs_0_), channel_id=1, source_target_pairs={{0,96},{32,0},{64,32},{96,64},{128,224},{160,128},{192,160},{224,1... | collective-permute-start | bytes 688136 | tf_op jit(solution)/shard_map/ppermute | solution.py:358
  69.8 13.8 %collective-permute-start.2 = (bf16[224,512]{1,0:T(8,128)(2,1)S(1)}, bf16[224,512]{1,0:T(8,128)(2,1)S(1)}, u32[]{:S(2)}, u32[]{:S(2)}) collective-permute-start(bf16[224,512]{1,0:T(8,128)(2,1)S(1)} %get-tuple-element.63.refs_0_), channel_id=1, source_target_pairs={{0,64},{32,96},{64,0},{96,32},{128,192},{160,224},{192,128},{224,1... | collective-permute-start | bytes 688136 | tf_op jit(solution)/shard_map/ppermute | solution.py:358
  74.1 9.8 %collective-permute-start.3 = (bf16[224,512]{1,0:T(8,128)(2,1)S(1)}, bf16[224,512]{1,0:T(8,128)(2,1)S(1)}, u32[]{:S(2)}, u32[]{:S(2)}) collective-permute-start(bf16[224,512]{1,0:T(8,128)(2,1)S(1)} %get-tuple-element.63.refs_0_), channel_id=1, source_target_pairs={{0,32},{32,64},{64,96},{96,0},{128,160},{160,192},{192,224},{224,1... | collective-permute-start | bytes 688136 | tf_op jit(solution)/shard_map/ppermute | solution.py:358
  78.8 5.1 %copy-start.7 = (f32[1024]{0:T(1024)S(1)}, f32[1024]{0:T(1024)}, u32[]{:S(2)}) copy-start(f32[1024]{0:T(1024)} %param.13) | copy-start | bytes 12292
  86.9 5.2 %copy-start.4 = (bf16[1,32,1024]{2,1,0:T(8,128)(2,1)S(1)}, bf16[1,32,1024]{2,1,0:T(8,128)(2,1)}, u32[]{:S(2)}) copy-start(bf16[1,32,1024]{2,1,0:T(8,128)(2,1)} %param.12) | copy-start | bytes 196612
  91.4 2.0 %collective-permute-start.4 = (bf16[32,1024]{1,0:T(8,128)(2,1)S(1)}, bf16[32,1024]{1,0:T(8,128)(2,1)S(1)}, u32[]{:S(2)}, u32[]{:S(2)}) collective-permute-start(bf16[32,1024]{1,0:T(8,128)(2,1)S(1)} %get-tuple-element.73), channel_id=1, source_target_pairs={{384,256},{416,288},{448,320},{480,352},{385,257},{417,289},{449,3... | collective-permute-start | bytes 196616 | tf_op jit(solution)/shard_map/ppermute | solution.py:398
  93.5 6.1 %collective-permute-start.6 = (bf16[32,1024]{1,0:T(8,128)(2,1)S(1)}, bf16[32,1024]{1,0:T(8,128)(2,1)S(1)}, u32[]{:S(2)}, u32[]{:S(2)}) collective-permute-start(bf16[32,1024]{1,0:T(8,128)(2,1)S(1)} %get-tuple-element.80), channel_id=1, source_target_pairs={{384,256},{416,288},{448,320},{480,352},{385,257},{417,289},{449,3... | collective-permute-start | bytes 196616 | tf_op jit(solution)/shard_map/ppermute | solution.py:407
  98.9 2.0 %collective-permute-start.5 = (bf16[32,1024]{1,0:T(8,128)(2,1)S(1)}, bf16[32,1024]{1,0:T(8,128)(2,1)S(1)}, u32[]{:S(2)}, u32[]{:S(2)}) collective-permute-start(bf16[32,1024]{1,0:T(8,128)(2,1)S(1)} %get-tuple-element.79), channel_id=1, source_target_pairs={{256,128},{288,160},{320,192},{352,224},{257,129},{289,161},{321,1... | collective-permute-start | bytes 196616 | tf_op jit(solution)/shard_map/ppermute | solution.py:398
  101.0 6.5 %collective-permute-start.8 = (bf16[32,1024]{1,0:T(8,128)(2,1)S(1)}, bf16[32,1024]{1,0:T(8,128)(2,1)S(1)}, u32[]{:S(2)}, u32[]{:S(2)}) collective-permute-start(bf16[32,1024]{1,0:T(8,128)(2,1)S(1)} %get-tuple-element.87), channel_id=1, source_target_pairs={{256,128},{288,160},{320,192},{352,224},{257,129},{289,161},{321,1... | collective-permute-start | bytes 196616 | tf_op jit(solution)/shard_map/ppermute | solution.py:407
  106.2 21.5 %collective-permute-start.7 = (bf16[32,1024]{1,0:T(8,128)(2,1)S(1)}, bf16[32,1024]{1,0:T(8,128)(2,1)S(1)}, u32[]{:S(2)}, u32[]{:S(2)}) collective-permute-start(bf16[32,1024]{1,0:T(8,128)(2,1)S(1)} %get-tuple-element.86), channel_id=1, source_target_pairs={{128,0},{160,32},{192,64},{224,96},{129,1},{161,33},{193,65},{225,... | collective-permute-start | bytes 196616 | tf_op jit(solution)/shard_map/ppermute | solution.py:398
  108.9 0.6 copy-start.10
  133.0 1.5 copy-start.2
  134.4 0.7 copy-start.8
  135.1 3.8 %collective-permute-start.9 = (bf16[16,32,512]{2,1,0:T(8,128)(2,1)S(1)}, bf16[16,32,512]{2,1,0:T(8,128)(2,1)S(1)}, u32[]{:S(2)}, u32[]{:S(2)}) collective-permute-start(bf16[16,32,512]{2,1,0:T(8,128)(2,1)S(1)} %get-tuple-element.97), channel_id=1, source_target_pairs={{0,1},{1,0},{2,3},{3,2},{4,5},{5,4},{6,7},{7,6},{8,9},{9,8},{10,11... | collective-permute-start | bytes 1572872 | tf_op jit(solution)/shard_map/ppermute | solution.py:306
  139.9 20.8 %all-to-all-start.1 = ((bf16[16,32,512]{2,1,0:T(8,128)(2,1)}), bf16[16,32,512]{2,1,0:T(8,128)(2,1)}, u32[]{:S(2)}, u32[]{:S(2)}) async-start(bf16[16,32,512]{2,1,0:T(8,128)(2,1)} %add_convert_fusion), calls=%async_computation.1 | async-start | bytes 1048576 | tf_op jit(solution)/shard_map/all_to_all | solution.py:309
  144.9 7.6 %collective-permute-start.10 = (bf16[32,1024]{1,0:T(8,128)(2,1)}, bf16[32,1024]{1,0:T(8,128)(2,1)S(1)}, u32[]{:S(2)}, u32[]{:S(2)}) collective-permute-start(bf16[32,1024]{1,0:T(8,128)(2,1)} %copy-done.10), channel_id=1, source_target_pairs={{128,0},{160,32},{192,64},{224,96},{129,1},{161,33},{193,65},{225,... | collective-permute-start | bytes 196616 | tf_op jit(solution)/shard_map/ppermute | solution.py:407
  146.2 1.0 copy-start
  147.2 0.9 copy-start.1
  148.1 0.9 copy-start.6
  149.1 0.9 copy-start.9
  150.0 2.5 %copy-start.3 = (bf16[128,1536]{1,0:T(8,128)(2,1)S(1)}, bf16[128,1536]{1,0:T(8,128)(2,1)}, u32[]{:S(2)}) copy-start(bf16[128,1536]{1,0:T(8,128)(2,1)} %copy-done.2) | copy-start | bytes 1179652

commit v6 on v5

--- a/solution.py
+++ b/solution.py
@@ -98,61 +98,60 @@
 
 def token_kernel(
     place, mem_hbm, tok_hbm, gout_hbm, gain_hbm, own_hbm, other_hbm,
-    normed_out, qg_out, part_out, kvp_out, wt_out, w, wo, mem, tok, gout, gain, sems
+    normed_out, qg_out, part_out, kvp_out, w_out, wo_out, mem, tok, gout, gain, sems
 ):
     core = place[1]
-    across, along, rows, _ = own_hbm.shape
-    pieces, later = [], []
+    near = [(mem_hbm, mem), (tok_hbm, tok), (gain_hbm, gain)]
+    first, second = [], []
     inner, outer = slice(0, D + 2 * KV), slice(D + 2 * KV, 2 * D + 2 * KV)
-    for source, side in ((own_hbm, core), (other_hbm, 1 - core)):
-        for i in range(across):
-            for j in range(along):
-                start = pl.multiple_of((j * across + i) * 2 * rows + side * rows, rows)
-                pieces.append((source.at[i, j, :, inner], w.at[pl.ds(start, rows), :]))
-                later.append((source.at[i, j, :, outer], wo.at[pl.ds(start, rows), :]))
-    pairs = [(mem_hbm, mem), (tok_hbm, tok), (gain_hbm, gain)] + pieces + [(gout_hbm, gout)] + later
-    copies = loads(pairs, sems)
+    for i in range(own_hbm.shape[0]):
+        for source, side in ((own_hbm, core), (other_hbm, 1 - core)):
+            first.append((source.at[i, :, :, inner], w_out.at[:, i, side]))
+            second.append((source.at[i, :, :, outer], wo_out.at[:, i, side]))
+    copies = loads(near + first + [(gout_hbm, gout)] + second, sems)
     for copy in copies[:3]:
         copy.wait()
     hidden = jnp.concatenate([mem[...].astype(F32), tok[...].astype(F32)], axis=0)
     _, normed = normalised(hidden, gain[...])
     normed_out[...] = normed
-    for copy in copies[3 : 3 + len(pieces)]:
+    for copy in copies[3 : 3 + len(first)]:
         copy.wait()
+    w = w_out[...].reshape(D, D + 2 * KV)
     q = nn(normed[MEM:], w[:, :D])
-    kv = nn(normed, w[:, D : D + 2 * KV]).astype(BF)
-    for copy in copies[3 + len(pieces) :]:
+    kv = nn(normed, w[:, D:]).astype(BF)
+    for copy in copies[3 + len(first) :]:
         copy.wait()
-    up = nn(gout[...], wo[...])
+    up = nn(gout[...], wo_out[...].reshape(D, D))
     k, v = kv[:, :KV], kv[:, KV:]
     key_at = lax.broadcasted_iota(jnp.int32, (ROWS, PER_GROUP * TOK), 0)
     row_at = lax.broadcasted_iota(jnp.int32, (ROWS, PER_GROUP * TOK), 1) % TOK
     seen = key_at <= row_at + MEM
     key_parts, value_parts = [], []
-    for g in range(GROUPS):
-        cols = group_columns(g)
-        zq = stacked(q[:, cols])
-        zu = stacked(up[:, cols])
-        krep, vrep = repeated(k, g), repeated(v, g)
-        raised = jnp.where(seen, jnp.exp(nt(krep, zq) * SCALE), 0.0)
-        probs = raised * (1.0 / jnp.sum(raised, axis=0, keepdims=True))
-        score_grad = centred(0, probs, probs * nt(vrep, zu))
-        key_parts.append(nn(score_grad, zq))
-        value_parts.append(nn(probs.astype(BF), zu))
-        qg_out[:, cols] = unstacked(tn(score_grad, krep)).astype(BF)
+    for pair in ((0, 1), (2, 3)):
+        zqs = [stacked(q[:, group_columns(g)]) for g in pair]
+        zus = [stacked(up[:, group_columns(g)]) for g in pair]
+        kreps, vreps = [repeated(k, g) for g in pair], [repeated(v, g) for g in pair]
+        raised = [jnp.where(seen, jnp.exp(nt(krep, zq) * SCALE), 0.0) for krep, zq in zip(kreps, zqs)]
+        products = [nt(vrep, zu) for vrep, zu in zip(vreps, zus)]
+        probs = [r * (1.0 / jnp.sum(r, axis=0, keepdims=True)) for r in raised]
+        score_grads = [centred(0, p, p * product) for p, product in zip(probs, products)]
+        value_parts += [nn(p.astype(BF), zu) for p, zu in zip(probs, zus)]
+        key_parts += [nn(grad, zq) for grad, zq in zip(score_grads, zqs)]
+        for g, grad, krep in zip(pair, score_grads, kreps):
+            qg_out[:, group_columns(g)] = unstacked(tn(grad, krep)).astype(BF)
     part = jnp.concatenate([folded(key_parts), folded(value_parts)], axis=1)
     part_out[...] = part
     kvp_out[:MEM, :] = part[:MEM].astype(BF)
     kvp_out[MEM:ROWS, :] = kv[MEM:]
     kvp_out[ROWS : ROWS + MEM, :] = mem[:, : D // 2]
     kvp_out[ROWS + MEM :, :] = mem[:, D // 2 :]
-    wt_out[...] = w[...].T
-
-
-def mix_kernel(last_hbm, gain_hbm, wo, wt, mixed_out, u_out, last, gain, sems):
+
+
+def mix_kernel(last_hbm, gain_hbm, w, wo, wt, mixed_out, u_out, last, gain, sems):
     for copy in loads([(last_hbm, last), (gain_hbm, gain)], sems):
         copy.wait()
     u_out[...] = nn(last[...], wo[...]).astype(BF)
+    wt[...] = w[...].T
     scaled = (wt[...].astype(F32) * gain[...]).astype(BF)
     mixed_out[...] = nn(scaled, wo[...]).astype(BF)
 
@@ -231,10 +230,16 @@
     kv_grad = kv_grad.astype(BF)
     kv_out[...] = kv_grad
     grad = tn(normed[...], kv_grad)
-    grad = grad.reshape(mine_out.shape[0], 2, mine_out.shape[1], 2 * KV)
+    pieces, depth, _ = mine_out.shape
+    share = 8 * pieces
     first = place[1] == 0
-    mine_out[...] = jnp.where(first, grad[:, 0], grad[:, 1]).astype(BF)
-    other_out[...] = jnp.where(first, grad[:, 1], grad[:, 0]).astype(BF)
+    for piece in range(pieces):
+        halves = [
+            jnp.concatenate([grad[at : at + 8] for at in range(core * share + piece * 8, D, 2 * share)], axis=0)
+            for core in range(2)
+        ]
+        mine_out[piece] = jnp.where(first, halves[0], halves[1]).astype(BF)
+        other_out[piece] = jnp.where(first, halves[1], halves[0]).astype(BF)
 
 
 def memory_kernel(turn, place, arrived, held, grads4, wt, mem4, inv4, gain, *outs):
@@ -301,19 +306,27 @@
     return own, lax.ppermute(own, "dp", [(i, i ^ 1) for i in range(docs)])
 
 
-def summed_over_documents(mine, other):
+def summed_over_group(mine, other):
     docs = lax.axis_size("dp")
     got = lax.ppermute(other, "dp", [(i, i ^ 1) for i in range(docs)])
     block = (mine.astype(F32) + got.astype(F32)).astype(BF)
-    if docs > 2:
-        block = lax.all_to_all(block, "dp", 0, 0, tiled=True, axis_index_groups=runs(docs, docs // 2, 2))
+    block = lax.all_to_all(block, "seg", 0, 0, tiled=True, axis_index_groups=runs(lax.axis_size("seg"), SPAN, 1))
+    return jnp.sum(block.astype(F32), axis=0).astype(BF)
+
+
+def summed_over_documents(block):
+    docs = lax.axis_size("dp")
+    chunks = docs // 2
+    block = block.reshape(chunks, 8, 2 * KV)
+    block = lax.all_to_all(block, "dp", 0, 0, tiled=True, axis_index_groups=runs(docs, chunks, 2))
     return jnp.sum(block.astype(F32), axis=0).astype(BF)
 
 
 def summed_over_segments(block):
     n_seg = lax.axis_size("seg")
     copies = jnp.broadcast_to(block[None], (n_seg,) + block.shape)
-    return jnp.sum(lax.all_to_all(copies, "seg", 0, 0, tiled=True).astype(F32), axis=0)
+    got = lax.all_to_all(copies, "seg", 0, 0, tiled=True).reshape(n_seg // SPAN, SPAN, 8, 2 * KV)
+    return jnp.sum(got.astype(F32), axis=0).reshape(SPAN * 8, 2 * KV)
 
 
 def body(tokens, grad_output, memories, grad_last, norm_gain, query_weight, key_weight, value_weight, out_weight):
@@ -325,22 +338,21 @@
     block = position // SPAN
     place = jnp.stack([position % SPAN, lax.axis_index("dp") % 2, turns - 1 - block]).astype(jnp.int32)
 
-    near_w, far_w = gathered(jnp.concatenate([query_weight, key_weight, value_weight, out_weight.T], axis=1))
-    near_w, far_w, place = lax.optimization_barrier((near_w, far_w, place))
+    weights = gathered(jnp.concatenate([query_weight, key_weight, value_weight, out_weight.T], axis=1))
+    *weights, place = lax.optimization_barrier((*weights, place))
 
     dma = pltpu.SemaphoreType.DMA
-    normed, qg, part, kvp, wt, w, wo = call(
+    normed, qg, part, kvp, w, wo = call(
         token_kernel,
         [
             shape((ROWS, D)),
             shape((TOK, D)),
             shape((ROWS, 2 * KV), F32),
             shape((ROWS + 2 * MEM, 2 * KV)),
-            shape((D + 2 * KV, D)),
-            shape((D, D + 2 * KV)),
-            shape((D, D)),
+            shape((docs // 8, 4, 2, D // docs, D + 2 * KV)),
+            shape((docs // 8, 4, 2, D // docs, D)),
         ],
-        (place, mem, tok, gout, gain, near_w, far_w),
+        (place, mem, tok, gout, gain, *weights),
         1_500_000_000,
         scalars=1,
         far=6,
@@ -349,17 +361,18 @@
             pltpu.VMEM((TOK, D), BF),
             pltpu.VMEM((TOK, D), BF),
             pltpu.VMEM((1, D), F32),
-            dma((4 + 2 * docs,)),
+            dma((4 + 16,)),
         ),
     )
+    w, wo = w.reshape(D, D + 2 * KV), wo.reshape(D, D)
     kvps = [kvp]
     for ahead in range(1, SPAN):
         route = [(i, i // SPAN * SPAN + (i - ahead) % SPAN) for i in range(n_seg)]
         kvps.append(lax.ppermute(kvp, "seg", route))
-    mixed, arrived = call(
+    wt, mixed, arrived = call(
         mix_kernel,
-        [shape((D + 2 * KV, D)), shape((MEM, D))],
-        (last, gain, wo, wt),
+        [shape((D + 2 * KV, D)), shape((D + 2 * KV, D)), shape((MEM, D))],
+        (last, gain, w, wo),
         4_000_000_000,
         far=2,
         scratch=(pltpu.VMEM((MEM, D), BF), pltpu.VMEM((1, D), F32), dma((2,))),
@@ -405,7 +418,7 @@
             )
             arrived, memory_send = lax.optimization_barrier((arrived, memory_send))
             memory_arrived = lax.ppermute(memory_send, "seg", route)
-    half = (docs // 2, D // docs, 2 * KV)
+    half = (SPAN, docs // 2 * 8, 2 * KV)
     kv_grad, mine, other = call(
         weight_kernel,
         [shape((ROWS, 2 * KV)), shape(half), shape(half)],
@@ -421,7 +434,8 @@
         scalars=1,
     )
     (grad_tokens,) = call(rows_kernel, [shape((TOK, D))], (tok, gout, gain, wt, qg, kv_grad), 500_000_000)
-    block = summed_over_documents(mine, other)
+    block = summed_over_group(mine, other)
+    block = summed_over_documents(block)
     block, grad_tokens, grad_memories = lax.optimization_barrier((block, grad_tokens, grad_memories))
     total = summed_over_segments(block) / docs
     return (grad_tokens[None], grad_memories[None, None], total[:, :KV], total[:, KV:])

time: 189 us -> 185 us (0.979)
  waiting for transfers between devices: 32.6 us -> 27.3 us
  blocking collectives: 78.5 us -> 80.6 us
    all_to_all x1, waiting for transfers between devices: 6.23 us -> 0.53 us  [summed_over_documents(): lax.all_to_all(block, 'dp', 0, 0, tiled=True, axis_index_groups=runs(docs...]
    all_to_all x1 -> x2, blocking collectives: 26 us -> 28.1 us  [the longest x1 14.3 us: summed_over_segments(): lax.all_to_all(copies, 'seg', 0, 0, tiled=True)]
  transfers between devices with their start and end apart: 12 -> 12, of which waited for: 6 -> 6; matrix products, arithmetic and copies ran while one was open for 0% -> 0% of each run, Pallas kernels for 11% -> 12%
where the time goes in v6:
time: 185 us; the launch traced here: 184 us
  blocking collectives  80.6 us (44%)
  Pallas kernels  40.7 us (22%)
  waiting for transfers between devices  27.3 us (15%)
  starting transfers between devices  25.5 us (14%)
  local copies, waits for them, and re-layouts  5.3 us (3%)
  other arithmetic  3.9 us (2%)
    pallas_call x13, Pallas kernels, call(): pl.pallas_call(kernel, out_shape=outs, in_specs=[smem] * scalars + [hbm]...  40.7 us
    all_to_all x1, blocking collectives, gathered(): lax.all_to_all(copies, 'dp', 0, 0, tiled=True, axis_index_groups=runs(doc...  31.8 us
    all_gather x1, blocking collectives, gathered(): lax.all_gather(shard, 'dp', axis=0, axis_index_groups=runs(docs, docs //...  20.6 us
    ppermute x3, waiting for transfers between devices, body(): arrived = lax.ppermute(send, 'seg', route)  18.2 us
    all_to_all x1, blocking collectives, summed_over_segments(): lax.all_to_all(copies, 'seg', 0, 0, tiled=True)  14.3 us
    all_to_all x1, blocking collectives, summed_over_group(): lax.all_to_all(block, 'seg', 0, 0, tiled=True, axis_index_groups=runs(lax...  13.9 us
    ppermute x3, starting transfers between devices, body(): kvps.append(lax.ppermute(kvp, 'seg', route))  11.2 us
    all_to_all x1, starting transfers between devices, summed_over_documents(): lax.all_to_all(block, 'dp', 0, 0, tiled=True, axis_index_groups=runs(docs...  5.06 us
  transfers between devices with their start and end apart: 12, of which 6 were waited for; matrix products, arithmetic and copies ran while one was open for 0% of the time, Pallas kernels for 12%

profile of v6, /device:TPU:8, one launch (start us, length us, event | category | flops | bytes accessed | tf_op | source)
XLA Modules:
  0.0 184.4 jit_solution(14877317493611671082)
XLA Ops:
  0.6 0.9 pad_maximum_fusion
  1.6 20.6 %all-gather = bf16[128,2560]{1,0:T(8,128)(2,1)S(1)} all-gather(bf16[32,2560]{1,0:T(8,128)(2,1)S(1)} %pad_maximum_fusion), channel_id=2, replica_groups={{0,8,16,24},{1,9,17,25},{2,10,18,26},{3,11,19,27},{4,12,20,28},{5,13,21..., dimensions={0}, use_global_device_ids=true | all-gather | bytes 819200 | tf_op jit(solution)/shard_map/all_gather | solution.py:303
  22.2 0.2 broadcast_in_dim.10
  22.5 31.8 %all_to_all.20.own_hbm = bf16[4,4,32,2560]{3,2,1,0:T(8,128)(2,1)S(1)} all-to-all(bf16[4,4,32,2560]{3,2,1,0:T(8,128)(2,1)S(1)} %broadcast_in_dim.10), channel_id=1, replica_groups={{0,2,4,6},{1,3,5,7},{8,10,12,14},{9,11,13,15},{16,18,20,22},{17,19,21,2..., dimensions={0} | all-to-all | bytes 5242880 | tf_op jit(solution)/shard_map/all_to_all | solution.py:305
  54.3 1.9 %collective-permute-start = (bf16[4,4,32,2560]{3,2,1,0:T(8,128)(2,1)S(1)}, bf16[4,4,32,2560]{3,2,1,0:T(8,128)(2,1)}, u32[]{:S(2)}, u32[]{:S(2)}) collective-permute-start(bf16[4,4,32,2560]{3,2,1,0:T(8,128)(2,1)S(1)} %all_to_all.20.own_hbm), channel_id=1, source_target_pairs={{0,1},{1,0},{2,3},{3,2},{4,5},{5,4},{6,7},{7,6},{8,9},{9,8},{10,11... | collective-permute-start | bytes 7864328 | tf_op jit(solution)/shard_map/ppermute | solution.py:306
  56.2 0.1 pad_add_fusion.place
  56.3 4.9 %collective-permute-done.other_hbm = bf16[4,4,32,2560]{3,2,1,0:T(8,128)(2,1)} collective-permute-done((bf16[4,4,32,2560]{3,2,1,0:T(8,128)(2,1)S(1)}, bf16[4,4,32,2560]{3,2,1,0:T(8,128)(2,1)}, u32[]{:S(2)}, u32[]{:S(2)}) %collective-permute-start) | collective-permute-done | bytes 2621472 | tf_op jit(solution)/shard_map/ppermute | solution.py:306
  61.2 5.3 %shard_map.120 = (bf16[160,1024]{1,0:T(8,128)(2,1)S(1)}, bf16[128,1024]{1,0:T(8,128)(2,1)S(1)}, f32[160,512]{1,0:T(8,128)S(1)}, bf16[224,512]{1,0:T(8,128)(2,1)S...) custom-call(s32[3]{0:T(128)S(1)} %pad_add_fusion.place, ...), custom_call_target="tpu_custom_call" | custom-call | flops 1500000000 | bytes 12226572 | tf_op jit(solution)/shard_map/pallas_call | solution.py:279
  66.5 0.0 copy-start.5
  66.5 2.2 %collective-permute-start.1 = (bf16[224,512]{1,0:T(8,128)(2,1)S(1)}, bf16[224,512]{1,0:T(8,128)(2,1)S(1)}, u32[]{:S(2)}, u32[]{:S(2)}) collective-permute-start(bf16[224,512]{1,0:T(8,128)(2,1)S(1)} %get-tuple-element.62.refs_0_), channel_id=1, source_target_pairs={{0,96},{32,0},{64,32},{96,64},{128,224},{160,128},{192,160},{224,1... | collective-permute-start | bytes 688136 | tf_op jit(solution)/shard_map/ppermute | solution.py:371
  68.7 4.3 %collective-permute-start.2 = (bf16[224,512]{1,0:T(8,128)(2,1)S(1)}, bf16[224,512]{1,0:T(8,128)(2,1)S(1)}, u32[]{:S(2)}, u32[]{:S(2)}) collective-permute-start(bf16[224,512]{1,0:T(8,128)(2,1)S(1)} %get-tuple-element.62.refs_0_), channel_id=1, source_target_pairs={{0,64},{32,96},{64,0},{96,32},{128,192},{160,224},{192,128},{224,1... | collective-permute-start | bytes 688136 | tf_op jit(solution)/shard_map/ppermute | solution.py:371
  73.0 4.7 %collective-permute-start.3 = (bf16[224,512]{1,0:T(8,128)(2,1)S(1)}, bf16[224,512]{1,0:T(8,128)(2,1)S(1)}, u32[]{:S(2)}, u32[]{:S(2)}) collective-permute-start(bf16[224,512]{1,0:T(8,128)(2,1)S(1)} %get-tuple-element.62.refs_0_), channel_id=1, source_target_pairs={{0,32},{32,64},{64,96},{96,0},{128,160},{160,192},{192,224},{224,1... | collective-permute-start | bytes 688136 | tf_op jit(solution)/shard_map/ppermute | solution.py:371
  77.7 4.7 %shard_map.121 = (bf16[1536,1024]{1,0:T(8,128)(2,1)S(1)}, bf16[1536,1024]{1,0:T(8,128)(2,1)S(1)}, bf16[32,1024]{1,0:T(8,128)(2,1)S(1)}) custom-call(bf16[32,1024]{1,0:T(8,128)(2,1)} %bitcast.27, f32[1,1024]{1,0:T(1,128)} %bitcast.31, bf16[1024,1536]{1,0:T(8,128)(2,1)S(1)} %bitcast.19, bf16[1024,1024]{1,0:T(8,128)(2,1)S(1)} %bitcast.21), custom_call_target="tpu_custom_call" | custom-call | flops 4000000000 | bytes 11669504 | tf_op jit(solution)/shard_map/pallas_call | solution.py:279
  82.5 0.3 collective-permute-done.3.refs_3_
  82.8 3.0 %shard_map.122 = (f32[16,160,128]{2,1,0:T(8,128)S(1)}, f32[16,128,160]{2,1,0:T(8,128)S(1)}, bf16[16,160,256]{2,1,0:T(8,128)(2,1)S(1)}, bf16[16,160,256]{2,1,0:T(...) custom-call(s32[3]{0:T(128)S(1)} %pad_add_fusion.place, ...), custom_call_target="tpu_custom_call" | custom-call | flops 400000000 | bytes 14291468 | tf_op jit(solution)/shard_map/pallas_call | solution.py:279
  85.8 4.6 %shard_map.123 = (bf16[32,1024]{1,0:T(8,128)(2,1)S(1)}, bf16[128,1024]{1,0:T(8,128)(2,1)S(1)}, bf16[128,1536]{1,0:T(8,128)(2,1)S(1)}) custom-call(s32[3]{0:T(128)S(1)} %pad_add_fusion.place, bf16[32,1024]{1,0:T(8,128)(2,1)S(1)} %get-tuple-element.60.arrived.before, bf16[32,1024]{1,0:T(8,128)(2,1)S(1)} %get-tuple-element.60.arrived.before, ...), custom_call_target="tpu_custom_call" | custom-call | flops 1000000000 | bytes 11862540 | tf_op jit(solution)/shard_map/pallas_call | solution.py:279
  90.3 0.7 collective-permute-start.4
  91.0 1.3 shard_map.124
  92.4 0.9 collective-permute-start.6
  93.3 4.6 %shard_map.125 = (bf16[32,1024]{1,0:T(8,128)(2,1)S(1)}, bf16[128,1024]{1,0:T(8,128)(2,1)S(1)}, bf16[128,1536]{1,0:T(8,128)(2,1)S(1)}) custom-call(s32[3]{0:T(128)S(1)} %pad_add_fusion.place, bf16[32,1024]{1,0:T(8,128)(2,1)S(1)} %collective-permute-done.4.arrived, bf16[128,1024]{1,0:T(8,128)(2,1)S(1)} %get-tuple-element.78.before, ...), custom_call_target="tpu_custom_call" | custom-call | flops 1000000000 | bytes 12059148 | tf_op jit(solution)/shard_map/pallas_call | solution.py:279
  97.8 0.7 collective-permute-start.5
  98.5 1.3 shard_map.126
  99.9 0.7 collective-permute-start.8
  100.5 4.6 %shard_map.127 = (bf16[32,1024]{1,0:T(8,128)(2,1)S(1)}, bf16[128,1024]{1,0:T(8,128)(2,1)S(1)}, bf16[128,1536]{1,0:T(8,128)(2,1)S(1)}) custom-call(s32[3]{0:T(128)S(1)} %pad_add_fusion.place, bf16[32,1024]{1,0:T(8,128)(2,1)S(1)} %collective-permute-done.5.arrived, bf16[128,1024]{1,0:T(8,128)(2,1)S(1)} %get-tuple-element.85.before, ...), custom_call_target="tpu_custom_call" | custom-call | flops 1000000000 | bytes 12059148 | tf_op jit(solution)/shard_map/pallas_call | solution.py:279
  105.1 1.3 collective-permute-start.7
  106.4 1.3 shard_map.128
  107.8 0.6 copy-done.10
  108.4 18.2 %collective-permute-done.7.arrived = bf16[32,1024]{1,0:T(8,128)(2,1)S(1)} collective-permute-done((bf16[32,1024]{1,0:T(8,128)(2,1)S(1)}, bf16[32,1024]{1,0:T(8,128)(2,1)S(1)}, u32[]{:S(2)}, u32[]{:S(2)}) %collective-permute-start.7) | collective-permute-done | bytes 65568 | tf_op jit(solution)/shard_map/ppermute | solution.py:411
  126.6 5.2 %shard_map.129 = (bf16[32,1024]{1,0:T(8,128)(2,1)}, bf16[128,1024]{1,0:T(8,128)(2,1)S(1)}, bf16[128,1536]{1,0:T(8,128)(2,1)S(1)}) custom-call(s32[3]{0:T(128)S(1)} %pad_add_fusion.place, bf16[32,1024]{1,0:T(8,128)(2,1)S(1)} %collective-permute-done.7.arrived, bf16[128,1024]{1,0:T(8,128)(2,1)S(1)} %get-tuple-element.92.before, ...), custom_call_target="tpu_custom_call" | custom-call | flops 1000000000 | bytes 12059148 | tf_op jit(solution)/shard_map/pallas_call | solution.py:279
  131.8 1.5 shard_map.130
  133.3 1.9 %collective-permute-start.9 = (bf16[4,128,512]{2,1,0:T(8,128)(2,1)S(1)}, bf16[4,128,512]{2,1,0:T(8,128)(2,1)S(1)}, u32[]{:S(2)}, u32[]{:S(2)}) collective-permute-start(bf16[4,128,512]{2,1,0:T(8,128)(2,1)S(1)} %get-tuple-element.97), channel_id=1, source_target_pairs={{0,1},{1,0},{2,3},{3,2},{4,5},{5,4},{6,7},{7,6},{8,9},{9,8},{10,11... | collective-permute-start | bytes 1572872 | tf_op jit(solution)/shard_map/ppermute | solution.py:311
  135.2 1.9 %collective-permute-done.9 = bf16[4,128,512]{2,1,0:T(8,128)(2,1)S(1)} collective-permute-done((bf16[4,128,512]{2,1,0:T(8,128)(2,1)S(1)}, bf16[4,128,512]{2,1,0:T(8,128)(2,1)S(1)}, u32[]{:S(2)}, u32[]{:S(2)}) %collective-permute-start.9) | collective-permute-done | bytes 524320 | tf_op jit(solution)/shard_map/ppermute | solution.py:311
  137.1 0.1 add_convert_fusion
  137.3 13.9 %all_to_all.21 = bf16[4,128,512]{2,1,0:T(8,128)(2,1)} all-to-all(bf16[4,128,512]{2,1,0:T(8,128)(2,1)S(1)} %add_convert_fusion), channel_id=1, replica_groups={{0,32,64,96},{128,160,192,224},{256,288,320,352},{384,416,448,480},{1,3..., dimensions={0} | all-to-all | bytes 1048576 | tf_op jit(solution)/shard_map/all_to_all | solution.py:313
  151.2 1.8 reduce_sum.33
  153.0 5.1 %all-to-all-start.2 = ((bf16[16,8,512]{2,1,0:T(8,128)(2,1)}), bf16[16,8,512]{2,1,0:T(8,128)(2,1)}, u32[]{:S(2)}, u32[]{:S(2)}) async-start(bf16[16,8,512]{2,1,0:T(8,128)(2,1)} %bitcast.40), calls=%async_computation.2 | async-start | bytes 262144 | tf_op jit(solution)/shard_map/all_to_all | solution.py:321
  158.0 1.3 collective-permute-start.10
  159.3 0.9 copy-done
  160.3 0.9 copy-done.1
  161.2 0.9 copy-done.6
  162.2 0.9 copy-done.9
  163.1 1.4 shard_map.131
  164.6 1.4 collective-permute-done.10.arrived
  166.0 2.0 %shard_map.132 = bf16[32,1024]{1,0:T(8,128)(2,1)} custom-call(s32[3]{0:T(128)S(1)} %pad_add_fusion.place, bf16[32,1024]{1,0:T(8,128)(2,1)S(1)} %collective-permute-done.10.arrived, bf16[32,1024]{1,0:T(8,128)(2,1)S(1)} %get-tuple-element.101.held, bf16[128,1536]{1,0:T(8,128)(2,1)S(1)} %copy-done.3, bf16[1536,1024]{1,0:T(8,128)(2,1)S(1)} %get-tuple-element.74.wt, ...), custom_call_target="tpu_custom_call" | custom-call | flops 400000000 | bytes 4002316 | tf_op jit(solution)/shard_map/pallas_call | solution.py:279
  168.0 0.5 all-to-all-done.2
  168.5 0.9 reduce_sum.34
  169.5 14.3 %all_to_all.22 = bf16[16,8,512]{2,1,0:T(8,128)(2,1)S(1)} all-to-all(bf16[16,8,512]{2,1,0:T(8,128)(2,1)S(1)} %broadcast_in_dim.25), channel_id=1, replica_groups=mesh['seg'=16,'dp'=32] {'seg'}, dimensions={0} | all-to-all | bytes 262144 | tf_op jit(solution)/shard_map/all_to_all | solution.py:328
  183.8 0.6 fusion
  (27 shorter events, 0.1 us)
Async XLA Ops:
  54.3 6.9 %copy-start.11 = (bf16[4,4,32,2560]{3,2,1,0:T(8,128)(2,1)}, bf16[4,4,32,2560]{3,2,1,0:T(8,128)(2,1)S(1)}, u32[]{:S(2)}) copy-start(bf16[4,4,32,2560]{3,2,1,0:T(8,128)(2,1)S(1)} %all_to_all.20.own_hbm) | copy-start | bytes 7864324
  54.3 6.9 %collective-permute-start = (bf16[4,4,32,2560]{3,2,1,0:T(8,128)(2,1)S(1)}, bf16[4,4,32,2560]{3,2,1,0:T(8,128)(2,1)}, u32[]{:S(2)}, u32[]{:S(2)}) collective-permute-start(bf16[4,4,32,2560]{3,2,1,0:T(8,128)(2,1)S(1)} %all_to_all.20.own_hbm), channel_id=1, source_target_pairs={{0,1},{1,0},{2,3},{3,2},{4,5},{5,4},{6,7},{7,6},{8,9},{9,8},{10,11... | collective-permute-start | bytes 7864328 | tf_op jit(solution)/shard_map/ppermute | solution.py:306
  66.5 16.0 %copy-start.5 = (bf16[128,1024]{1,0:T(8,128)(2,1)}, bf16[128,1024]{1,0:T(8,128)(2,1)S(1)}, u32[]{:S(2)}) copy-start(bf16[128,1024]{1,0:T(8,128)(2,1)S(1)} %get-tuple-element.98.qg) | copy-start | bytes 786436
  66.5 16.0 %collective-permute-start.1 = (bf16[224,512]{1,0:T(8,128)(2,1)S(1)}, bf16[224,512]{1,0:T(8,128)(2,1)S(1)}, u32[]{:S(2)}, u32[]{:S(2)}) collective-permute-start(bf16[224,512]{1,0:T(8,128)(2,1)S(1)} %get-tuple-element.62.refs_0_), channel_id=1, source_target_pairs={{0,96},{32,0},{64,32},{96,64},{128,224},{160,128},{192,160},{224,1... | collective-permute-start | bytes 688136 | tf_op jit(solution)/shard_map/ppermute | solution.py:371
  68.7 13.8 %collective-permute-start.2 = (bf16[224,512]{1,0:T(8,128)(2,1)S(1)}, bf16[224,512]{1,0:T(8,128)(2,1)S(1)}, u32[]{:S(2)}, u32[]{:S(2)}) collective-permute-start(bf16[224,512]{1,0:T(8,128)(2,1)S(1)} %get-tuple-element.62.refs_0_), channel_id=1, source_target_pairs={{0,64},{32,96},{64,0},{96,32},{128,192},{160,224},{192,128},{224,1... | collective-permute-start | bytes 688136 | tf_op jit(solution)/shard_map/ppermute | solution.py:371
  73.0 9.8 %collective-permute-start.3 = (bf16[224,512]{1,0:T(8,128)(2,1)S(1)}, bf16[224,512]{1,0:T(8,128)(2,1)S(1)}, u32[]{:S(2)}, u32[]{:S(2)}) collective-permute-start(bf16[224,512]{1,0:T(8,128)(2,1)S(1)} %get-tuple-element.62.refs_0_), channel_id=1, source_target_pairs={{0,32},{32,64},{64,96},{96,0},{128,160},{160,192},{192,224},{224,1... | collective-permute-start | bytes 688136 | tf_op jit(solution)/shard_map/ppermute | solution.py:371
  77.7 5.1 %copy-start.7 = (f32[1024]{0:T(1024)S(1)}, f32[1024]{0:T(1024)}, u32[]{:S(2)}) copy-start(f32[1024]{0:T(1024)} %param.13) | copy-start | bytes 12292
  85.7 5.2 %copy-start.4 = (bf16[1,32,1024]{2,1,0:T(8,128)(2,1)S(1)}, bf16[1,32,1024]{2,1,0:T(8,128)(2,1)}, u32[]{:S(2)}) copy-start(bf16[1,32,1024]{2,1,0:T(8,128)(2,1)} %param.12) | copy-start | bytes 196612
  90.3 2.0 %collective-permute-start.4 = (bf16[32,1024]{1,0:T(8,128)(2,1)S(1)}, bf16[32,1024]{1,0:T(8,128)(2,1)S(1)}, u32[]{:S(2)}, u32[]{:S(2)}) collective-permute-start(bf16[32,1024]{1,0:T(8,128)(2,1)S(1)} %get-tuple-element.72), channel_id=1, source_target_pairs={{384,256},{416,288},{448,320},{480,352},{385,257},{417,289},{449,3... | collective-permute-start | bytes 196616 | tf_op jit(solution)/shard_map/ppermute | solution.py:411
  92.4 6.1 %collective-permute-start.6 = (bf16[32,1024]{1,0:T(8,128)(2,1)S(1)}, bf16[32,1024]{1,0:T(8,128)(2,1)S(1)}, u32[]{:S(2)}, u32[]{:S(2)}) collective-permute-start(bf16[32,1024]{1,0:T(8,128)(2,1)S(1)} %get-tuple-element.80), channel_id=1, source_target_pairs={{384,256},{416,288},{448,320},{480,352},{385,257},{417,289},{449,3... | collective-permute-start | bytes 196616 | tf_op jit(solution)/shard_map/ppermute | solution.py:420
  97.8 2.0 %collective-permute-start.5 = (bf16[32,1024]{1,0:T(8,128)(2,1)S(1)}, bf16[32,1024]{1,0:T(8,128)(2,1)S(1)}, u32[]{:S(2)}, u32[]{:S(2)}) collective-permute-start(bf16[32,1024]{1,0:T(8,128)(2,1)S(1)} %get-tuple-element.79), channel_id=1, source_target_pairs={{256,128},{288,160},{320,192},{352,224},{257,129},{289,161},{321,1... | collective-permute-start | bytes 196616 | tf_op jit(solution)/shard_map/ppermute | solution.py:411
  99.9 6.5 %collective-permute-start.8 = (bf16[32,1024]{1,0:T(8,128)(2,1)S(1)}, bf16[32,1024]{1,0:T(8,128)(2,1)S(1)}, u32[]{:S(2)}, u32[]{:S(2)}) collective-permute-start(bf16[32,1024]{1,0:T(8,128)(2,1)S(1)} %get-tuple-element.87), channel_id=1, source_target_pairs={{256,128},{288,160},{320,192},{352,224},{257,129},{289,161},{321,1... | collective-permute-start | bytes 196616 | tf_op jit(solution)/shard_map/ppermute | solution.py:420
  105.1 21.5 %collective-permute-start.7 = (bf16[32,1024]{1,0:T(8,128)(2,1)S(1)}, bf16[32,1024]{1,0:T(8,128)(2,1)S(1)}, u32[]{:S(2)}, u32[]{:S(2)}) collective-permute-start(bf16[32,1024]{1,0:T(8,128)(2,1)S(1)} %get-tuple-element.86), channel_id=1, source_target_pairs={{128,0},{160,32},{192,64},{224,96},{129,1},{161,33},{193,65},{225,... | collective-permute-start | bytes 196616 | tf_op jit(solution)/shard_map/ppermute | solution.py:411
  107.8 0.6 copy-start.10
  131.8 1.5 copy-start.2
  133.3 4.0 %copy-start.8 = (bf16[160,512]{1,0:T(8,128)(2,1)}, bf16[160,512]{1,0:T(8,128)(2,1)S(1)}, u32[]{:S(2)}) copy-start(bf16[160,512]{1,0:T(8,128)(2,1)S(1)} %get-tuple-element.99.kv_grad) | copy-start | bytes 491524
  133.3 3.8 %collective-permute-start.9 = (bf16[4,128,512]{2,1,0:T(8,128)(2,1)S(1)}, bf16[4,128,512]{2,1,0:T(8,128)(2,1)S(1)}, u32[]{:S(2)}, u32[]{:S(2)}) collective-permute-start(bf16[4,128,512]{2,1,0:T(8,128)(2,1)S(1)} %get-tuple-element.97), channel_id=1, source_target_pairs={{0,1},{1,0},{2,3},{3,2},{4,5},{5,4},{6,7},{7,6},{8,9},{9,8},{10,11... | collective-permute-start | bytes 1572872 | tf_op jit(solution)/shard_map/ppermute | solution.py:311
  153.0 15.5 %all-to-all-start.2 = ((bf16[16,8,512]{2,1,0:T(8,128)(2,1)}), bf16[16,8,512]{2,1,0:T(8,128)(2,1)}, u32[]{:S(2)}, u32[]{:S(2)}) async-start(bf16[16,8,512]{2,1,0:T(8,128)(2,1)} %bitcast.40), calls=%async_computation.2 | async-start | bytes 262144 | tf_op jit(solution)/shard_map/all_to_all | solution.py:321
  158.0 8.0 %collective-permute-start.10 = (bf16[32,1024]{1,0:T(8,128)(2,1)}, bf16[32,1024]{1,0:T(8,128)(2,1)S(1)}, u32[]{:S(2)}, u32[]{:S(2)}) collective-permute-start(bf16[32,1024]{1,0:T(8,128)(2,1)} %copy-done.10), channel_id=1, source_target_pairs={{128,0},{160,32},{192,64},{224,96},{129,1},{161,33},{193,65},{225,... | collective-permute-start | bytes 196616 | tf_op jit(solution)/shard_map/ppermute | solution.py:420
  159.3 1.0 copy-start
  160.3 0.9 copy-start.1
  161.2 0.9 copy-start.6
  162.2 0.9 copy-start.9
  163.1 2.9 %copy-start.3 = (bf16[128,1536]{1,0:T(8,128)(2,1)S(1)}, bf16[128,1536]{1,0:T(8,128)(2,1)}, u32[]{:S(2)}) copy-start(bf16[128,1536]{1,0:T(8,128)(2,1)} %copy-done.2) | copy-start | bytes 1179652

commit v7 on v6

--- a/solution.py
+++ b/solution.py
@@ -261,7 +261,10 @@
     outs[0][...] = own.astype(BF)
 
 
-def rows_kernel(tok, gout, gain, wt, qg, kv_grad, out):
+def rows_kernel(tok_hbm, gout_hbm, gain_hbm, qg_hbm, kv_hbm, wt, out, tok, gout, gain, qg, kv_grad, sems):
+    pairs = [(tok_hbm, tok), (gain_hbm, gain), (qg_hbm, qg), (kv_hbm, kv_grad), (gout_hbm, gout)]
+    for copy in loads(pairs, sems):
+        copy.wait()
     hidden = tok[...].astype(F32)
     inverse, _ = normalised(hidden, gain[...])
     normed_grad = nn(qg[...], wt[:D, :]) + nn(kv_grad[MEM:, :], wt[D:, :])
@@ -433,7 +436,21 @@
         400_000_000,
         scalars=1,
     )
-    (grad_tokens,) = call(rows_kernel, [shape((TOK, D))], (tok, gout, gain, wt, qg, kv_grad), 500_000_000)
+    (grad_tokens,) = call(
+        rows_kernel,
+        [shape((TOK, D))],
+        (tok, gout, gain, qg, kv_grad, wt),
+        500_000_000,
+        far=5,
+        scratch=(
+            pltpu.VMEM((TOK, D), BF),
+            pltpu.VMEM((TOK, D), BF),
+            pltpu.VMEM((1, D), F32),
+            pltpu.VMEM((TOK, D), BF),
+            pltpu.VMEM((ROWS, 2 * KV), BF),
+            dma((5,)),
+        ),
+    )
     block = summed_over_group(mine, other)
     block = summed_over_documents(block)
     block, grad_tokens, grad_memories = lax.optimization_barrier((block, grad_tokens, grad_memories))

time: 185 us -> 185 us (level)
  local copies, waits for them, and re-layouts: 5.3 us -> 1.54 us
  waiting for transfers between devices: 27.3 us -> 29.6 us
    unnamed x24 -> x18, local copies, waits for them, and re-layouts: 4.41 us -> 0.65 us
    ppermute x3, waiting for transfers between devices: 1.45 us -> 3.99 us  [body(): memory_arrived = lax.ppermute(memory_send, 'seg', route)]
where the time goes in v7:
time: 185 us; the launch traced here: 184 us
  blocking collectives  80.7 us (44%)
  Pallas kernels  42 us (23%)
  waiting for transfers between devices  29.6 us (16%)
  starting transfers between devices  25.7 us (14%)
  other arithmetic  3.91 us (2%)
    pallas_call x13, Pallas kernels, call(): pl.pallas_call(kernel, out_shape=outs, in_specs=[smem] * scalars + [hbm]...  42 us
    all_to_all x1, blocking collectives, gathered(): lax.all_to_all(copies, 'dp', 0, 0, tiled=True, axis_index_groups=runs(doc...  31.8 us
    all_gather x1, blocking collectives, gathered(): lax.all_gather(shard, 'dp', axis=0, axis_index_groups=runs(docs, docs //...  20.6 us
    ppermute x3, waiting for transfers between devices, body(): arrived = lax.ppermute(send, 'seg', route)  18.1 us
    all_to_all x1, blocking collectives, summed_over_segments(): lax.all_to_all(copies, 'seg', 0, 0, tiled=True)  14.3 us
    all_to_all x1, blocking collectives, summed_over_group(): lax.all_to_all(block, 'seg', 0, 0, tiled=True, axis_index_groups=runs(lax...  13.9 us
    ppermute x3, starting transfers between devices, body(): kvps.append(lax.ppermute(kvp, 'seg', route))  11.2 us
    all_to_all x1, starting transfers between devices, summed_over_documents(): lax.all_to_all(block, 'dp', 0, 0, tiled=True, axis_index_groups=runs(docs...  5.06 us
  transfers between devices with their start and end apart: 12, of which 6 were waited for; matrix products, arithmetic and copies ran while one was open for 0% of the time, Pallas kernels for 12%

profile of v7, /device:TPU:8, one launch (start us, length us, event | category | flops | bytes accessed | tf_op | source)
XLA Modules:
  0.0 184.4 jit_solution(4710170302234800123)
XLA Ops:
  0.6 0.9 pad_maximum_fusion
  1.6 20.6 %all-gather = bf16[128,2560]{1,0:T(8,128)(2,1)S(1)} all-gather(bf16[32,2560]{1,0:T(8,128)(2,1)S(1)} %pad_maximum_fusion), channel_id=2, replica_groups={{0,8,16,24},{1,9,17,25},{2,10,18,26},{3,11,19,27},{4,12,20,28},{5,13,21..., dimensions={0}, use_global_device_ids=true | all-gather | bytes 819200 | tf_op jit(solution)/shard_map/all_gather | solution.py:306
  22.2 0.2 broadcast_in_dim.10
  22.5 31.8 %all_to_all.20.own_hbm = bf16[4,4,32,2560]{3,2,1,0:T(8,128)(2,1)S(1)} all-to-all(bf16[4,4,32,2560]{3,2,1,0:T(8,128)(2,1)S(1)} %broadcast_in_dim.10), channel_id=1, replica_groups={{0,2,4,6},{1,3,5,7},{8,10,12,14},{9,11,13,15},{16,18,20,22},{17,19,21,2..., dimensions={0} | all-to-all | bytes 5242880 | tf_op jit(solution)/shard_map/all_to_all | solution.py:308
  54.3 1.9 %collective-permute-start = (bf16[4,4,32,2560]{3,2,1,0:T(8,128)(2,1)S(1)}, bf16[4,4,32,2560]{3,2,1,0:T(8,128)(2,1)}, u32[]{:S(2)}, u32[]{:S(2)}) collective-permute-start(bf16[4,4,32,2560]{3,2,1,0:T(8,128)(2,1)S(1)} %all_to_all.20.own_hbm), channel_id=1, source_target_pairs={{0,1},{1,0},{2,3},{3,2},{4,5},{5,4},{6,7},{7,6},{8,9},{9,8},{10,11... | collective-permute-start | bytes 7864328 | tf_op jit(solution)/shard_map/ppermute | solution.py:309
  56.2 0.1 pad_add_fusion.place
  56.3 4.9 %collective-permute-done.other_hbm = bf16[4,4,32,2560]{3,2,1,0:T(8,128)(2,1)} collective-permute-done((bf16[4,4,32,2560]{3,2,1,0:T(8,128)(2,1)S(1)}, bf16[4,4,32,2560]{3,2,1,0:T(8,128)(2,1)}, u32[]{:S(2)}, u32[]{:S(2)}) %collective-permute-start) | collective-permute-done | bytes 2621472 | tf_op jit(solution)/shard_map/ppermute | solution.py:309
  61.2 5.3 %shard_map.120 = (bf16[160,1024]{1,0:T(8,128)(2,1)S(1)}, bf16[128,1024]{1,0:T(8,128)(2,1)S(1)}, f32[160,512]{1,0:T(8,128)S(1)}, bf16[224,512]{1,0:T(8,128)(2,1)S...) custom-call(s32[3]{0:T(128)S(1)} %pad_add_fusion.place, ...), custom_call_target="tpu_custom_call" | custom-call | flops 1500000000 | bytes 12226572 | tf_op jit(solution)/shard_map/pallas_call | solution.py:282
  66.5 2.2 %collective-permute-start.1 = (bf16[224,512]{1,0:T(8,128)(2,1)S(1)}, bf16[224,512]{1,0:T(8,128)(2,1)S(1)}, u32[]{:S(2)}, u32[]{:S(2)}) collective-permute-start(bf16[224,512]{1,0:T(8,128)(2,1)S(1)} %get-tuple-element.62.refs_0_), channel_id=1, source_target_pairs={{0,96},{32,0},{64,32},{96,64},{128,224},{160,128},{192,160},{224,1... | collective-permute-start | bytes 688136 | tf_op jit(solution)/shard_map/ppermute | solution.py:374
  68.7 4.3 %collective-permute-start.2 = (bf16[224,512]{1,0:T(8,128)(2,1)S(1)}, bf16[224,512]{1,0:T(8,128)(2,1)S(1)}, u32[]{:S(2)}, u32[]{:S(2)}) collective-permute-start(bf16[224,512]{1,0:T(8,128)(2,1)S(1)} %get-tuple-element.62.refs_0_), channel_id=1, source_target_pairs={{0,64},{32,96},{64,0},{96,32},{128,192},{160,224},{192,128},{224,1... | collective-permute-start | bytes 688136 | tf_op jit(solution)/shard_map/ppermute | solution.py:374
  73.0 4.7 %collective-permute-start.3 = (bf16[224,512]{1,0:T(8,128)(2,1)S(1)}, bf16[224,512]{1,0:T(8,128)(2,1)S(1)}, u32[]{:S(2)}, u32[]{:S(2)}) collective-permute-start(bf16[224,512]{1,0:T(8,128)(2,1)S(1)} %get-tuple-element.62.refs_0_), channel_id=1, source_target_pairs={{0,32},{32,64},{64,96},{96,0},{128,160},{160,192},{192,224},{224,1... | collective-permute-start | bytes 688136 | tf_op jit(solution)/shard_map/ppermute | solution.py:374
  77.7 0.0 copy-start.4
  77.7 4.7 %shard_map.121 = (bf16[1536,1024]{1,0:T(8,128)(2,1)S(1)}, bf16[1536,1024]{1,0:T(8,128)(2,1)S(1)}, bf16[32,1024]{1,0:T(8,128)(2,1)S(1)}) custom-call(bf16[32,1024]{1,0:T(8,128)(2,1)} %bitcast.23, f32[1,1024]{1,0:T(1,128)} %bitcast.27, bf16[1024,1536]{1,0:T(8,128)(2,1)S(1)} %bitcast.19, bf16[1024,1024]{1,0:T(8,128)(2,1)S(1)} %bitcast.21), custom_call_target="tpu_custom_call" | custom-call | flops 4000000000 | bytes 11669504 | tf_op jit(solution)/shard_map/pallas_call | solution.py:282
  82.4 0.0 collective-permute-done.1.refs_1_
  82.4 0.3 collective-permute-done.3.refs_3_
  82.8 2.9 %shard_map.122 = (f32[16,160,128]{2,1,0:T(8,128)S(1)}, f32[16,128,160]{2,1,0:T(8,128)S(1)}, bf16[16,160,256]{2,1,0:T(8,128)(2,1)S(1)}, bf16[16,160,256]{2,1,0:T(...) custom-call(s32[3]{0:T(128)S(1)} %pad_add_fusion.place, ...), custom_call_target="tpu_custom_call" | custom-call | flops 400000000 | bytes 14291468 | tf_op jit(solution)/shard_map/pallas_call | solution.py:282
  85.7 0.0 copy-start.2
  85.7 4.5 %shard_map.123 = (bf16[32,1024]{1,0:T(8,128)(2,1)S(1)}, bf16[128,1024]{1,0:T(8,128)(2,1)S(1)}, bf16[128,1536]{1,0:T(8,128)(2,1)S(1)}) custom-call(s32[3]{0:T(128)S(1)} %pad_add_fusion.place, bf16[32,1024]{1,0:T(8,128)(2,1)S(1)} %get-tuple-element.60.arrived.before, bf16[32,1024]{1,0:T(8,128)(2,1)S(1)} %get-tuple-element.60.arrived.before, ...), custom_call_target="tpu_custom_call" | custom-call | flops 1000000000 | bytes 11862540 | tf_op jit(solution)/shard_map/pallas_call | solution.py:282
  90.3 0.7 collective-permute-start.4
  91.0 1.4 shard_map.124
  92.4 0.0 collective-permute-done.4.arrived
  92.4 0.9 collective-permute-start.6
  93.3 4.6 %shard_map.125 = (bf16[32,1024]{1,0:T(8,128)(2,1)S(1)}, bf16[128,1024]{1,0:T(8,128)(2,1)S(1)}, bf16[128,1536]{1,0:T(8,128)(2,1)S(1)}) custom-call(s32[3]{0:T(128)S(1)} %pad_add_fusion.place, bf16[32,1024]{1,0:T(8,128)(2,1)S(1)} %collective-permute-done.4.arrived, bf16[128,1024]{1,0:T(8,128)(2,1)S(1)} %get-tuple-element.78.before, ...), custom_call_target="tpu_custom_call" | custom-call | flops 1000000000 | bytes 12059148 | tf_op jit(solution)/shard_map/pallas_call | solution.py:282
  97.8 0.7 collective-permute-start.5
  98.5 0.0 collective-permute-done.6.arrived
  98.5 1.4 shard_map.126
  99.9 0.7 collective-permute-start.8
  100.6 4.6 %shard_map.127 = (bf16[32,1024]{1,0:T(8,128)(2,1)S(1)}, bf16[128,1024]{1,0:T(8,128)(2,1)S(1)}, bf16[128,1536]{1,0:T(8,128)(2,1)S(1)}) custom-call(s32[3]{0:T(128)S(1)} %pad_add_fusion.place, bf16[32,1024]{1,0:T(8,128)(2,1)S(1)} %collective-permute-done.5.arrived, bf16[128,1024]{1,0:T(8,128)(2,1)S(1)} %get-tuple-element.85.before, ...), custom_call_target="tpu_custom_call" | custom-call | flops 1000000000 | bytes 12059148 | tf_op jit(solution)/shard_map/pallas_call | solution.py:282
  105.2 1.3 collective-permute-start.7
  106.5 1.4 shard_map.128
  107.8 0.6 copy-done.7
  108.5 18.1 %collective-permute-done.7.arrived = bf16[32,1024]{1,0:T(8,128)(2,1)S(1)} collective-permute-done((bf16[32,1024]{1,0:T(8,128)(2,1)S(1)}, bf16[32,1024]{1,0:T(8,128)(2,1)S(1)}, u32[]{:S(2)}, u32[]{:S(2)}) %collective-permute-start.7) | collective-permute-done | bytes 65568 | tf_op jit(solution)/shard_map/ppermute | solution.py:414
  126.6 5.2 %shard_map.129 = (bf16[32,1024]{1,0:T(8,128)(2,1)}, bf16[128,1024]{1,0:T(8,128)(2,1)S(1)}, bf16[128,1536]{1,0:T(8,128)(2,1)S(1)}) custom-call(s32[3]{0:T(128)S(1)} %pad_add_fusion.place, bf16[32,1024]{1,0:T(8,128)(2,1)S(1)} %collective-permute-done.7.arrived, bf16[128,1024]{1,0:T(8,128)(2,1)S(1)} %get-tuple-element.92.before, ...), custom_call_target="tpu_custom_call" | custom-call | flops 1000000000 | bytes 12059148 | tf_op jit(solution)/shard_map/pallas_call | solution.py:282
  131.8 1.5 shard_map.130
  133.3 1.9 %collective-permute-start.9 = (bf16[4,128,512]{2,1,0:T(8,128)(2,1)S(1)}, bf16[4,128,512]{2,1,0:T(8,128)(2,1)S(1)}, u32[]{:S(2)}, u32[]{:S(2)}) collective-permute-start(bf16[4,128,512]{2,1,0:T(8,128)(2,1)S(1)} %get-tuple-element.97), channel_id=1, source_target_pairs={{0,1},{1,0},{2,3},{3,2},{4,5},{5,4},{6,7},{7,6},{8,9},{9,8},{10,11... | collective-permute-start | bytes 1572872 | tf_op jit(solution)/shard_map/ppermute | solution.py:314
  135.2 1.9 %collective-permute-done.9 = bf16[4,128,512]{2,1,0:T(8,128)(2,1)S(1)} collective-permute-done((bf16[4,128,512]{2,1,0:T(8,128)(2,1)S(1)}, bf16[4,128,512]{2,1,0:T(8,128)(2,1)S(1)}, u32[]{:S(2)}, u32[]{:S(2)}) %collective-permute-start.9) | collective-permute-done | bytes 524320 | tf_op jit(solution)/shard_map/ppermute | solution.py:314
  137.1 0.1 add_convert_fusion
  137.2 13.9 %all_to_all.21 = bf16[4,128,512]{2,1,0:T(8,128)(2,1)} all-to-all(bf16[4,128,512]{2,1,0:T(8,128)(2,1)S(1)} %add_convert_fusion), channel_id=1, replica_groups={{0,32,64,96},{128,160,192,224},{256,288,320,352},{384,416,448,480},{1,3..., dimensions={0} | all-to-all | bytes 1048576 | tf_op jit(solution)/shard_map/all_to_all | solution.py:316
  151.1 1.8 reduce_sum.33
  152.9 5.1 %all-to-all-start.2 = ((bf16[16,8,512]{2,1,0:T(8,128)(2,1)}), bf16[16,8,512]{2,1,0:T(8,128)(2,1)}, u32[]{:S(2)}, u32[]{:S(2)}) async-start(bf16[16,8,512]{2,1,0:T(8,128)(2,1)} %bitcast.40), calls=%async_computation.2 | async-start | bytes 262144 | tf_op jit(solution)/shard_map/all_to_all | solution.py:324
  158.0 1.4 collective-permute-start.10
  159.4 2.7 %shard_map.131 = bf16[128,1024]{1,0:T(8,128)(2,1)} custom-call(bf16[128,1024]{1,0:T(8,128)(2,1)} %bitcast.36, bf16[128,1024]{1,0:T(8,128)(2,1)} %bitcast.38, f32[1,1024]{1,0:T(1,128)} %bitcast.28, bf16[128,1024]{1,0:T(8,128)(2,1)} %copy-done.3, bf16[160,512]{1,0:T(8,128)(2,1)} %copy-done.6, bf16[1536,1024]{1,0:T(8,128)(2,1)S(1)} %get-tuple-element.74.wt), custom_call_target="tpu_custom_call" | custom-call | flops 500000000 | bytes 4362240 | tf_op jit(solution)/shard_map/pallas_call | solution.py:282
  162.1 4.0 %collective-permute-done.10.arrived = bf16[32,1024]{1,0:T(8,128)(2,1)S(1)} collective-permute-done((bf16[32,1024]{1,0:T(8,128)(2,1)}, bf16[32,1024]{1,0:T(8,128)(2,1)S(1)}, u32[]{:S(2)}, u32[]{:S(2)}) %collective-permute-start.10) | collective-permute-done | bytes 65568 | tf_op jit(solution)/shard_map/ppermute | solution.py:423
  166.1 2.0 %shard_map.132 = bf16[32,1024]{1,0:T(8,128)(2,1)} custom-call(s32[3]{0:T(128)S(1)} %pad_add_fusion.place, bf16[32,1024]{1,0:T(8,128)(2,1)S(1)} %collective-permute-done.10.arrived, bf16[32,1024]{1,0:T(8,128)(2,1)S(1)} %get-tuple-element.101.held, bf16[128,1536]{1,0:T(8,128)(2,1)S(1)} %copy-done.1, bf16[1536,1024]{1,0:T(8,128)(2,1)S(1)} %get-tuple-element.74.wt, ...), custom_call_target="tpu_custom_call" | custom-call | flops 400000000 | bytes 4002316 | tf_op jit(solution)/shard_map/pallas_call | solution.py:282
  168.1 0.4 all-to-all-done.2
  168.4 0.9 reduce_sum.34
  169.4 14.3 %all_to_all.22 = bf16[16,8,512]{2,1,0:T(8,128)(2,1)S(1)} all-to-all(bf16[16,8,512]{2,1,0:T(8,128)(2,1)S(1)} %broadcast_in_dim.25), channel_id=1, replica_groups=mesh['seg'=16,'dp'=32] {'seg'}, dimensions={0} | all-to-all | bytes 262144 | tf_op jit(solution)/shard_map/all_to_all | solution.py:331
  183.8 0.6 fusion
  (21 shorter events, 0.1 us)
Async XLA Ops:
  54.3 6.9 %copy-start.8 = (bf16[4,4,32,2560]{3,2,1,0:T(8,128)(2,1)}, bf16[4,4,32,2560]{3,2,1,0:T(8,128)(2,1)S(1)}, u32[]{:S(2)}) copy-start(bf16[4,4,32,2560]{3,2,1,0:T(8,128)(2,1)S(1)} %all_to_all.20.own_hbm) | copy-start | bytes 7864324
  54.3 6.9 %collective-permute-start = (bf16[4,4,32,2560]{3,2,1,0:T(8,128)(2,1)S(1)}, bf16[4,4,32,2560]{3,2,1,0:T(8,128)(2,1)}, u32[]{:S(2)}, u32[]{:S(2)}) collective-permute-start(bf16[4,4,32,2560]{3,2,1,0:T(8,128)(2,1)S(1)} %all_to_all.20.own_hbm), channel_id=1, source_target_pairs={{0,1},{1,0},{2,3},{3,2},{4,5},{5,4},{6,7},{7,6},{8,9},{9,8},{10,11... | collective-permute-start | bytes 7864328 | tf_op jit(solution)/shard_map/ppermute | solution.py:309
  66.5 15.9 %copy-start.3 = (bf16[128,1024]{1,0:T(8,128)(2,1)}, bf16[128,1024]{1,0:T(8,128)(2,1)S(1)}, u32[]{:S(2)}) copy-start(bf16[128,1024]{1,0:T(8,128)(2,1)S(1)} %get-tuple-element.98.qg_hbm) | copy-start | bytes 786436
  66.5 16.0 %collective-permute-start.1 = (bf16[224,512]{1,0:T(8,128)(2,1)S(1)}, bf16[224,512]{1,0:T(8,128)(2,1)S(1)}, u32[]{:S(2)}, u32[]{:S(2)}) collective-permute-start(bf16[224,512]{1,0:T(8,128)(2,1)S(1)} %get-tuple-element.62.refs_0_), channel_id=1, source_target_pairs={{0,96},{32,0},{64,32},{96,64},{128,224},{160,128},{192,160},{224,1... | collective-permute-start | bytes 688136 | tf_op jit(solution)/shard_map/ppermute | solution.py:374
  68.7 13.8 %collective-permute-start.2 = (bf16[224,512]{1,0:T(8,128)(2,1)S(1)}, bf16[224,512]{1,0:T(8,128)(2,1)S(1)}, u32[]{:S(2)}, u32[]{:S(2)}) collective-permute-start(bf16[224,512]{1,0:T(8,128)(2,1)S(1)} %get-tuple-element.62.refs_0_), channel_id=1, source_target_pairs={{0,64},{32,96},{64,0},{96,32},{128,192},{160,224},{192,128},{224,1... | collective-permute-start | bytes 688136 | tf_op jit(solution)/shard_map/ppermute | solution.py:374
  73.0 9.8 %collective-permute-start.3 = (bf16[224,512]{1,0:T(8,128)(2,1)S(1)}, bf16[224,512]{1,0:T(8,128)(2,1)S(1)}, u32[]{:S(2)}, u32[]{:S(2)}) collective-permute-start(bf16[224,512]{1,0:T(8,128)(2,1)S(1)} %get-tuple-element.62.refs_0_), channel_id=1, source_target_pairs={{0,32},{32,64},{64,96},{96,0},{128,160},{160,192},{192,224},{224,1... | collective-permute-start | bytes 688136 | tf_op jit(solution)/shard_map/ppermute | solution.py:374
  77.7 5.1 %copy-start.4 = (f32[1024]{0:T(1024)S(1)}, f32[1024]{0:T(1024)}, u32[]{:S(2)}) copy-start(f32[1024]{0:T(1024)} %param.13) | copy-start | bytes 12292
  85.7 5.2 %copy-start.2 = (bf16[1,32,1024]{2,1,0:T(8,128)(2,1)S(1)}, bf16[1,32,1024]{2,1,0:T(8,128)(2,1)}, u32[]{:S(2)}) copy-start(bf16[1,32,1024]{2,1,0:T(8,128)(2,1)} %param.12) | copy-start | bytes 196612
  90.3 2.1 %collective-permute-start.4 = (bf16[32,1024]{1,0:T(8,128)(2,1)S(1)}, bf16[32,1024]{1,0:T(8,128)(2,1)S(1)}, u32[]{:S(2)}, u32[]{:S(2)}) collective-permute-start(bf16[32,1024]{1,0:T(8,128)(2,1)S(1)} %get-tuple-element.72), channel_id=1, source_target_pairs={{384,256},{416,288},{448,320},{480,352},{385,257},{417,289},{449,3... | collective-permute-start | bytes 196616 | tf_op jit(solution)/shard_map/ppermute | solution.py:414
  92.4 6.1 %collective-permute-start.6 = (bf16[32,1024]{1,0:T(8,128)(2,1)S(1)}, bf16[32,1024]{1,0:T(8,128)(2,1)S(1)}, u32[]{:S(2)}, u32[]{:S(2)}) collective-permute-start(bf16[32,1024]{1,0:T(8,128)(2,1)S(1)} %get-tuple-element.80), channel_id=1, source_target_pairs={{384,256},{416,288},{448,320},{480,352},{385,257},{417,289},{449,3... | collective-permute-start | bytes 196616 | tf_op jit(solution)/shard_map/ppermute | solution.py:423
  97.8 2.1 %collective-permute-start.5 = (bf16[32,1024]{1,0:T(8,128)(2,1)S(1)}, bf16[32,1024]{1,0:T(8,128)(2,1)S(1)}, u32[]{:S(2)}, u32[]{:S(2)}) collective-permute-start(bf16[32,1024]{1,0:T(8,128)(2,1)S(1)} %get-tuple-element.79), channel_id=1, source_target_pairs={{256,128},{288,160},{320,192},{352,224},{257,129},{289,161},{321,1... | collective-permute-start | bytes 196616 | tf_op jit(solution)/shard_map/ppermute | solution.py:414
  99.9 6.5 %collective-permute-start.8 = (bf16[32,1024]{1,0:T(8,128)(2,1)S(1)}, bf16[32,1024]{1,0:T(8,128)(2,1)S(1)}, u32[]{:S(2)}, u32[]{:S(2)}) collective-permute-start(bf16[32,1024]{1,0:T(8,128)(2,1)S(1)} %get-tuple-element.87), channel_id=1, source_target_pairs={{256,128},{288,160},{320,192},{352,224},{257,129},{289,161},{321,1... | collective-permute-start | bytes 196616 | tf_op jit(solution)/shard_map/ppermute | solution.py:423
  105.2 21.4 %collective-permute-start.7 = (bf16[32,1024]{1,0:T(8,128)(2,1)S(1)}, bf16[32,1024]{1,0:T(8,128)(2,1)S(1)}, u32[]{:S(2)}, u32[]{:S(2)}) collective-permute-start(bf16[32,1024]{1,0:T(8,128)(2,1)S(1)} %get-tuple-element.86), channel_id=1, source_target_pairs={{128,0},{160,32},{192,64},{224,96},{129,1},{161,33},{193,65},{225,... | collective-permute-start | bytes 196616 | tf_op jit(solution)/shard_map/ppermute | solution.py:414
  107.8 0.6 copy-start.7
  131.8 1.5 copy-start
  133.3 4.0 %copy-start.6 = (bf16[160,512]{1,0:T(8,128)(2,1)}, bf16[160,512]{1,0:T(8,128)(2,1)S(1)}, u32[]{:S(2)}) copy-start(bf16[160,512]{1,0:T(8,128)(2,1)S(1)} %get-tuple-element.99.kv_hbm) | copy-start | bytes 491524
  133.3 3.8 %collective-permute-start.9 = (bf16[4,128,512]{2,1,0:T(8,128)(2,1)S(1)}, bf16[4,128,512]{2,1,0:T(8,128)(2,1)S(1)}, u32[]{:S(2)}, u32[]{:S(2)}) collective-permute-start(bf16[4,128,512]{2,1,0:T(8,128)(2,1)S(1)} %get-tuple-element.97), channel_id=1, source_target_pairs={{0,1},{1,0},{2,3},{3,2},{4,5},{5,4},{6,7},{7,6},{8,9},{9,8},{10,11... | collective-permute-start | bytes 1572872 | tf_op jit(solution)/shard_map/ppermute | solution.py:314
  151.1 15.0 %copy-start.5 = (f32[1024]{0:T(1024)S(1)}, f32[1024]{0:T(1024)}, u32[]{:S(2)}) copy-start(f32[1024]{0:T(1024)} %param.13) | copy-start | bytes 12292
  152.9 15.6 %all-to-all-start.2 = ((bf16[16,8,512]{2,1,0:T(8,128)(2,1)}), bf16[16,8,512]{2,1,0:T(8,128)(2,1)}, u32[]{:S(2)}, u32[]{:S(2)}) async-start(bf16[16,8,512]{2,1,0:T(8,128)(2,1)} %bitcast.40), calls=%async_computation.2 | async-start | bytes 262144 | tf_op jit(solution)/shard_map/all_to_all | solution.py:324
  158.0 8.1 %copy-start.1 = (bf16[128,1536]{1,0:T(8,128)(2,1)S(1)}, bf16[128,1536]{1,0:T(8,128)(2,1)}, u32[]{:S(2)}) copy-start(bf16[128,1536]{1,0:T(8,128)(2,1)} %copy-done) | copy-start | bytes 1179652
  158.0 8.1 %collective-permute-start.10 = (bf16[32,1024]{1,0:T(8,128)(2,1)}, bf16[32,1024]{1,0:T(8,128)(2,1)S(1)}, u32[]{:S(2)}, u32[]{:S(2)}) collective-permute-start(bf16[32,1024]{1,0:T(8,128)(2,1)} %copy-done.7), channel_id=1, source_target_pairs={{128,0},{160,32},{192,64},{224,96},{129,1},{161,33},{193,65},{225,... | collective-permute-start | bytes 196616 | tf_op jit(solution)/shard_map/ppermute | solution.py:423

commit v8 on v7

--- a/solution.py
+++ b/solution.py
@@ -314,7 +314,10 @@
     got = lax.ppermute(other, "dp", [(i, i ^ 1) for i in range(docs)])
     block = (mine.astype(F32) + got.astype(F32)).astype(BF)
     block = lax.all_to_all(block, "seg", 0, 0, tiled=True, axis_index_groups=runs(lax.axis_size("seg"), SPAN, 1))
-    return jnp.sum(block.astype(F32), axis=0).astype(BF)
+    total = block[0].astype(F32)
+    for member in range(1, SPAN):
+        total = total + block[member].astype(F32)
+    return total.astype(BF)
 
 
 def summed_over_documents(block):

time: 185 us -> 183 us (0.989)
  no operation moved by 1% of the time
where the time goes in v8:
time: 183 us
  blocking collectives  80 us (44%)
  Pallas kernels  42 us (23%)
  waiting for transfers between devices  29.6 us (16%)
  starting transfers between devices  25.7 us (14%)
  other arithmetic  2.82 us (2%)
    pallas_call x13, Pallas kernels, call(): pl.pallas_call(kernel, out_shape=outs, in_specs=[smem] * scalars + [hbm]...  42 us
    all_to_all x1, blocking collectives, gathered(): lax.all_to_all(copies, 'dp', 0, 0, tiled=True, axis_index_groups=runs(doc...  31.8 us
    all_gather x1, blocking collectives, gathered(): lax.all_gather(shard, 'dp', axis=0, axis_index_groups=runs(docs, docs //...  20.6 us
    ppermute x3, waiting for transfers between devices, body(): arrived = lax.ppermute(send, 'seg', route)  18.1 us
    all_to_all x1, blocking collectives, summed_over_segments(): lax.all_to_all(copies, 'seg', 0, 0, tiled=True)  14.3 us
    all_to_all x1, blocking collectives, summed_over_group(): lax.all_to_all(block, 'seg', 0, 0, tiled=True, axis_index_groups=runs(lax...  13.2 us
    ppermute x3, starting transfers between devices, body(): kvps.append(lax.ppermute(kvp, 'seg', route))  11.2 us
    all_to_all x1, starting transfers between devices, summed_over_documents(): lax.all_to_all(block, 'dp', 0, 0, tiled=True, axis_index_groups=runs(docs...  5.06 us
  transfers between devices with their start and end apart: 12, of which 6 were waited for; matrix products, arithmetic and copies ran while one was open for 0% of the time, Pallas kernels for 12%

profile of v8, /device:TPU:8, one launch (start us, length us, event | category | flops | bytes accessed | tf_op | source)
XLA Modules:
  0.0 182.7 jit_solution(6487499077310272513)
XLA Ops:
  0.6 0.9 pad_maximum_fusion
  1.6 20.6 %all-gather = bf16[128,2560]{1,0:T(8,128)(2,1)S(1)} all-gather(bf16[32,2560]{1,0:T(8,128)(2,1)S(1)} %pad_maximum_fusion), channel_id=2, replica_groups={{0,8,16,24},{1,9,17,25},{2,10,18,26},{3,11,19,27},{4,12,20,28},{5,13,21..., dimensions={0}, use_global_device_ids=true | all-gather | bytes 819200 | tf_op jit(solution)/shard_map/all_gather | solution.py:306
  22.2 0.2 broadcast_in_dim.10
  22.5 31.8 %all_to_all.20.own_hbm = bf16[4,4,32,2560]{3,2,1,0:T(8,128)(2,1)S(1)} all-to-all(bf16[4,4,32,2560]{3,2,1,0:T(8,128)(2,1)S(1)} %broadcast_in_dim.10), channel_id=1, replica_groups={{0,2,4,6},{1,3,5,7},{8,10,12,14},{9,11,13,15},{16,18,20,22},{17,19,21,2..., dimensions={0} | all-to-all | bytes 5242880 | tf_op jit(solution)/shard_map/all_to_all | solution.py:308
  54.3 1.9 %collective-permute-start = (bf16[4,4,32,2560]{3,2,1,0:T(8,128)(2,1)S(1)}, bf16[4,4,32,2560]{3,2,1,0:T(8,128)(2,1)}, u32[]{:S(2)}, u32[]{:S(2)}) collective-permute-start(bf16[4,4,32,2560]{3,2,1,0:T(8,128)(2,1)S(1)} %all_to_all.20.own_hbm), channel_id=1, source_target_pairs={{0,1},{1,0},{2,3},{3,2},{4,5},{5,4},{6,7},{7,6},{8,9},{9,8},{10,11... | collective-permute-start | bytes 7864328 | tf_op jit(solution)/shard_map/ppermute | solution.py:309
  56.2 0.1 pad_add_fusion.place
  56.3 4.9 %collective-permute-done.other_hbm = bf16[4,4,32,2560]{3,2,1,0:T(8,128)(2,1)} collective-permute-done((bf16[4,4,32,2560]{3,2,1,0:T(8,128)(2,1)S(1)}, bf16[4,4,32,2560]{3,2,1,0:T(8,128)(2,1)}, u32[]{:S(2)}, u32[]{:S(2)}) %collective-permute-start) | collective-permute-done | bytes 2621472 | tf_op jit(solution)/shard_map/ppermute | solution.py:309
  61.2 5.3 %shard_map.120 = (bf16[160,1024]{1,0:T(8,128)(2,1)S(1)}, bf16[128,1024]{1,0:T(8,128)(2,1)S(1)}, f32[160,512]{1,0:T(8,128)S(1)}, bf16[224,512]{1,0:T(8,128)(2,1)S...) custom-call(s32[3]{0:T(128)S(1)} %pad_add_fusion.place, ...), custom_call_target="tpu_custom_call" | custom-call | flops 1500000000 | bytes 12226572 | tf_op jit(solution)/shard_map/pallas_call | solution.py:282
  66.5 2.2 %collective-permute-start.1 = (bf16[224,512]{1,0:T(8,128)(2,1)S(1)}, bf16[224,512]{1,0:T(8,128)(2,1)S(1)}, u32[]{:S(2)}, u32[]{:S(2)}) collective-permute-start(bf16[224,512]{1,0:T(8,128)(2,1)S(1)} %get-tuple-element.62.refs_0_), channel_id=1, source_target_pairs={{0,96},{32,0},{64,32},{96,64},{128,224},{160,128},{192,160},{224,1... | collective-permute-start | bytes 688136 | tf_op jit(solution)/shard_map/ppermute | solution.py:377
  68.7 4.3 %collective-permute-start.2 = (bf16[224,512]{1,0:T(8,128)(2,1)S(1)}, bf16[224,512]{1,0:T(8,128)(2,1)S(1)}, u32[]{:S(2)}, u32[]{:S(2)}) collective-permute-start(bf16[224,512]{1,0:T(8,128)(2,1)S(1)} %get-tuple-element.62.refs_0_), channel_id=1, source_target_pairs={{0,64},{32,96},{64,0},{96,32},{128,192},{160,224},{192,128},{224,1... | collective-permute-start | bytes 688136 | tf_op jit(solution)/shard_map/ppermute | solution.py:377
  73.0 4.7 %collective-permute-start.3 = (bf16[224,512]{1,0:T(8,128)(2,1)S(1)}, bf16[224,512]{1,0:T(8,128)(2,1)S(1)}, u32[]{:S(2)}, u32[]{:S(2)}) collective-permute-start(bf16[224,512]{1,0:T(8,128)(2,1)S(1)} %get-tuple-element.62.refs_0_), channel_id=1, source_target_pairs={{0,32},{32,64},{64,96},{96,0},{128,160},{160,192},{192,224},{224,1... | collective-permute-start | bytes 688136 | tf_op jit(solution)/shard_map/ppermute | solution.py:377
  77.7 0.0 copy-start.4
  77.7 4.7 %shard_map.121 = (bf16[1536,1024]{1,0:T(8,128)(2,1)S(1)}, bf16[1536,1024]{1,0:T(8,128)(2,1)S(1)}, bf16[32,1024]{1,0:T(8,128)(2,1)S(1)}) custom-call(bf16[32,1024]{1,0:T(8,128)(2,1)} %bitcast.24, f32[1,1024]{1,0:T(1,128)} %bitcast.28, bf16[1024,1536]{1,0:T(8,128)(2,1)S(1)} %bitcast.20, bf16[1024,1024]{1,0:T(8,128)(2,1)S(1)} %bitcast.22), custom_call_target="tpu_custom_call" | custom-call | flops 4000000000 | bytes 11669504 | tf_op jit(solution)/shard_map/pallas_call | solution.py:282
  82.4 0.0 collective-permute-done.1.refs_1_
  82.4 0.3 collective-permute-done.3.refs_3_
  82.8 2.9 %shard_map.122 = (f32[16,160,128]{2,1,0:T(8,128)S(1)}, f32[16,128,160]{2,1,0:T(8,128)S(1)}, bf16[16,160,256]{2,1,0:T(8,128)(2,1)S(1)}, bf16[16,160,256]{2,1,0:T(...) custom-call(s32[3]{0:T(128)S(1)} %pad_add_fusion.place, ...), custom_call_target="tpu_custom_call" | custom-call | flops 400000000 | bytes 14291468 | tf_op jit(solution)/shard_map/pallas_call | solution.py:282
  85.7 0.0 copy-start.2
  85.7 4.5 %shard_map.123 = (bf16[32,1024]{1,0:T(8,128)(2,1)S(1)}, bf16[128,1024]{1,0:T(8,128)(2,1)S(1)}, bf16[128,1536]{1,0:T(8,128)(2,1)S(1)}) custom-call(s32[3]{0:T(128)S(1)} %pad_add_fusion.place, bf16[32,1024]{1,0:T(8,128)(2,1)S(1)} %get-tuple-element.60.arrived.before, bf16[32,1024]{1,0:T(8,128)(2,1)S(1)} %get-tuple-element.60.arrived.before, ...), custom_call_target="tpu_custom_call" | custom-call | flops 1000000000 | bytes 11862540 | tf_op jit(solution)/shard_map/pallas_call | solution.py:282
  90.3 0.7 collective-permute-start.4
  91.0 1.4 shard_map.124
  92.4 0.0 collective-permute-done.4.arrived
  92.4 0.9 collective-permute-start.6
  93.3 4.6 %shard_map.125 = (bf16[32,1024]{1,0:T(8,128)(2,1)S(1)}, bf16[128,1024]{1,0:T(8,128)(2,1)S(1)}, bf16[128,1536]{1,0:T(8,128)(2,1)S(1)}) custom-call(s32[3]{0:T(128)S(1)} %pad_add_fusion.place, bf16[32,1024]{1,0:T(8,128)(2,1)S(1)} %collective-permute-done.4.arrived, bf16[128,1024]{1,0:T(8,128)(2,1)S(1)} %get-tuple-element.78.before, ...), custom_call_target="tpu_custom_call" | custom-call | flops 1000000000 | bytes 12059148 | tf_op jit(solution)/shard_map/pallas_call | solution.py:282
  97.8 0.7 collective-permute-start.5
  98.5 0.0 collective-permute-done.6.arrived
  98.5 1.4 shard_map.126
  99.9 0.7 collective-permute-start.8
  100.6 4.6 %shard_map.127 = (bf16[32,1024]{1,0:T(8,128)(2,1)S(1)}, bf16[128,1024]{1,0:T(8,128)(2,1)S(1)}, bf16[128,1536]{1,0:T(8,128)(2,1)S(1)}) custom-call(s32[3]{0:T(128)S(1)} %pad_add_fusion.place, bf16[32,1024]{1,0:T(8,128)(2,1)S(1)} %collective-permute-done.5.arrived, bf16[128,1024]{1,0:T(8,128)(2,1)S(1)} %get-tuple-element.85.before, ...), custom_call_target="tpu_custom_call" | custom-call | flops 1000000000 | bytes 12059148 | tf_op jit(solution)/shard_map/pallas_call | solution.py:282
  105.2 1.3 collective-permute-start.7
  106.5 1.4 shard_map.128
  107.8 0.6 copy-done.7
  108.5 18.1 %collective-permute-done.7.arrived = bf16[32,1024]{1,0:T(8,128)(2,1)S(1)} collective-permute-done((bf16[32,1024]{1,0:T(8,128)(2,1)S(1)}, bf16[32,1024]{1,0:T(8,128)(2,1)S(1)}, u32[]{:S(2)}, u32[]{:S(2)}) %collective-permute-start.7) | collective-permute-done | bytes 65568 | tf_op jit(solution)/shard_map/ppermute | solution.py:417
  126.6 5.2 %shard_map.129 = (bf16[32,1024]{1,0:T(8,128)(2,1)}, bf16[128,1024]{1,0:T(8,128)(2,1)S(1)}, bf16[128,1536]{1,0:T(8,128)(2,1)S(1)}) custom-call(s32[3]{0:T(128)S(1)} %pad_add_fusion.place, bf16[32,1024]{1,0:T(8,128)(2,1)S(1)} %collective-permute-done.7.arrived, bf16[128,1024]{1,0:T(8,128)(2,1)S(1)} %get-tuple-element.92.before, ...), custom_call_target="tpu_custom_call" | custom-call | flops 1000000000 | bytes 12059148 | tf_op jit(solution)/shard_map/pallas_call | solution.py:282
  131.8 1.5 shard_map.130
  133.3 1.9 %collective-permute-start.9 = (bf16[4,128,512]{2,1,0:T(8,128)(2,1)S(1)}, bf16[4,128,512]{2,1,0:T(8,128)(2,1)S(1)}, u32[]{:S(2)}, u32[]{:S(2)}) collective-permute-start(bf16[4,128,512]{2,1,0:T(8,128)(2,1)S(1)} %get-tuple-element.97), channel_id=1, source_target_pairs={{0,1},{1,0},{2,3},{3,2},{4,5},{5,4},{6,7},{7,6},{8,9},{9,8},{10,11... | collective-permute-start | bytes 1572872 | tf_op jit(solution)/shard_map/ppermute | solution.py:314
  135.2 1.9 %collective-permute-done.9 = bf16[4,128,512]{2,1,0:T(8,128)(2,1)S(1)} collective-permute-done((bf16[4,128,512]{2,1,0:T(8,128)(2,1)S(1)}, bf16[4,128,512]{2,1,0:T(8,128)(2,1)S(1)}, u32[]{:S(2)}, u32[]{:S(2)}) %collective-permute-start.9) | collective-permute-done | bytes 524320 | tf_op jit(solution)/shard_map/ppermute | solution.py:314
  137.1 0.1 add_convert_fusion
  137.2 13.2 %all_to_all.21 = bf16[4,128,512]{2,1,0:T(8,128)(2,1)S(1)} all-to-all(bf16[4,128,512]{2,1,0:T(8,128)(2,1)S(1)} %add_convert_fusion), channel_id=1, replica_groups={{0,32,64,96},{128,160,192,224},{256,288,320,352},{384,416,448,480},{1,3..., dimensions={0} | all-to-all | bytes 1048576 | tf_op jit(solution)/shard_map/all_to_all | solution.py:316
  150.4 0.7 fusion
  151.1 5.1 %all-to-all-start.2 = ((bf16[16,8,512]{2,1,0:T(8,128)(2,1)}), bf16[16,8,512]{2,1,0:T(8,128)(2,1)}, u32[]{:S(2)}, u32[]{:S(2)}) async-start(bf16[16,8,512]{2,1,0:T(8,128)(2,1)} %fusion), calls=%async_computation.2 | async-start | bytes 262144 | tf_op jit(solution)/shard_map/all_to_all | solution.py:327
  156.2 1.4 collective-permute-start.10
  157.6 2.7 %shard_map.131 = bf16[128,1024]{1,0:T(8,128)(2,1)} custom-call(bf16[128,1024]{1,0:T(8,128)(2,1)} %bitcast.37, bf16[128,1024]{1,0:T(8,128)(2,1)} %bitcast.39, f32[1,1024]{1,0:T(1,128)} %bitcast.29, bf16[128,1024]{1,0:T(8,128)(2,1)} %copy-done.3, bf16[160,512]{1,0:T(8,128)(2,1)} %copy-done.6, bf16[1536,1024]{1,0:T(8,128)(2,1)S(1)} %get-tuple-element.74.wt), custom_call_target="tpu_custom_call" | custom-call | flops 500000000 | bytes 4362240 | tf_op jit(solution)/shard_map/pallas_call | solution.py:282
  160.3 4.0 %collective-permute-done.10.arrived = bf16[32,1024]{1,0:T(8,128)(2,1)S(1)} collective-permute-done((bf16[32,1024]{1,0:T(8,128)(2,1)}, bf16[32,1024]{1,0:T(8,128)(2,1)S(1)}, u32[]{:S(2)}, u32[]{:S(2)}) %collective-permute-start.10) | collective-permute-done | bytes 65568 | tf_op jit(solution)/shard_map/ppermute | solution.py:426
  164.3 2.0 %shard_map.132 = bf16[32,1024]{1,0:T(8,128)(2,1)} custom-call(s32[3]{0:T(128)S(1)} %pad_add_fusion.place, bf16[32,1024]{1,0:T(8,128)(2,1)S(1)} %collective-permute-done.10.arrived, bf16[32,1024]{1,0:T(8,128)(2,1)S(1)} %get-tuple-element.101.held, bf16[128,1536]{1,0:T(8,128)(2,1)S(1)} %copy-done.1, bf16[1536,1024]{1,0:T(8,128)(2,1)S(1)} %get-tuple-element.74.wt, ...), custom_call_target="tpu_custom_call" | custom-call | flops 400000000 | bytes 4002316 | tf_op jit(solution)/shard_map/pallas_call | solution.py:282
  166.3 0.4 all-to-all-done.2
  166.7 0.9 reduce_sum.21
  167.6 14.3 %all_to_all.22 = bf16[16,8,512]{2,1,0:T(8,128)(2,1)S(1)} all-to-all(bf16[16,8,512]{2,1,0:T(8,128)(2,1)S(1)} %broadcast_in_dim.25), channel_id=1, replica_groups=mesh['seg'=16,'dp'=32] {'seg'}, dimensions={0} | all-to-all | bytes 262144 | tf_op jit(solution)/shard_map/all_to_all | solution.py:334
  182.0 0.6 fusion.1
  (21 shorter events, 0.1 us)
Async XLA Ops:
  54.3 6.9 %copy-start.8 = (bf16[4,4,32,2560]{3,2,1,0:T(8,128)(2,1)}, bf16[4,4,32,2560]{3,2,1,0:T(8,128)(2,1)S(1)}, u32[]{:S(2)}) copy-start(bf16[4,4,32,2560]{3,2,1,0:T(8,128)(2,1)S(1)} %all_to_all.20.own_hbm) | copy-start | bytes 7864324
  54.3 6.9 %collective-permute-start = (bf16[4,4,32,2560]{3,2,1,0:T(8,128)(2,1)S(1)}, bf16[4,4,32,2560]{3,2,1,0:T(8,128)(2,1)}, u32[]{:S(2)}, u32[]{:S(2)}) collective-permute-start(bf16[4,4,32,2560]{3,2,1,0:T(8,128)(2,1)S(1)} %all_to_all.20.own_hbm), channel_id=1, source_target_pairs={{0,1},{1,0},{2,3},{3,2},{4,5},{5,4},{6,7},{7,6},{8,9},{9,8},{10,11... | collective-permute-start | bytes 7864328 | tf_op jit(solution)/shard_map/ppermute | solution.py:309
  66.5 15.9 %copy-start.3 = (bf16[128,1024]{1,0:T(8,128)(2,1)}, bf16[128,1024]{1,0:T(8,128)(2,1)S(1)}, u32[]{:S(2)}) copy-start(bf16[128,1024]{1,0:T(8,128)(2,1)S(1)} %get-tuple-element.98.qg_hbm) | copy-start | bytes 786436
  66.5 16.0 %collective-permute-start.1 = (bf16[224,512]{1,0:T(8,128)(2,1)S(1)}, bf16[224,512]{1,0:T(8,128)(2,1)S(1)}, u32[]{:S(2)}, u32[]{:S(2)}) collective-permute-start(bf16[224,512]{1,0:T(8,128)(2,1)S(1)} %get-tuple-element.62.refs_0_), channel_id=1, source_target_pairs={{0,96},{32,0},{64,32},{96,64},{128,224},{160,128},{192,160},{224,1... | collective-permute-start | bytes 688136 | tf_op jit(solution)/shard_map/ppermute | solution.py:377
  68.7 13.8 %collective-permute-start.2 = (bf16[224,512]{1,0:T(8,128)(2,1)S(1)}, bf16[224,512]{1,0:T(8,128)(2,1)S(1)}, u32[]{:S(2)}, u32[]{:S(2)}) collective-permute-start(bf16[224,512]{1,0:T(8,128)(2,1)S(1)} %get-tuple-element.62.refs_0_), channel_id=1, source_target_pairs={{0,64},{32,96},{64,0},{96,32},{128,192},{160,224},{192,128},{224,1... | collective-permute-start | bytes 688136 | tf_op jit(solution)/shard_map/ppermute | solution.py:377
  73.0 9.8 %collective-permute-start.3 = (bf16[224,512]{1,0:T(8,128)(2,1)S(1)}, bf16[224,512]{1,0:T(8,128)(2,1)S(1)}, u32[]{:S(2)}, u32[]{:S(2)}) collective-permute-start(bf16[224,512]{1,0:T(8,128)(2,1)S(1)} %get-tuple-element.62.refs_0_), channel_id=1, source_target_pairs={{0,32},{32,64},{64,96},{96,0},{128,160},{160,192},{192,224},{224,1... | collective-permute-start | bytes 688136 | tf_op jit(solution)/shard_map/ppermute | solution.py:377
  77.7 5.1 %copy-start.4 = (f32[1024]{0:T(1024)S(1)}, f32[1024]{0:T(1024)}, u32[]{:S(2)}) copy-start(f32[1024]{0:T(1024)} %param.13) | copy-start | bytes 12292
  85.7 5.2 %copy-start.2 = (bf16[1,32,1024]{2,1,0:T(8,128)(2,1)S(1)}, bf16[1,32,1024]{2,1,0:T(8,128)(2,1)}, u32[]{:S(2)}) copy-start(bf16[1,32,1024]{2,1,0:T(8,128)(2,1)} %param.12) | copy-start | bytes 196612
  90.3 2.1 %collective-permute-start.4 = (bf16[32,1024]{1,0:T(8,128)(2,1)S(1)}, bf16[32,1024]{1,0:T(8,128)(2,1)S(1)}, u32[]{:S(2)}, u32[]{:S(2)}) collective-permute-start(bf16[32,1024]{1,0:T(8,128)(2,1)S(1)} %get-tuple-element.72), channel_id=1, source_target_pairs={{384,256},{416,288},{448,320},{480,352},{385,257},{417,289},{449,3... | collective-permute-start | bytes 196616 | tf_op jit(solution)/shard_map/ppermute | solution.py:417
  92.4 6.1 %collective-permute-start.6 = (bf16[32,1024]{1,0:T(8,128)(2,1)S(1)}, bf16[32,1024]{1,0:T(8,128)(2,1)S(1)}, u32[]{:S(2)}, u32[]{:S(2)}) collective-permute-start(bf16[32,1024]{1,0:T(8,128)(2,1)S(1)} %get-tuple-element.80), channel_id=1, source_target_pairs={{384,256},{416,288},{448,320},{480,352},{385,257},{417,289},{449,3... | collective-permute-start | bytes 196616 | tf_op jit(solution)/shard_map/ppermute | solution.py:426
  97.8 2.1 %collective-permute-start.5 = (bf16[32,1024]{1,0:T(8,128)(2,1)S(1)}, bf16[32,1024]{1,0:T(8,128)(2,1)S(1)}, u32[]{:S(2)}, u32[]{:S(2)}) collective-permute-start(bf16[32,1024]{1,0:T(8,128)(2,1)S(1)} %get-tuple-element.79), channel_id=1, source_target_pairs={{256,128},{288,160},{320,192},{352,224},{257,129},{289,161},{321,1... | collective-permute-start | bytes 196616 | tf_op jit(solution)/shard_map/ppermute | solution.py:417
  99.9 6.5 %collective-permute-start.8 = (bf16[32,1024]{1,0:T(8,128)(2,1)S(1)}, bf16[32,1024]{1,0:T(8,128)(2,1)S(1)}, u32[]{:S(2)}, u32[]{:S(2)}) collective-permute-start(bf16[32,1024]{1,0:T(8,128)(2,1)S(1)} %get-tuple-element.87), channel_id=1, source_target_pairs={{256,128},{288,160},{320,192},{352,224},{257,129},{289,161},{321,1... | collective-permute-start | bytes 196616 | tf_op jit(solution)/shard_map/ppermute | solution.py:426
  105.2 21.4 %collective-permute-start.7 = (bf16[32,1024]{1,0:T(8,128)(2,1)S(1)}, bf16[32,1024]{1,0:T(8,128)(2,1)S(1)}, u32[]{:S(2)}, u32[]{:S(2)}) collective-permute-start(bf16[32,1024]{1,0:T(8,128)(2,1)S(1)} %get-tuple-element.86), channel_id=1, source_target_pairs={{128,0},{160,32},{192,64},{224,96},{129,1},{161,33},{193,65},{225,... | collective-permute-start | bytes 196616 | tf_op jit(solution)/shard_map/ppermute | solution.py:417
  107.8 0.6 copy-start.7
  131.8 1.5 copy-start
  133.3 4.0 %copy-start.6 = (bf16[160,512]{1,0:T(8,128)(2,1)}, bf16[160,512]{1,0:T(8,128)(2,1)S(1)}, u32[]{:S(2)}) copy-start(bf16[160,512]{1,0:T(8,128)(2,1)S(1)} %get-tuple-element.99.kv_hbm) | copy-start | bytes 491524
  133.3 3.8 %collective-permute-start.9 = (bf16[4,128,512]{2,1,0:T(8,128)(2,1)S(1)}, bf16[4,128,512]{2,1,0:T(8,128)(2,1)S(1)}, u32[]{:S(2)}, u32[]{:S(2)}) collective-permute-start(bf16[4,128,512]{2,1,0:T(8,128)(2,1)S(1)} %get-tuple-element.97), channel_id=1, source_target_pairs={{0,1},{1,0},{2,3},{3,2},{4,5},{5,4},{6,7},{7,6},{8,9},{9,8},{10,11... | collective-permute-start | bytes 1572872 | tf_op jit(solution)/shard_map/ppermute | solution.py:314
  150.4 13.9 %copy-start.5 = (f32[1024]{0:T(1024)S(1)}, f32[1024]{0:T(1024)}, u32[]{:S(2)}) copy-start(f32[1024]{0:T(1024)} %param.13) | copy-start | bytes 12292
  151.1 15.6 %all-to-all-start.2 = ((bf16[16,8,512]{2,1,0:T(8,128)(2,1)}), bf16[16,8,512]{2,1,0:T(8,128)(2,1)}, u32[]{:S(2)}, u32[]{:S(2)}) async-start(bf16[16,8,512]{2,1,0:T(8,128)(2,1)} %fusion), calls=%async_computation.2 | async-start | bytes 262144 | tf_op jit(solution)/shard_map/all_to_all | solution.py:327
  156.2 8.1 %copy-start.1 = (bf16[128,1536]{1,0:T(8,128)(2,1)S(1)}, bf16[128,1536]{1,0:T(8,128)(2,1)}, u32[]{:S(2)}) copy-start(bf16[128,1536]{1,0:T(8,128)(2,1)} %copy-done) | copy-start | bytes 1179652
  156.2 8.1 %collective-permute-start.10 = (bf16[32,1024]{1,0:T(8,128)(2,1)}, bf16[32,1024]{1,0:T(8,128)(2,1)S(1)}, u32[]{:S(2)}, u32[]{:S(2)}) collective-permute-start(bf16[32,1024]{1,0:T(8,128)(2,1)} %copy-done.7), channel_id=1, source_target_pairs={{128,0},{160,32},{192,64},{224,96},{129,1},{161,33},{193,65},{225,... | collective-permute-start | bytes 196616 | tf_op jit(solution)/shard_map/ppermute | solution.py:426
